TPU v7x, 32 devices: a whole 2x2x4 slice. The times are simulated.
32 devices in a mesh: dp: 8 (over z, x), tensor: 4 (over y, core).
Axes of the slice: x: 2, y: 2, z: 4, core: 2. Of those that a mesh axis runs over, the one named last changes fastest.
Arguments:
- lang_in: bfloat16 [256, 20, 768], P(('dp', 'tensor')), may hold values from -6 to 6
- vis_in: bfloat16 [256, 36, 768], P(('dp', 'tensor')), may hold values from -6 to 6
- word_lengths: int32 [256], P('dp'), may hold values from 5 to 20, as said below
- lang_cot: bfloat16 [256, 20, 768], P(('dp', 'tensor')), may hold values from -6 to 6
- vis_cot: bfloat16 [256, 36, 768], P(('dp', 'tensor')), may hold values from -6 to 6
- attn_master: float32 [3, 4, 768, 768], P(None, None, 'dp', 'tensor'), may hold values from -0.4330127 to 0.4330127
- attn_first: float32 [3, 4, 768, 768], P(None, None, 'dp', 'tensor'), may hold values from -0.00390625 to 0.00390625
- attn_second: float32 [3, 4, 768, 768], P(None, None, 'dp', 'tensor'), may hold values from 3.0234602e-08 to 4.8375364e-07
- ffn_master: float32 [2, 2, 768, 3072], P(None, None, 'dp', 'tensor'), may hold values from -0.25980762 to 0.25980762
- ffn_first: float32 [2, 2, 768, 3072], P(None, None, 'dp', 'tensor'), may hold values from -0.00390625 to 0.00390625
- ffn_second: float32 [2, 2, 768, 3072], P(None, None, 'dp', 'tensor'), may hold values from 3.0234602e-08 to 4.8375364e-07
- vectors: float32 [29, 768], replicated, may hold values from -0.8 to 2.07
- vector_first: float32 [29, 768], replicated, may hold values from -0.00390625 to 0.00390625
- vector_second: float32 [29, 768], replicated, may hold values from 3.0234602e-08 to 4.8375364e-07
Outputs:
- lang_out: float32 [256, 20, 768], P(('dp', 'tensor'))
- vis_out: float32 [256, 36, 768], P(('dp', 'tensor'))
- lang_grad: float32 [256, 20, 768], P(('dp', 'tensor'))
- vis_grad: float32 [256, 36, 768], P(('dp', 'tensor'))
- attn_new: float32 [3, 4, 768, 768], P(None, None, 'dp', 'tensor')
- attn_first_new: float32 [3, 4, 768, 768], P(None, None, 'dp', 'tensor')
- attn_second_new: float32 [3, 4, 768, 768], P(None, None, 'dp', 'tensor')
- attn_copy: bfloat16 [3, 4, 768, 768], P(None, None, 'dp', 'tensor')
- ffn_new: float32 [2, 2, 768, 3072], P(None, None, 'dp', 'tensor')
- ffn_first_new: float32 [2, 2, 768, 3072], P(None, None, 'dp', 'tensor')
- ffn_second_new: float32 [2, 2, 768, 3072], P(None, None, 'dp', 'tensor')
- ffn_copy: bfloat16 [2, 2, 768, 3072], P(None, None, 'dp', 'tensor')
- vector_new: float32 [29, 768], replicated
- vector_first_new: float32 [29, 768], replicated
- vector_second_new: float32 [29, 768], replicated
- ffn_bias_grad: float32 [2, 768], replicated
- grad_norm: float32 [], replicated
Inputs may be any that keep to these rules, and one draw needn't show every extreme that they name: `word_lengths`: word positions from an item's length up to 20 are padding; some item has 5 words and some has 20.
All inputs are finite; a program needn't handle non-finite values.
Results may differ from a plain program's by a relative error of at most 0.035.
Values may be sent and summed in bfloat16 or wider, within the bound.
A program may use at most 192 MiB of HBM per device.

v0:
```python
import jax
import jax.numpy as jnp
from jax import lax
from jax.sharding import PartitionSpec as P

HD = 64
STEP = 10


NORM_EPSILON = 1e-06
MASKED = -1000000000.0
BETA_FIRST = 0.5
BETA_SECOND = 0.5
ADAM_EPSILON = 1e-08
WEIGHT_DECAY = 0.01
RATE_MATRIX = 0.03
RATE_VECTOR = 0.3
CLIP_NORM = 1.0


def normalize(inputs, norm_gain, norm_shift):
    average = jnp.mean(inputs, -1, keepdims=True)
    centered = inputs - average
    variance = jnp.mean(centered * centered, -1, keepdims=True)
    return centered * lax.rsqrt(variance + NORM_EPSILON) * norm_gain + norm_shift


def norm_backward(inputs, norm_gain, norm_shift, grad_out):
    _, pull_back = jax.vjp(normalize, inputs, norm_gain, norm_shift)
    return pull_back(grad_out)


def smooth_gate(inputs):
    return jax.nn.gelu(inputs, approximate=False)


def product(left_rows, right_matrix):
    return jnp.dot(left_rows, right_matrix, preferred_element_type=jnp.float32)


def contract_last(left_rows, right_matrix):
    return lax.dot_general(
        left_rows,
        right_matrix,
        (((left_rows.ndim - 1,), (1,)), ((), ())),
        preferred_element_type=jnp.float32,
    )


def outer_sum(left_rows, right_rows):
    flat_left = left_rows.reshape(-1, left_rows.shape[-1])
    flat_right = right_rows.reshape(-1, right_rows.shape[-1])
    return lax.dot_general(
        flat_left, flat_right, (((0,), (0,)), ((), ())), preferred_element_type=jnp.float32
    )


def token_sum(values):
    return jnp.sum(values.astype(jnp.float32), (0, 1))


def split_heads(values):
    return values.reshape(values.shape[0], values.shape[1], -1, HD)


def merge_heads(values):
    return values.reshape(values.shape[0], values.shape[1], -1)


def project(query_rows, key_rows, weights, query_bias, value_bias):
    queries = (product(query_rows, weights[0]) + query_bias).astype(jnp.bfloat16)
    keys_low = product(key_rows, weights[1]).astype(jnp.bfloat16)
    values = (product(key_rows, weights[2]) + value_bias).astype(jnp.bfloat16)
    return (queries, keys_low, values)


def score_rows(queries, keys_low, keep_mask):
    scores = jnp.einsum(
        "bqhd,bkhd->bhqk",
        split_heads(queries),
        split_heads(keys_low),
        preferred_element_type=jnp.float32,
    ) * HD ** (-0.5)
    if keep_mask is not None:
        scores = jnp.where(keep_mask[:, None, None, :], scores, MASKED)
    return scores


def attend_forward(query_rows, key_rows, keep_mask, weights, query_bias, value_bias):
    queries, keys_low, values = project(query_rows, key_rows, weights, query_bias, value_bias)
    scores = score_rows(queries, keys_low, keep_mask)
    maximum = jnp.max(scores, -1, keepdims=True)
    exponent = jnp.exp(scores - maximum)
    denominator = jnp.sum(exponent, -1, keepdims=True)
    attention_low = (exponent / denominator).astype(jnp.bfloat16)
    mixture = jnp.einsum(
        "bhqk,bkhd->bqhd", attention_low, split_heads(values), preferred_element_type=jnp.float32
    )
    mixture = merge_heads(mixture).astype(jnp.bfloat16)
    return (contract_last(mixture, weights[3]), maximum + jnp.log(denominator))


def attend_backward(
    query_rows, key_rows, keep_mask, weights, query_bias, value_bias, log_total, grad_rows
):
    queries, keys_low, values = project(query_rows, key_rows, weights, query_bias, value_bias)
    scores = score_rows(queries, keys_low, keep_mask)
    attention = jnp.exp(scores - log_total)
    attention_low = attention.astype(jnp.bfloat16)
    mixture = jnp.einsum(
        "bhqk,bkhd->bqhd", attention_low, split_heads(values), preferred_element_type=jnp.float32
    )
    mixture = merge_heads(mixture).astype(jnp.bfloat16)
    grad_output = outer_sum(grad_rows, mixture)
    grad_mixture = split_heads(product(grad_rows, weights[3]).astype(jnp.bfloat16))
    grad_attention = jnp.einsum(
        "bqhd,bkhd->bhqk", grad_mixture, split_heads(values), preferred_element_type=jnp.float32
    )
    grad_values = merge_heads(
        jnp.einsum(
            "bhqk,bqhd->bkhd", attention_low, grad_mixture, preferred_element_type=jnp.float32
        )
    ).astype(jnp.bfloat16)
    grad_scores = (
        attention * (grad_attention - jnp.sum(attention * grad_attention, -1, keepdims=True))
    ).astype(jnp.bfloat16)
    score_scale = HD ** (-0.5)
    grad_queries = merge_heads(
        jnp.einsum(
            "bhqk,bkhd->bqhd",
            grad_scores,
            split_heads(keys_low),
            preferred_element_type=jnp.float32,
        )
        * score_scale
    ).astype(jnp.bfloat16)
    grad_keys = merge_heads(
        jnp.einsum(
            "bhqk,bqhd->bkhd", grad_scores, split_heads(queries), preferred_element_type=jnp.float32
        )
        * score_scale
    ).astype(jnp.bfloat16)
    grad_weights = jnp.stack(
        [
            outer_sum(query_rows, grad_queries),
            outer_sum(key_rows, grad_keys),
            outer_sum(key_rows, grad_values),
            grad_output,
        ]
    )
    bias_grads = (token_sum(grad_queries), token_sum(grad_values))
    grad_query_rows = contract_last(grad_queries, weights[0])
    grad_key_rows = contract_last(grad_keys, weights[1]) + contract_last(grad_values, weights[2])
    return (grad_query_rows, grad_key_rows, grad_weights, bias_grads)


def feed_forward(hidden_rows, weights, hidden_bias):
    hidden_pre = product(hidden_rows, weights[0]) + hidden_bias
    activation_low = smooth_gate(hidden_pre).astype(jnp.bfloat16)
    return (contract_last(activation_low, weights[1]), hidden_pre)


def feed_backward(hidden_rows, weights, hidden_pre, grad_rows):
    activation, gate_pull = jax.vjp(smooth_gate, hidden_pre)
    activation_low = activation.astype(jnp.bfloat16)
    grad_down = outer_sum(grad_rows, activation_low)
    grad_activation = product(grad_rows, weights[1])
    grad_pre = gate_pull(grad_activation)[0].astype(jnp.bfloat16)
    grad_up = outer_sum(hidden_rows, grad_pre)
    grad_hidden_rows = contract_last(grad_pre, weights[0])
    return (grad_hidden_rows, jnp.stack([grad_up, grad_down]), token_sum(grad_pre))


def spread(word_state, region_state):
    return (
        lax.all_gather(word_state.astype(jnp.bfloat16), "tensor", axis=0, tiled=True),
        lax.all_gather(region_state.astype(jnp.bfloat16), "tensor", axis=0, tiled=True),
    )


def collect(word_terms, region_terms):
    return (
        lax.psum_scatter(
            word_terms.astype(jnp.bfloat16), "tensor", scatter_dimension=0, tiled=True
        ).astype(jnp.float32),
        lax.psum_scatter(
            region_terms.astype(jnp.bfloat16), "tensor", scatter_dimension=0, tiled=True
        ).astype(jnp.float32),
    )


def fetch_rows(word_grads, region_grads):
    return (
        lax.all_gather(word_grads.astype(jnp.bfloat16), "tensor", axis=0, tiled=True),
        lax.all_gather(region_grads.astype(jnp.bfloat16), "tensor", axis=0, tiled=True),
    )


def give_back(word_terms, region_terms):
    return (
        lax.psum_scatter(
            word_terms.astype(jnp.bfloat16), "tensor", scatter_dimension=0, tiled=True
        ).astype(jnp.float32),
        lax.psum_scatter(
            region_terms.astype(jnp.bfloat16), "tensor", scatter_dimension=0, tiled=True
        ).astype(jnp.float32),
    )


def adam_update(master, first, second, grad, rate):
    first = BETA_FIRST * first + (1.0 - BETA_FIRST) * grad
    second = BETA_SECOND * second + (1.0 - BETA_SECOND) * grad * grad
    first_hat = first / (1.0 - BETA_FIRST**STEP)
    second_hat = second / (1.0 - BETA_SECOND**STEP)
    fresh = master - rate * (
        first_hat / (jnp.sqrt(second_hat) + ADAM_EPSILON) + WEIGHT_DECAY * master
    )
    return (fresh, first, second)


def body(
    lang_in,
    vis_in,
    word_lengths,
    lang_cot,
    vis_cot,
    attn_master,
    attn_first,
    attn_second,
    ffn_master,
    ffn_first,
    ffn_second,
    vectors,
    vector_first,
    vector_second,
):
    tensor_rank = lax.axis_index("tensor")
    attn_weights, ffn_weights = (
        lax.all_gather(attn_master.astype(jnp.bfloat16), "dp", axis=2, tiled=True),
        lax.all_gather(ffn_master.astype(jnp.bfloat16), "dp", axis=2, tiled=True),
    )
    head_cols = attn_weights.shape[3]
    hidden_cols = ffn_weights.shape[3]
    model_width = attn_weights.shape[2]
    hidden_total = hidden_cols * lax.axis_size("tensor")
    own_items = lang_in.shape[0]
    positions = jnp.arange(lang_in.shape[1], dtype=jnp.int32)
    keep_group = positions[None, :] < word_lengths[:, None]
    own_lengths = lax.dynamic_slice_in_dim(word_lengths, tensor_rank * own_items, own_items)
    keep_words = (positions[None, :] < own_lengths[:, None]).astype(jnp.float32)

    def head_part(row_values):
        return lax.dynamic_slice_in_dim(row_values, tensor_rank * head_cols, head_cols)

    def head_place(row_values):
        return lax.dynamic_update_slice_in_dim(
            jnp.zeros((model_width,), jnp.float32), row_values, tensor_rank * head_cols, 0
        )

    def hidden_place(row_values):
        return lax.dynamic_update_slice_in_dim(
            jnp.zeros((hidden_total,), jnp.float32), row_values, tensor_rank * hidden_cols, 0
        )

    hidden_biases = vectors[21:].reshape(2, hidden_total)
    hidden_bias = [
        lax.dynamic_slice_in_dim(hidden_biases[stream], tensor_rank * hidden_cols, hidden_cols)
        for stream in range(2)
    ]
    query_bias = [head_part(vectors[block_index]) for block_index in range(3)]
    value_bias = [head_part(vectors[3 + block_index]) for block_index in range(3)]
    word_state = lang_in.astype(jnp.float32)
    region_state = vis_in.astype(jnp.float32)
    word_rows, region_rows = spread(lang_in, vis_in)
    word_branch, word_cross_total = attend_forward(
        word_rows, region_rows, None, attn_weights[0], query_bias[0], value_bias[0]
    )
    region_branch, region_cross_total = attend_forward(
        region_rows, word_rows, keep_group, attn_weights[0], query_bias[0], value_bias[0]
    )
    word_branch, region_branch = collect(word_branch, region_branch)
    word_cross_sum = word_branch + vectors[6] + word_state
    region_cross_sum = region_branch + vectors[6] + region_state
    word_after_cross = normalize(word_cross_sum, vectors[9], vectors[14])
    region_after_cross = normalize(region_cross_sum, vectors[9], vectors[14])
    word_self_rows, region_self_rows = spread(word_after_cross, region_after_cross)
    word_branch, word_self_total = attend_forward(
        word_self_rows, word_self_rows, keep_group, attn_weights[1], query_bias[1], value_bias[1]
    )
    region_branch, region_self_total = attend_forward(
        region_self_rows, region_self_rows, None, attn_weights[2], query_bias[2], value_bias[2]
    )
    word_branch, region_branch = collect(word_branch, region_branch)
    word_self_sum = word_branch + vectors[7] + word_after_cross
    region_self_sum = region_branch + vectors[8] + region_after_cross
    word_after_self = normalize(word_self_sum, vectors[10], vectors[15])
    region_after_self = normalize(region_self_sum, vectors[11], vectors[16])
    word_feed_rows, region_feed_rows = spread(word_after_self, region_after_self)
    word_branch, word_pre = feed_forward(word_feed_rows, ffn_weights[0], hidden_bias[0])
    region_branch, region_pre = feed_forward(region_feed_rows, ffn_weights[1], hidden_bias[1])
    word_branch, region_branch = collect(word_branch, region_branch)
    word_feed_sum = word_branch + vectors[19] + word_after_self
    region_feed_sum = region_branch + vectors[20] + region_after_self
    lang_out = normalize(word_feed_sum, vectors[12], vectors[17])
    vis_out = normalize(region_feed_sum, vectors[13], vectors[18])
    vector_grad = jnp.zeros(vectors.shape, jnp.float32)
    grad_word = lang_cot.astype(jnp.float32) * keep_words[:, :, None]
    grad_region = vis_cot.astype(jnp.float32)
    word_sum_grad, gain_grad, shift_grad = norm_backward(
        word_feed_sum, vectors[12], vectors[17], grad_word
    )
    vector_grad = (
        vector_grad.at[12]
        .add(gain_grad)
        .at[17]
        .add(shift_grad)
        .at[19]
        .add(token_sum(word_sum_grad))
    )
    region_sum_grad, gain_grad, shift_grad = norm_backward(
        region_feed_sum, vectors[13], vectors[18], grad_region
    )
    vector_grad = (
        vector_grad.at[13]
        .add(gain_grad)
        .at[18]
        .add(shift_grad)
        .at[20]
        .add(token_sum(region_sum_grad))
    )
    word_grad_rows, region_grad_rows = fetch_rows(word_sum_grad, region_sum_grad)
    word_back, word_ffn_grad, word_bias_grad = feed_backward(
        word_feed_rows, ffn_weights[0], word_pre, word_grad_rows
    )
    region_back, region_ffn_grad, region_bias_grad = feed_backward(
        region_feed_rows, ffn_weights[1], region_pre, region_grad_rows
    )
    ffn_grad = jnp.stack([word_ffn_grad, region_ffn_grad])
    hidden_grads = jnp.concatenate(
        [hidden_place(word_bias_grad), hidden_place(region_bias_grad)]
    ).reshape(-1, model_width)
    vector_grad = vector_grad.at[21:].add(hidden_grads)
    word_back, region_back = give_back(word_back, region_back)
    grad_word = word_sum_grad + word_back
    grad_region = region_sum_grad + region_back
    word_sum_grad, gain_grad, shift_grad = norm_backward(
        word_self_sum, vectors[10], vectors[15], grad_word
    )
    vector_grad = (
        vector_grad.at[10].add(gain_grad).at[15].add(shift_grad).at[7].add(token_sum(word_sum_grad))
    )
    region_sum_grad, gain_grad, shift_grad = norm_backward(
        region_self_sum, vectors[11], vectors[16], grad_region
    )
    vector_grad = (
        vector_grad.at[11]
        .add(gain_grad)
        .at[16]
        .add(shift_grad)
        .at[8]
        .add(token_sum(region_sum_grad))
    )
    word_grad_rows, region_grad_rows = fetch_rows(word_sum_grad, region_sum_grad)
    word_query_back, word_key_back, word_attn_grad, word_bias_pair = attend_backward(
        word_self_rows,
        word_self_rows,
        keep_group,
        attn_weights[1],
        query_bias[1],
        value_bias[1],
        word_self_total,
        word_grad_rows,
    )
    region_query_back, region_key_back, region_attn_grad, region_bias_pair = attend_backward(
        region_self_rows,
        region_self_rows,
        None,
        attn_weights[2],
        query_bias[2],
        value_bias[2],
        region_self_total,
        region_grad_rows,
    )
    vector_grad = (
        vector_grad.at[1]
        .add(head_place(word_bias_pair[0]))
        .at[4]
        .add(head_place(word_bias_pair[1]))
    )
    vector_grad = (
        vector_grad.at[2]
        .add(head_place(region_bias_pair[0]))
        .at[5]
        .add(head_place(region_bias_pair[1]))
    )
    word_back, region_back = give_back(
        word_query_back + word_key_back, region_query_back + region_key_back
    )
    grad_word = word_sum_grad + word_back
    grad_region = region_sum_grad + region_back
    word_sum_grad, gain_grad, shift_grad = norm_backward(
        word_cross_sum, vectors[9], vectors[14], grad_word
    )
    vector_grad = (
        vector_grad.at[9].add(gain_grad).at[14].add(shift_grad).at[6].add(token_sum(word_sum_grad))
    )
    region_sum_grad, gain_grad, shift_grad = norm_backward(
        region_cross_sum, vectors[9], vectors[14], grad_region
    )
    vector_grad = (
        vector_grad.at[9]
        .add(gain_grad)
        .at[14]
        .add(shift_grad)
        .at[6]
        .add(token_sum(region_sum_grad))
    )
    word_grad_rows, region_grad_rows = fetch_rows(word_sum_grad, region_sum_grad)
    word_query_back, region_key_back, first_cross_grad, first_bias_pair = attend_backward(
        word_rows,
        region_rows,
        None,
        attn_weights[0],
        query_bias[0],
        value_bias[0],
        word_cross_total,
        word_grad_rows,
    )
    region_query_back, word_key_back, second_cross_grad, second_bias_pair = attend_backward(
        region_rows,
        word_rows,
        keep_group,
        attn_weights[0],
        query_bias[0],
        value_bias[0],
        region_cross_total,
        region_grad_rows,
    )
    vector_grad = vector_grad.at[0].add(head_place(first_bias_pair[0] + second_bias_pair[0]))
    vector_grad = vector_grad.at[3].add(head_place(first_bias_pair[1] + second_bias_pair[1]))
    word_back, region_back = give_back(
        word_query_back + word_key_back, region_query_back + region_key_back
    )
    lang_grad = word_sum_grad + word_back
    vis_grad = region_sum_grad + region_back
    attn_grad = jnp.stack([first_cross_grad + second_cross_grad, word_attn_grad, region_attn_grad])
    vector_total = lax.psum(vector_grad, ("dp", "tensor"))
    attn_share, ffn_share = (
        lax.psum_scatter(
            attn_grad.astype(jnp.bfloat16), "dp", scatter_dimension=2, tiled=True
        ).astype(jnp.float32),
        lax.psum_scatter(
            ffn_grad.astype(jnp.bfloat16), "dp", scatter_dimension=2, tiled=True
        ).astype(jnp.float32),
    )
    matrix_squares = jnp.sum(attn_share * attn_share) + jnp.sum(ffn_share * ffn_share)
    square_total = lax.psum(matrix_squares, ("dp", "tensor"))
    grad_norm = jnp.sqrt(square_total + jnp.sum(vector_total * vector_total))
    clip_scale = CLIP_NORM / jnp.maximum(grad_norm, CLIP_NORM)
    vector_clipped = vector_total * clip_scale
    attn_new, attn_first_new, attn_second_new = adam_update(
        attn_master, attn_first, attn_second, attn_share * clip_scale, RATE_MATRIX
    )
    ffn_new, ffn_first_new, ffn_second_new = adam_update(
        ffn_master, ffn_first, ffn_second, ffn_share * clip_scale, RATE_MATRIX
    )
    vector_new, vector_first_new, vector_second_new = adam_update(
        vectors, vector_first, vector_second, vector_clipped, RATE_VECTOR
    )
    return (
        lang_out,
        vis_out,
        lang_grad,
        vis_grad,
        attn_new,
        attn_first_new,
        attn_second_new,
        attn_new.astype(jnp.bfloat16),
        ffn_new,
        ffn_first_new,
        ffn_second_new,
        ffn_new.astype(jnp.bfloat16),
        vector_new,
        vector_first_new,
        vector_second_new,
        vector_clipped[19:21],
        grad_norm,
    )


def solution(mesh):
    return jax.shard_map(
        body,
        mesh=mesh,
        in_specs=(
            P(("dp", "tensor"), None, None),
            P(("dp", "tensor"), None, None),
            P("dp"),
            P(("dp", "tensor"), None, None),
            P(("dp", "tensor"), None, None),
            P(None, None, "dp", "tensor"),
            P(None, None, "dp", "tensor"),
            P(None, None, "dp", "tensor"),
            P(None, None, "dp", "tensor"),
            P(None, None, "dp", "tensor"),
            P(None, None, "dp", "tensor"),
            P(),
            P(),
            P(),
        ),
        out_specs=(
            P(("dp", "tensor"), None, None),
            P(("dp", "tensor"), None, None),
            P(("dp", "tensor"), None, None),
            P(("dp", "tensor"), None, None),
            P(None, None, "dp", "tensor"),
            P(None, None, "dp", "tensor"),
            P(None, None, "dp", "tensor"),
            P(None, None, "dp", "tensor"),
            P(None, None, "dp", "tensor"),
            P(None, None, "dp", "tensor"),
            P(None, None, "dp", "tensor"),
            P(None, None, "dp", "tensor"),
            P(),
            P(),
            P(),
            P(),
            P(),
        ),
        check_vma=False,
    )
```

profile of v0, /device:TPU:0, one launch (start us, length us, event | category | flops | bytes accessed | tf_op | source)
XLA Modules:
  0.0 1136.9 jit_solution(555211572350936780)
XLA Ops:
  11.1 11.6 %all_gather.44 = bf16[32,20,768]{2,0,1:T(8,128)(2,1)} all-gather(bf16[8,20,768]{2,0,1:T(8,128)(2,1)S(1)} %copy-done.20), channel_id=1, replica_groups=mesh['dp'=8,'tensor'=4] {'tensor'}, dimensions={0}, use_global_device_ids=true | all-gather | bytes 1228800 | tf_op jit(solution)/shard_map/all_gather | solution.py:176
  22.7 70.7 %all-gather.11.cloned.1.call-done = bf16[3,4,768,192]{3,1,0,2:T(4,128)(2,1)} async-done(((bf16[3,4,96,192]{3,1,0,2:T(4,128)(2,1)}), bf16[3,4,768,192]{3,1,0,2:T(4,128)(2,1)}) %all-gather.11.cloned.1.call-update) | async-done | bytes 3538960 | tf_op jit(solution)/shard_map/all_gather | solution.py:239
  93.4 14.2 %fusion.297 = (bf16[1,1,768,192]{3,1,0,2:T(2,128)(2,1)}, bf16[1,1,768,192]{3,1,0,2:T(2,128)(2,1)}, bf16[1,1,768,192]{3,1,0,2:T(2,128)(2,1)}, bf16[1,1,768,192]{3...) fusion(bf16[3,4,768,192]{3,1,0,2:T(4,128)(2,1)} %all-gather.11., ...), kind=kLoop, calls=%fused_computation.533 | loop fusion | bytes 7077888 | tf_op jit(solution)/shard_map/slice | solution.py:100
  113.9 3.8 fusion.65
  117.7 3.5 reshape.1424
  137.9 3.3 fusion.85
  157.0 3.1 convolution_convert_fusion.3
  180.8 14.5 %reduce-scatter.29.cloned.1.call-done = bf16[8,36,768]{2,1,0:T(8,128)(2,1)} async-done(((bf16[32,36,768]{2,1,0:T(8,128)(2,1)}), bf16[8,36,768]{2,1,0:T(8,128)(2,1)}) %reduce-scatter.29.cloned.1.call-update) | async-done | bytes 442384 | tf_op jit(solution)/shard_map/reduce_scatter | solution.py:186
  199.8 9.3 all_gather.45
  230.6 3.0 fusion.79
  245.0 3.4 reshape.1404
  248.4 3.2 convolution_convert_fusion.2
  257.4 27.2 %reduce-scatter.31.cloned.1.call-done = bf16[8,36,768]{2,1,0:T(8,128)(2,1)} async-done(((bf16[32,36,768]{2,1,0:T(8,128)(2,1)}), bf16[8,36,768]{2,1,0:T(8,128)(2,1)}) %reduce-scatter.31.cloned.1.call-update) | async-done | bytes 442384 | tf_op jit(solution)/shard_map/reduce_scatter | solution.py:186
  289.8 9.9 all_gather.46
  299.7 67.5 %all-gather.13.cloned.1.call-done = bf16[2,2,768,768]{3,2,1,0:T(8,128)(2,1)} async-done(((bf16[2,2,96,768]{3,2,1,0:T(8,128)(2,1)}), bf16[2,2,768,768]{3,2,1,0:T(8,128)(2,1)}) %all-gather.13.cloned.1.call-update) | async-done | bytes 4718608 | tf_op jit(solution)/shard_map/all_gather | solution.py:240
  370.1 5.3 multiply_convert_fusion.6
  379.1 9.2 all-gather.17.cloned.1.call-done
  388.3 5.5 convert_reduce_fusion.1
  393.8 9.8 multiply_convert_fusion
  404.9 4.3 convolution_convert_fusion.1
  410.0 5.9 reduce-scatter.47.cloned.1.call-done
  418.0 31.3 %reduce-scatter.33.cloned.1.call-done = bf16[8,36,768]{2,1,0:T(8,128)(2,1)} async-done(((bf16[32,36,768]{2,1,0:T(8,128)(2,1)}), bf16[8,36,768]{2,1,0:T(8,128)(2,1)}) %reduce-scatter.33.cloned.1.call-update) | async-done | bytes 442384 | tf_op jit(solution)/shard_map/reduce_scatter | solution.py:186
  462.5 14.9 %all_gather.50 = bf16[32,20,768]{2,0,1:T(8,128)(2,1)S(1)} all-gather(bf16[8,20,768]{2,0,1:T(8,128)(2,1)S(1)} %add_convert_fusion.11), channel_id=1, replica_groups=mesh['dp'=8,'tensor'=4] {'tensor'}, dimensions={0}, use_global_device_ids=true | all-gather | bytes 1228800 | tf_op jit(solution)/shard_map/all_gather | solution.py:194
  477.4 3.7 convert_reduce_fusion.9
  484.9 8.9 convert_reduce_fusion.2
  495.1 4.4 convolution_convert_fusion
  505.1 3.4 reshape.1406
  523.4 19.5 %reduce-scatter.35.cloned.1.call-done = bf16[8,36,768]{2,1,0:T(8,128)(2,1)} async-done(((bf16[32,36,768]{2,1,0:T(8,128)(2,1)}), bf16[8,36,768]{2,1,0:T(8,128)(2,1)}) %reduce-scatter.35.cloned.1.call-update) | async-done | bytes 442384 | tf_op jit(solution)/shard_map/reduce_scatter | solution.py:204
  542.9 3.0 multiply_reduce_fusion.6
  548.6 9.5 all_gather.51
  587.5 3.8 fusion.73
  591.3 3.4 reshape.1429
  601.8 3.4 convert_element_type.595
  609.1 3.4 convert_element_type.591
  617.0 3.4 convert_element_type.588
  645.4 3.4 reshape.1408
  667.5 3.4 fusion.59
  678.8 14.5 %all_gather.52 = bf16[32,20,768]{2,0,1:T(8,128)(2,1)S(1)} all-gather(bf16[8,20,768]{2,0,1:T(8,128)(2,1)S(1)} %get-tuple-element.462), channel_id=1, replica_groups=mesh['dp'=8,'tensor'=4] {'tensor'}, dimensions={0}, use_global_device_ids=true | all-gather | bytes 1228800 | tf_op jit(solution)/shard_map/all_gather | solution.py:194
  711.9 3.8 fusion.76
  773.6 8.1 copy.353
  781.7 8.8 reshape.1421
  800.0 118.8 %all-reduce.3.cloned.1.call-done = f32[29,768]{1,0:T(8,128)} async-done(((f32[29,768]{1,0:T(8,128)}), f32[29,768]{1,0:T(8,128)}) %all-reduce.3.cloned.1.call-update) | async-done | bytes 89104 | tf_op jit(solution)/shard_map/psum | solution.py:447
  920.3 27.0 %reduce-scatter.53.cloned.1.call-done = bf16[8,15360]{1,0:T(8,128)(2,1)} async-done(((bf16[32,15360]{1,0:T(8,128)(2,1)}), bf16[8,15360]{1,0:T(8,128)(2,1)}) %reduce-scatter.53.cloned.1.call-update) | async-done | bytes 245776
  949.3 31.3 %reduce-scatter.39.cloned.1.call-done = bf16[8,36,768]{2,1,0:T(8,128)(2,1)} async-done(((bf16[32,36,768]{2,1,0:T(8,128)(2,1)}), bf16[8,36,768]{2,1,0:T(8,128)(2,1)}) %reduce-scatter.39.cloned.1.call-update) | async-done | bytes 442384 | tf_op jit(solution)/shard_map/reduce_scatter | solution.py:204
  982.8 80.6 %reduce-scatter.55.cloned.1.call-done = bf16[96,2304]{1,0:T(8,128)(2,1)} async-done(((bf16[768,2304]{1,0:T(8,128)(2,1)}), bf16[96,2304]{1,0:T(8,128)(2,1)}) %reduce-scatter.55.cloned.1.call-update) | async-done | bytes 442384
  1070.5 40.4 %psum.14 = f32[]{:T(128)} all-reduce(f32[]{:T(128)S(6)} %add.833), channel_id=1, replica_groups=mesh['dp'=8,'tensor'=4] {'dp','tensor'}, use_global_device_ids=true, to_apply=%region_52.53 | all-reduce | flops 1 | bytes 8 | tf_op jit(solution)/shard_map/psum | solution.py:457
  1113.7 4.0 fusion.283
  1125.0 4.0 fusion.281
  (814 shorter events, 363.5 us)
Async XLA Ops:
  7.2 86.2 %all-gather.11.cloned.1.call-start = ((), (), s32[]{:S(2)}) async-start(), calls=%async_computation.15 | async-start | bytes 5308416 | tf_op jit(solution)/shard_map/all_gather | solution.py:239
  10.2 103.7 %all-gather.9.cloned.1.call-start = ((), (), s32[]{:S(2)}) async-start(), calls=%async_computation.14 | async-start | bytes 2211840 | tf_op jit(solution)/shard_map/all_gather | solution.py:177
  11.0 168.7 %reduce-scatter.43.cloned.1.call-start = ((), (), s32[]{:S(2)}) async-start(), calls=%async_computation.30 | async-start | bytes 1228800
  137.4 57.9 %reduce-scatter.29.cloned.1.call-start = ((), (), s32[]{:S(2)}) async-start(), calls=%async_computation.17 | async-start | bytes 2457600 | tf_op jit(solution)/shard_map/reduce_scatter | solution.py:186
  160.1 66.3 %all-gather.15.cloned.1.call-start = ((), (), s32[]{:S(2)}) async-start(), calls=%async_computation.18 | async-start | bytes 2211840 | tf_op jit(solution)/shard_map/all_gather | solution.py:177
  160.9 38.7 %copy-start.158 = (f32[768]{0:T(1024)}, f32[768]{0:T(1024)S(1)}, u32[]{:S(2)}) copy-start(f32[768]{0:T(1024)S(1)} %get-tuple-element.405) | copy-start | bytes 9220
  172.9 22.5 %copy-start.6 = (bf16[8,36,768]{2,0,1:T(8,128)(2,1)S(1)}, bf16[8,36,768]{2,0,1:T(8,128)(2,1)}, u32[]{:S(2)}) copy-start(bf16[8,36,768]{2,0,1:T(8,128)(2,1)} %param.65) | copy-start | bytes 1327108
  175.1 55.5 %copy-start.98 = (bf16[1,1,768,192]{2,3,1,0:T(8,128)(2,1)}, bf16[1,1,768,192]{2,3,1,0:T(8,128)(2,1)S(1)}, u32[]{:S(2)}) copy-start(bf16[1,1,768,192]{2,3,1,0:T(8,128)(2,1)S(1)} %copy.382) | copy-start | bytes 884740
  199.3 55.7 %reduce-scatter.45.cloned.1.call-start = ((), (), s32[]{:S(2)}) async-start(), calls=%async_computation.31 | async-start | bytes 1228800
  199.6 55.4 %copy-start.129 = (f32[8,20]{0,1:T(8,128)}, f32[8,20]{0,1:T(8,128)S(1)}, u32[]{:S(2)}) copy-start(f32[8,20]{0,1:T(8,128)S(1)} %fusion.266) | copy-start | bytes 1924
  226.2 58.4 %reduce-scatter.31.cloned.1.call-start = ((), (), s32[]{:S(2)}) async-start(), calls=%async_computation.19 | async-start | bytes 2457600 | tf_op jit(solution)/shard_map/reduce_scatter | solution.py:186
  251.6 33.0 %copy-start.145 = (f32[8,36]{1,0:T(8,128)S(1)}, f32[8,36]{1,0:T(8,128)}, u32[]{:S(2)}) copy-start(f32[8,36]{1,0:T(8,128)} %copy-done.144) | copy-start | bytes 3460
  251.6 33.0 %copy-start.151 = (f32[8,36]{1,0:T(8,128)S(1)}, f32[8,36]{1,0:T(8,128)}, u32[]{:S(2)}) copy-start(f32[8,36]{1,0:T(8,128)} %copy-done.150) | copy-start | bytes 3460
  251.6 33.0 %copy-start.179 = (f32[768]{0:T(1024)S(1)}, f32[768]{0:T(1024)}, u32[]{:S(2)}) copy-start(f32[768]{0:T(1024)} %get-tuple-element.398) | copy-start | bytes 9220
  251.6 115.6 %all-gather.13.cloned.1.call-start = ((), (), s32[]{:S(2)}) async-start(), calls=%async_computation.16 | async-start | bytes 5308416 | tf_op jit(solution)/shard_map/all_gather | solution.py:240
  253.9 134.5 %all-gather.17.cloned.1.call-start = ((), (), s32[]{:S(2)}) async-start(), calls=%async_computation.20 | async-start | bytes 2211840 | tf_op jit(solution)/shard_map/all_gather | solution.py:177
  257.2 30.2 %copy-start.153 = (f32[768]{0:T(1024)S(1)}, f32[768]{0:T(1024)}, u32[]{:S(2)}) copy-start(f32[768]{0:T(1024)} %get-tuple-element.397) | copy-start | bytes 9220
  257.2 30.2 %copy-start.169 = (f32[768]{0:T(1024)S(1)}, f32[768]{0:T(1024)}, u32[]{:S(2)}) copy-start(f32[768]{0:T(1024)} %get-tuple-element.396) | copy-start | bytes 9220
  257.3 31.2 %copy-start.149 = (f32[8,20]{0,1:T(8,128)}, f32[8,20]{0,1:T(8,128)S(1)}, u32[]{:S(2)}) copy-start(f32[8,20]{0,1:T(8,128)S(1)} %multiply_reduce_fusion.19) | copy-start | bytes 1924
  286.5 162.8 %copy-start.142 = (f32[8,36]{1,0:T(8,128)}, f32[8,36]{1,0:T(8,128)S(1)}, u32[]{:S(2)}) copy-start(f32[8,36]{1,0:T(8,128)S(1)} %broadcast_multiply_fusion.5) | copy-start | bytes 3460
  286.7 162.5 %copy-start.156 = (f32[8,36]{1,0:T(8,128)}, f32[8,36]{1,0:T(8,128)S(1)}, u32[]{:S(2)}) copy-start(f32[8,36]{1,0:T(8,128)S(1)} %fusion.270) | copy-start | bytes 3460
  288.5 127.4 %reduce-scatter.47.cloned.1.call-start = ((), (), s32[]{:S(2)}) async-start(), calls=%async_computation.32 | async-start | bytes 1228800
  288.6 127.3 %copy-start.131 = (f32[8,20]{0,1:T(8,128)}, f32[8,20]{0,1:T(8,128)S(1)}, u32[]{:S(2)}) copy-start(f32[8,20]{0,1:T(8,128)S(1)} %fusion.267) | copy-start | bytes 1924
  379.1 70.2 %reduce-scatter.33.cloned.1.call-start = ((), (), s32[]{:S(2)}) async-start(), calls=%async_computation.21 | async-start | bytes 2457600 | tf_op jit(solution)/shard_map/reduce_scatter | solution.py:186
  409.3 40.0 %copy-start.177 = (f32[768]{0:T(1024)S(1)}, f32[768]{0:T(1024)}, u32[]{:S(2)}) copy-start(f32[768]{0:T(1024)} %get-tuple-element.395) | copy-start | bytes 9220
  409.3 75.6 %all-gather.19.cloned.1.call-start = ((), (), s32[]{:S(2)}) async-start(), calls=%async_computation.22 | async-start | bytes 2211840 | tf_op jit(solution)/shard_map/all_gather | solution.py:195
  418.0 33.4 %copy-start.168 = (f32[768]{0:T(1024)S(1)}, f32[768]{0:T(1024)}, u32[]{:S(2)}) copy-start(f32[768]{0:T(1024)} %get-tuple-element.394) | copy-start | bytes 9220
  455.8 61.3 %reduce-scatter.49.cloned.1.call-start = ((), (), s32[]{:S(2)}) async-start(), calls=%async_computation.33 | async-start | bytes 1228800
  457.1 20.3 %copy-start.88 = (f32[32,20,768]{2,0,1:T(8,128)S(1)}, f32[32,20,768]{2,0,1:T(8,128)}, u32[]{:S(2)}) copy-start(f32[32,20,768]{2,0,1:T(8,128)} %get-tuple-element.442) | copy-start | bytes 5898244
  461.7 19.5 %copy-start.141 = (f32[8,20]{0,1:T(8,128)}, f32[8,20]{0,1:T(8,128)S(1)}, u32[]{:S(2)}) copy-start(f32[8,20]{0,1:T(8,128)S(1)} %negate_multiply_fusion.4) | copy-start | bytes 1924
  484.8 58.1 %reduce-scatter.35.cloned.1.call-start = ((), (), s32[]{:S(2)}) async-start(), calls=%async_computation.23 | async-start | bytes 2457600 | tf_op jit(solution)/shard_map/reduce_scatter | solution.py:204
  499.5 87.9 %all-gather.21.cloned.1.call-start = ((), (), s32[]{:S(2)}) async-start(), calls=%async_computation.24 | async-start | bytes 2211840 | tf_op jit(solution)/shard_map/all_gather | solution.py:195
  521.8 24.7 %copy-start.139 = (f32[8,20]{0,1:T(8,128)}, f32[8,20]{0,1:T(8,128)S(1)}, u32[]{:S(2)}) copy-start(f32[8,20]{0,1:T(8,128)S(1)} %negate_multiply_fusion.3) | copy-start | bytes 1924
  548.5 108.3 %reduce-scatter.51.cloned.1.call-start = ((), (), s32[]{:S(2)}) async-start(), calls=%async_computation.34 | async-start | bytes 1228800
  587.2 74.3 %reduce-scatter.37.cloned.1.call-start = ((), (), s32[]{:S(2)}) async-start(), calls=%async_computation.25 | async-start | bytes 2457600 | tf_op jit(solution)/shard_map/reduce_scatter | solution.py:204
  626.0 85.2 %all-gather.23.cloned.1.call-start = ((), (), s32[]{:S(2)}) async-start(), calls=%async_computation.26 | async-start | bytes 2211840 | tf_op jit(solution)/shard_map/all_gather | solution.py:195
  667.3 130.7 %reduce-scatter.41.cloned.1.call-start = ((), (), s32[]{:S(2)}) async-start(), calls=%async_computation.28 | async-start | bytes 5308416 | tf_op jit(solution)/shard_map/reduce_scatter | solution.py:452
  677.1 241.6 %all-reduce.3.cloned.1.call-start = ((), (), s32[]{:S(2)}) async-start(), calls=%async_computation.29 | async-start | bytes 196608 | tf_op jit(solution)/shard_map/psum | solution.py:447
  678.8 18.1 %copy-start.27 = (bf16[32,36,3,64]{3,2,1,0:T(4,128)(2,1)S(1)}, bf16[32,36,3,64]{3,2,1,0:T(4,128)(2,1)}, u32[]{:S(2)}) copy-start(bf16[32,36,3,64]{3,2,1,0:T(4,128)(2,1)} %reshape.1423) | copy-start | bytes 1327108
  678.8 18.1 %copy-start.91 = (f32[32,3,20]{2,1,0:T(4,128)S(1)}, f32[32,3,20]{2,1,0:T(4,128)}, u32[]{:S(2)}) copy-start(f32[32,3,20]{2,1,0:T(4,128)} %copy-done.90) | copy-start | bytes 23044
  733.5 213.8 %reduce-scatter.53.cloned.1.call-start = ((), (), s32[]{:S(2)}) async-start(), calls=%async_computation.35 | async-start | bytes 1228800
  736.8 243.9 %reduce-scatter.39.cloned.1.call-start = ((), (), s32[]{:S(2)}) async-start(), calls=%async_computation.27 | async-start | bytes 2457600 | tf_op jit(solution)/shard_map/reduce_scatter | solution.py:204
  755.6 307.8 %reduce-scatter.55.cloned.1.call-start = ((), (), s32[]{:S(2)}) async-start(), calls=%async_computation.36 | async-start | bytes 3981312
  795.5 185.2 %copy-start.24 = (f32[8,36,768]{2,1,0:T(8,128)S(1)}, f32[8,36,768]{2,1,0:T(8,128)}, u32[]{:S(2)}) copy-start(f32[8,36,768]{2,1,0:T(8,128)} %copy-done.23) | copy-start | bytes 2654212
  1065.9 46.4 %copy-start.126 = (f32[29,768]{1,0:T(8,128)S(1)}, f32[29,768]{1,0:T(8,128)}, u32[]{:S(2)}) copy-start(f32[29,768]{1,0:T(8,128)} %all-reduce.3.cloned.1.call-done) | copy-start | bytes 267268
  1065.9 46.4 %copy-start.128 = (f32[29,768]{1,0:T(8,128)S(1)}, f32[29,768]{1,0:T(8,128)}, u32[]{:S(2)}) copy-start(f32[29,768]{1,0:T(8,128)} %param.75) | copy-start | bytes 267268
  1065.9 46.4 %copy-start.160 = (f32[29,768]{1,0:T(8,128)S(1)}, f32[29,768]{1,0:T(8,128)}, u32[]{:S(2)}) copy-start(f32[29,768]{1,0:T(8,128)} %param.76) | copy-start | bytes 267268
  1065.9 46.4 %copy-start.161 = (f32[29,768]{1,0:T(8,128)S(1)}, f32[29,768]{1,0:T(8,128)}, u32[]{:S(2)}) copy-start(f32[29,768]{1,0:T(8,128)} %param.77) | copy-start | bytes 267268
  (188 other events, 618.1 us)
Sparse Core Ops, SparseCore 0:
  10.8 82.5 all-gather.10
  95.0 18.8 all-gather.8
  137.5 24.4 reduce-scatter.42
  164.6 30.6 reduce-scatter.28
  199.4 20.7 all-gather.14
  226.3 24.8 reduce-scatter.44
  253.9 30.6 reduce-scatter.30
  287.3 79.8 all-gather.12
  369.4 18.8 all-gather.16
  391.3 24.4 reduce-scatter.46
  418.6 30.6 reduce-scatter.32
  455.9 25.8 all-gather.18
  484.9 24.6 reduce-scatter.48
  512.2 30.6 reduce-scatter.34
  548.7 20.7 all-gather.20
  587.3 24.9 reduce-scatter.50
  626.1 31.0 reduce-scatter.36
  667.4 25.8 all-gather.22
  696.9 95.4 reduce-scatter.40
  798.4 120.2 all-reduce.2
  921.9 25.3 reduce-scatter.52
  950.0 30.6 reduce-scatter.38
  984.3 79.0 reduce-scatter.54
where the time goes:
time: 1150 us; the launch traced here: 1140 us
  waiting for transfers between devices  507 us (44%)
  local copies, waits for them, and re-layouts  224 us (19%)
  matrix products  175 us (15%)
  blocking collectives  110 us (10%)
  other arithmetic  95.9 us (8%)
  between operations  21.1 us (2%)
    psum x1, waiting for transfers between devices, body(): vector_total = lax.psum(vector_grad, ('dp', 'tensor'))  119 us
    unnamed x30, waiting for transfers between devices  115 us
    unnamed x458, local copies, waits for them, and re-layouts  94.9 us
    reduce_scatter x3, waiting for transfers between devices, collect(): lax.psum_scatter(region_terms.astype(jnp.bfloat16), 'tensor', scatter_dim...  73.1 us
    all_gather x1, waiting for transfers between devices, body(): lax.all_gather(attn_master.astype(jnp.bfloat16), 'dp', axis=2, tiled=True)  70.7 us
    all_gather x1, waiting for transfers between devices, body(): lax.all_gather(ffn_master.astype(jnp.bfloat16), 'dp', axis=2, tiled=True)  67.5 us
    dot_general x20, matrix products, product(): return jnp.dot(left_rows, right_matrix, preferred_element_type=jnp.float32)  61.1 us
    reduce_scatter x3, waiting for transfers between devices, give_back(): lax.psum_scatter(region_terms.astype(jnp.bfloat16), 'tensor', scatter_dim...  50.8 us
  transfers between devices with their start and end apart: 23, of which 13 were waited for; matrix products, arithmetic and copies ran while one was open for 35% of the time, Pallas kernels for 0%

commit v1 on v0

--- a/solution.py
+++ b/solution.py
@@ -1,12 +1,14 @@
+import functools
+
 import jax
 import jax.numpy as jnp
 from jax import lax
+from jax.experimental import pallas as pl
+from jax.experimental.pallas import tpu as pltpu
 from jax.sharding import PartitionSpec as P
 
 HD = 64
 STEP = 10
-
-
 NORM_EPSILON = 1e-06
 MASKED = -1000000000.0
 BETA_FIRST = 0.5
@@ -16,6 +18,846 @@
 RATE_MATRIX = 0.03
 RATE_VECTOR = 0.3
 CLIP_NORM = 1.0
+
+MESH = pl.DeviceIdType.MESH
+F32 = jnp.float32
+BF16 = jnp.bfloat16
+
+LP, RP = 24, 40
+WO, RO = 8 * LP, 8 * RP
+WALL, ALL = 2 * WO, 2 * WO + 2 * RO
+OWN = WO + RO
+D = 768
+NU = 7
+SEGS = ((0, 0, WO), (WO, WALL, RO))
+SIBS = ((0, WO, WO), (WO, WALL + RO, RO))
+
+
+def nn(a, b):
+    return jnp.dot(a, b, preferred_element_type=F32)
+
+
+def nt(a, b):
+    return lax.dot_general(a, b, (((1,), (1,)), ((), ())), preferred_element_type=F32)
+
+
+def tn(a, b):
+    return lax.dot_general(a, b, (((0,), (0,)), ((), ())), preferred_element_type=F32)
+
+
+def low_lanes(rows):
+    return lax.broadcasted_iota(jnp.int32, (rows, 128), 1) < HD
+
+
+def swap(v):
+    return pltpu.roll(v, HD, 1)
+
+
+def kernel(
+    sh_a, sh_f, xin, cot, vec, km,
+    out3, gx, g32, vgo, sqo, ra1, ra2, ra3, rb1, rb2, rb3,
+    W, H, DYA, DYB, Z, XS, YO, YS, YR, Q, K, V, F, PW, PR, A, GP, E, DO, G3, ST, ST3, VG, VR, VZ, SQ, SR, SZ,
+    lsem, cs, cr, ags, agr, rss, rsr, vs, vr,
+):
+    d = lax.axis_index("dp")
+    t = lax.axis_index("tensor")
+    z, x = d // 2, d % 2
+    y, c = t // 2, t % 2
+    oy, ox = 1 - y, 1 - x
+
+    def at(zz, xx, yy, cc):
+        return (zz * 2 + xx, yy * 2 + cc)
+
+    core_n, y_n, x_n = at(z, x, y, 1 - c), at(z, x, oy, c), at(z, ox, y, c)
+    zk = [(z + k) % 4 for k in range(4)]
+    z_n = [at(zk[k], x, y, c) for k in range(4)]
+
+    barrier = pltpu.get_barrier_semaphore()
+    partners = [core_n, y_n, x_n] + z_n[1:]
+    for p in partners:
+        pl.semaphore_signal(barrier, inc=1, device_id=p, device_id_type=MESH)
+    pl.semaphore_wait(barrier, len(partners))
+
+    def remote(src, dst, ss, rs, dev):
+        return pltpu.make_async_remote_copy(
+            src_ref=src, dst_ref=dst, send_sem=ss, recv_sem=rs, device_id=dev, device_id_type=MESH
+        )
+
+    def local(src, dst, sem):
+        return pltpu.make_async_copy(src, dst, sem)
+
+    rows_of = (pl.ds(0, 48), pl.ds(48, 48))
+
+    def shard(u, part, dy, dx, dz):
+        return W.at[u, y if dy == 0 else oy, zk[dz], x if dx == 0 else ox, rows_of[part], :]
+
+    def sid(dy, dx, dz):
+        return dy * 8 + dx * 4 + dz
+
+    ag_sends = {}
+
+    def ag_send(u, part, dy, dx, dz, way):
+        src = shard(u, part, dy, dx, dz)
+        if way == "x":
+            there, dev = sid(dy, 1 - dx, dz), x_n
+        elif way == "y":
+            there, dev = sid(1 - dy, dx, dz), y_n
+        else:
+            there, dev = sid(dy, dx, (dz - way) % 4), z_n[way]
+        n = ag_sends.setdefault((u, part), [])
+        cp = remote(src, src, ags.at[u, part, len(n)], agr.at[u, part, there], dev)
+        cp.start()
+        n.append(cp)
+
+    def ag_recv(u, part, dy, dx, dz):
+        src = shard(u, part, dy, dx, dz)
+        remote(src, src, ags.at[u, part, 15], agr.at[u, part, sid(dy, dx, dz)], x_n).wait_recv()
+
+    def ag0(u):
+        for part in (0, 1):
+            for k in (1, 3, 2):
+                ag_send(u, part, 0, 0, 0, k)
+            ag_send(u, part, 0, 0, 0, "x")
+            ag_send(u, part, 0, 0, 0, "y")
+
+    def ag1(u):
+        for k in (1, 3, 2):
+            for part in (0, 1):
+                ag_recv(u, part, 0, 0, k)
+                ag_send(u, part, 0, 0, k, "x")
+                ag_send(u, part, 0, 0, k, "y")
+
+    def ag2(u):
+        for k in (0, 1, 3, 2):
+            ag_recv(u, 0, 0, 1, k)
+            ag_send(u, 0, 0, 1, k, "y")
+            ag_recv(u, 1, 1, 0, k)
+            ag_send(u, 1, 1, 0, k, "x")
+
+    def ag3(u):
+        for k in (0, 1, 3, 2):
+            for dx in (0, 1):
+                ag_recv(u, 0, 1, dx, k)
+            for dy in (0, 1):
+                ag_recv(u, 1, dy, 1, k)
+        for part in (0, 1):
+            for cp in ag_sends[(u, part)]:
+                cp.wait_send()
+
+    core_count = [0]
+
+    def core_copy(src, dst):
+        i = core_count[0]
+        core_count[0] += 1
+        cp = remote(src, dst, cs.at[i], cr.at[i], core_n)
+        cp.start()
+        return cp
+
+    def share_rows(ref):
+        return [
+            core_copy(ref.at[pl.ds(0, WO)], ref.at[pl.ds(WO, WO)]),
+            core_copy(ref.at[pl.ds(WALL, RO)], ref.at[pl.ds(WALL + RO, RO)]),
+        ]
+
+    def wait_all(cps):
+        for cp in cps:
+            cp.wait()
+
+    def branch_sum(terms):
+        for o, r, n in SIBS:
+            YS[o : o + n, :] = terms(r, n).astype(BF16)
+        cp = core_copy(YS, YR)
+        for o, r, n in SEGS:
+            YO[o : o + n, :] = terms(r, n)
+        return cp
+
+    own_w = [
+        local(sh_a, W.at[pl.ds(0, 3), y, z, x], lsem.at[0]),
+        local(sh_f, W.at[pl.ds(3, 4), y, z, x], lsem.at[1]),
+        local(xin.at[pl.ds(0, WO)], H.at[0, pl.ds(0, WO)], lsem.at[2]),
+        local(xin.at[pl.ds(WO, RO)], H.at[0, pl.ds(WALL, RO)], lsem.at[3]),
+    ]
+    for cp in own_w:
+        cp.start()
+    for cp in own_w:
+        cp.wait()
+    ag0(0)
+    h0 = share_rows(H.at[0])
+    ag0(1)
+    for o, r, n in SEGS:
+        XS[o : o + n, :] = H[0, r : r + n, :].astype(F32)
+    VG[...] = jnp.zeros_like(VG)
+
+    def item_rows(n, half):
+        r = lax.broadcasted_iota(jnp.int32, (2 * n, 128), 0)
+        return ((r >= half) & (r < n)) | (r >= n + half)
+
+    lane_w = lax.broadcasted_iota(jnp.int32, (1, 128), 1)
+    item_w = lane_w >= LP
+    item_r = lane_w >= RP
+    good_r = (lane_w < 36) | ((lane_w >= RP) & (lane_w < RP + 36))
+    one = lambda m: jnp.where(m, 1.0, 0.0)
+    ir_w, ir_r = one(item_rows(2 * LP, LP)), one(item_rows(2 * RP, RP))
+    mask_wr = ((ir_w == one(item_r)) & good_r)[:, : 2 * RP]
+    mask_rr = ((ir_r == one(item_r)) & good_r)[:, : 2 * RP]
+    mask_ww = (ir_w == one(item_w))[:, : 2 * LP]
+    mask_rw = (ir_r == one(item_w))[:, : 2 * LP]
+
+    def word_keys(i):
+        return km[pl.ds(i, 1), :][:, : 2 * LP] > 0.5
+
+    def weights_of(u, yy, a, b):
+        return W[u, yy, :, :, :, a:b].reshape(D, b - a)
+
+    def project(sec, u, r, n):
+        h = H[sec, r : r + n, :]
+        r0 = nn(h, weights_of(u, 0, 0, 640)) + vec[32 + 2 * u : 33 + 2 * u, 0:640]
+        r1 = nn(h, weights_of(u, 1, 0, 640)) + vec[33 + 2 * u : 34 + 2 * u, 0:640]
+        lo = low_lanes(n)
+        rr = pl.ds(r, n)
+        Q[sec, rr, 0:128] = r0[:, 0:128].astype(BF16)
+        Q[sec, rr, 128:256] = r1[:, 0:128].astype(BF16)
+        m0, m1 = r0[:, 128:256], r1[:, 128:256]
+        Q[sec, rr, 256:384] = jnp.where(lo, m0, swap(m1)).astype(BF16)
+        K[sec, rr, 256:384] = jnp.where(lo, swap(m0), m1).astype(BF16)
+        K[sec, rr, 0:128] = r0[:, 256:384].astype(BF16)
+        K[sec, rr, 128:256] = r1[:, 256:384].astype(BF16)
+        V[sec, rr, 0:128] = r0[:, 384:512].astype(BF16)
+        V[sec, rr, 128:256] = r1[:, 384:512].astype(BF16)
+        V[sec, rr, 256:384] = jnp.where(lo, r0[:, 512:640], swap(r1[:, 512:640])).astype(BF16)
+
+    def stacked(ref, sec, rows, n, w):
+        v = ref[sec, rows, w * 128 : w * 128 + 128]
+        lo = low_lanes(n)
+        zero = jnp.zeros_like(v)
+        return jnp.concatenate([jnp.where(lo, v, zero), jnp.where(lo, zero, v)], axis=0)
+
+    def attend(sec, i, qr, nq, kr, nk, mask, pref):
+        lo = low_lanes(nq)
+        for w in range(3):
+            cols = slice(w * 128, w * 128 + 128)
+            s = nt(stacked(Q, sec, qr, nq, w), K[sec, kr, cols]) * (HD**-0.5)
+            s = jnp.where(mask, s, MASKED)
+            e = jnp.exp(s - jnp.max(s, axis=1, keepdims=True))
+            p = (e / jnp.sum(e, axis=1, keepdims=True)).astype(BF16)
+            pref[sec, pl.ds(pl.multiple_of((i * 3 + w) * 2 * nq, 32), 2 * nq), 0:nk] = p
+            o = nn(p, V[sec, kr, cols])
+            o = jnp.where(lo, o[:nq], o[nq:])
+            if w < 2:
+                F[sec, w, qr, 128:256] = o.astype(BF16)
+            else:
+                zero = jnp.zeros_like(o)
+                F[sec, 0, qr, 0:128] = jnp.where(lo, zero, swap(o)).astype(BF16)
+                F[sec, 1, qr, 0:128] = jnp.where(lo, zero, o).astype(BF16)
+
+    def pair_rows(i):
+        return (
+            pl.ds(pl.multiple_of(i * 2 * LP, 16), 2 * LP),
+            pl.ds(pl.multiple_of(WALL + i * 2 * RP, 16), 2 * RP),
+        )
+
+    def attention(sec):
+        def pair(i, carry):
+            wr, rr = pair_rows(i)
+            keys = word_keys(i)
+            if sec == 0:
+                attend(0, i, wr, 2 * LP, rr, 2 * RP, mask_wr, PW)
+                attend(0, i, rr, 2 * RP, wr, 2 * LP, mask_rw & keys, PR)
+            else:
+                attend(1, i, wr, 2 * LP, wr, 2 * LP, mask_ww & keys, PW)
+                attend(1, i, rr, 2 * RP, rr, 2 * RP, mask_rr, PR)
+            return carry
+
+        lax.fori_loop(0, 8, pair, 0)
+
+    def out_project(sec, unit_of):
+        def terms(r, n):
+            u = unit_of(r)
+            return nt(F[sec, 0, r : r + n, :], weights_of(u, 0, 512, 768)) + nt(
+                F[sec, 1, r : r + n, :], weights_of(u, 1, 512, 768)
+            )
+
+        return branch_sum(terms)
+
+    CH = 64
+
+    def over_own(fn):
+        for s, (o, r, n) in enumerate(SEGS):
+            def step(j, carry, o=o, r=r, s=s):
+                fn(pl.ds(pl.multiple_of(o + j * CH, CH), CH), pl.ds(pl.multiple_of(r + j * CH, CH), CH), s)
+                return carry
+
+            lax.fori_loop(0, n // CH, step, 0)
+
+    def stats(v):
+        mean = jnp.mean(v, axis=1, keepdims=True)
+        cen = v - mean
+        rstd = lax.rsqrt(jnp.mean(cen * cen, axis=1, keepdims=True) + NORM_EPSILON)
+        return cen * rstd, rstd
+
+    def row(k):
+        return vec[k : k + 1, :]
+
+    def norm_forward(zi, bias, gain, shift, nxt):
+        def fn(oo, rr, s):
+            v = YO[oo, :] + YR[oo, :].astype(F32) + row(bias[s]) + XS[oo, :]
+            Z[zi, oo, :] = v
+            xh, _ = stats(v)
+            out = xh * row(gain[s]) + row(shift[s])
+            if nxt is None:
+                YO[oo, :] = out
+            else:
+                XS[oo, :] = out
+                H[nxt, rr, :] = out.astype(BF16)
+
+        over_own(fn)
+
+    def norm_backward(zi, first, gain, rows_g, rows_s, rows_b, DY):
+        def fn(oo, rr, s):
+            if first:
+                dout = cot[oo, :].astype(F32)
+            else:
+                dout = XS[oo, :] + YO[oo, :] + YR[oo, :].astype(F32)
+            xh, rstd = stats(Z[zi, oo, :])
+            dx = dout * row(gain[s])
+            dz = rstd * (
+                dx - jnp.mean(dx, axis=1, keepdims=True) - xh * jnp.mean(dx * xh, axis=1, keepdims=True)
+            )
+            VG[rows_g[s] : rows_g[s] + 1, :] += jnp.sum(dout * xh, axis=0, keepdims=True)
+            VG[rows_s[s] : rows_s[s] + 1, :] += jnp.sum(dout, axis=0, keepdims=True)
+            VG[rows_b[s] : rows_b[s] + 1, :] += jnp.sum(dz, axis=0, keepdims=True)
+            XS[oo, :] = dz
+            DY[rr, :] = dz.astype(BF16)
+
+        over_own(fn)
+
+    def gate_rows(n, y2, r):
+        def step(j, carry):
+            jj = pl.ds(pl.multiple_of(j * 16, 16), 16)
+            u = YO[jj, :]
+            half = 0.5 * (1.0 + lax.erf(u * (0.5**0.5)))
+            A[y2, pl.ds(pl.multiple_of(r + j * 16, 16), 16), :] = (u * half).astype(BF16)
+            slope = half + u * (jnp.exp(-0.5 * u * u) * 0.3989422804014327)
+            GP[y2, pl.ds(pl.multiple_of(r + j * 16, 16), 16), :] = slope.astype(BF16)
+            return carry
+
+        lax.fori_loop(0, n // 16, step, 0)
+
+    STREAM = ((0, WO), (WALL, RO))
+
+    def feed_up(s):
+        r0, n = STREAM[s]
+        for half in range(2):
+            r = r0 + half * n
+            for y2 in range(2):
+                YO[0:n, :] = nn(H[2, r : r + n, :], weights_of(3 + 2 * s, y2, 0, D)) + vec[
+                    38 + 2 * s + y2 : 39 + 2 * s + y2, :
+                ]
+                gate_rows(n, y2, r)
+
+    def feed_down(r, n):
+        u = 4 if r < WALL else 6
+        return nt(A[0, r : r + n, :], weights_of(u, 0, 0, D)) + nt(A[1, r : r + n, :], weights_of(u, 1, 0, D))
+
+    def put_grad(u, yy, m, value):
+        W[u, yy, 2 * m : 2 * m + 2, :, :, :] = value.astype(BF16).reshape(2, 2, 96, D)
+
+    def feed_back(s, DY):
+        r0, n = STREAM[s]
+        r1 = r0 + 2 * n
+        u1, u2 = 3 + 2 * s, 4 + 2 * s
+        for y2 in range(2):
+            total = jnp.zeros((1, D), F32)
+            for half in range(2):
+                r = r0 + half * n
+                du = nt_rows_gate(DY, u2, y2, r, n)
+                total = total + jnp.sum(du.astype(F32), axis=0, keepdims=True)
+            k = 21 + 2 * s + y2
+            VG[k : k + 1, :] = total
+            for m in range(2):
+                put_grad(u2, y2, m, tn(DY[r0:r1, m * 384 : m * 384 + 384], A[y2, r0:r1, :]))
+
+    def nt_rows_gate(DY, u2, y2, r, n):
+        da = nn(DY[r : r + n, :], weights_of(u2, y2, 0, D))
+        du = (da * GP[y2, r : r + n, :].astype(F32)).astype(BF16)
+        GP[y2, r : r + n, :] = du
+        return du
+
+    def feed_hidden_back(r, n):
+        u = 3 if r < WALL else 5
+        return nt(GP[0, r : r + n, :], weights_of(u, 0, 0, D)) + nt(GP[1, r : r + n, :], weights_of(u, 1, 0, D))
+
+    def feed_up_grad(s):
+        r0, n = STREAM[s]
+        r1 = r0 + 2 * n
+        for y2 in range(2):
+            for m in range(2):
+                put_grad(3 + 2 * s, y2, m, tn(H[2, r0:r1, m * 384 : m * 384 + 384], GP[y2, r0:r1, :]))
+
+    def grad_mixture(u, r, n, DY):
+        dy = DY[r : r + n, :]
+        r0 = nn(dy, weights_of(u, 0, 512, 768))
+        r1 = nn(dy, weights_of(u, 1, 512, 768))
+        rr = pl.ds(r, n)
+        DO[0, rr, 0:128] = r0[:, 128:256].astype(BF16)
+        DO[0, rr, 128:256] = r1[:, 128:256].astype(BF16)
+        DO[0, rr, 256:384] = jnp.where(low_lanes(n), swap(r0[:, 0:128]), r1[:, 0:128]).astype(BF16)
+
+    def attend_back(sec, i, qr, nq, kr, nk, pref):
+        lo = low_lanes(nq)
+        dqs, dks, dvs = [], [], []
+        for w in range(3):
+            cols = slice(w * 128, w * 128 + 128)
+            p = pref[sec, pl.ds(pl.multiple_of((i * 3 + w) * 2 * nq, 32), 2 * nq), 0:nk]
+            dos = stacked(DO, 0, qr, nq, w)
+            dp = nt(dos, V[sec, kr, cols])
+            pf = p.astype(F32)
+            ds = (pf * (dp - jnp.sum(pf * dp, axis=1, keepdims=True))).astype(BF16)
+            dq = nn(ds, K[sec, kr, cols]) * (HD**-0.5)
+            dqs.append(jnp.where(lo, dq[:nq], dq[nq:]))
+            dks.append(tn(ds, stacked(Q, sec, qr, nq, w)) * (HD**-0.5))
+            dvs.append(tn(p, dos))
+        return dqs, dks, dvs
+
+    def put_pack(rows, n, dqs, dks, dvs):
+        lo = low_lanes(n)
+        zero = jnp.zeros((n, 128), F32)
+        for w in range(2):
+            E[w, rows, 0:128] = dqs[w].astype(BF16)
+            E[w, rows, 256:384] = dks[w].astype(BF16)
+            E[w, rows, 384:512] = dvs[w].astype(BF16)
+        E[0, rows, 128:256] = jnp.where(lo, dqs[2], swap(dks[2])).astype(BF16)
+        E[1, rows, 128:256] = jnp.where(lo, swap(dqs[2]), dks[2]).astype(BF16)
+        E[0, rows, 512:640] = jnp.where(lo, dvs[2], zero).astype(BF16)
+        E[1, rows, 512:640] = jnp.where(lo, swap(dvs[2]), zero).astype(BF16)
+
+    def attention_back(sec):
+        def pair(i, carry):
+            wr, rr = pair_rows(i)
+            if sec == 0:
+                qw, kr_, vr_ = attend_back(0, i, wr, 2 * LP, rr, 2 * RP, PW)
+                qr_, kw, vw = attend_back(0, i, rr, 2 * RP, wr, 2 * LP, PR)
+            else:
+                qw, kw, vw = attend_back(1, i, wr, 2 * LP, wr, 2 * LP, PW)
+                qr_, kr_, vr_ = attend_back(1, i, rr, 2 * RP, rr, 2 * RP, PR)
+            put_pack(wr, 2 * LP, qw, kw, vw)
+            put_pack(rr, 2 * RP, qr_, kr_, vr_)
+            return carry
+
+        lax.fori_loop(0, 8, pair, 0)
+
+    def branch_back(unit_of):
+        def terms(r, n):
+            u = unit_of(r)
+            return nt(E[0, r : r + n, :], weights_of(u, 0, 0, 640)) + nt(E[1, r : r + n, :], weights_of(u, 1, 0, 640))
+
+        return branch_sum(terms)
+
+    def attn_grad(sec, u, r0, r1, DY):
+        for yy in range(2):
+            k = 15 + 2 * u + yy
+            VG[k : k + 1, 0:640] = jnp.sum(E[yy, r0:r1, :].astype(F32), axis=0, keepdims=True)
+            for m in range(2):
+                mc = slice(m * 384, m * 384 + 384)
+                a = tn(H[sec, r0:r1, mc], E[yy, r0:r1, :])
+                b = tn(DY[r0:r1, mc], F[sec, yy, r0:r1, :])
+                put_grad(u, yy, m, jnp.concatenate([a[:, 0:512], a[:, 512:640] + b[:, 0:128], b[:, 128:256]], axis=1))
+
+    top, bot = rows_of
+    rs_sends = []
+
+    def rs_send(u, k, src, dst, dev):
+        cp = remote(src, dst, rss.at[u, k], rsr.at[u, k], dev)
+        cp.start()
+        rs_sends.append(cp)
+
+    def rs_recv(u, k, dst):
+        remote(dst, dst, rss.at[u, k], rsr.at[u, k], x_n).wait_recv()
+
+    def rs1(u):
+        rs_send(u, 0, W.at[u, oy, :, :, top, :], ra1.at[u], y_n)
+        rs_send(u, 1, W.at[u, :, :, ox, bot, :], rb1.at[u], x_n)
+
+    def add_in(dst, stage):
+        def step(j, carry):
+            dst(j)[...] = (dst(j)[...].astype(F32) + stage[j].astype(F32)).astype(BF16)
+            return carry
+
+        lax.fori_loop(0, 4, step, 0)
+
+    def rs2(u):
+        rs_recv(u, 0, ra1.at[u])
+        a = local(ra1.at[u, :, ox], ST.at[0], lsem.at[0])
+        a.start()
+        rs_recv(u, 1, rb1.at[u])
+        b = local(rb1.at[u, oy], ST.at[1], lsem.at[1])
+        b.start()
+        a.wait()
+        add_in(lambda j: W.at[u, y, j, ox, top, :], ST.at[0])
+        rs_send(u, 2, W.at[u, y, :, ox, top, :], ra2.at[u], x_n)
+        b.wait()
+        add_in(lambda j: W.at[u, oy, j, x, bot, :], ST.at[1])
+        rs_send(u, 3, W.at[u, oy, :, x, bot, :], rb2.at[u], y_n)
+
+    def rs3(u):
+        rs_recv(u, 2, ra2.at[u])
+        rs_recv(u, 3, rb2.at[u])
+        cps = [
+            local(ra1.at[u, :, x], ST.at[0], lsem.at[0]),
+            local(ra2.at[u], ST.at[1], lsem.at[1]),
+            local(rb1.at[u, y], ST.at[2], lsem.at[2]),
+            local(rb2.at[u], ST.at[3], lsem.at[3]),
+        ]
+        for cp in cps:
+            cp.start()
+        for cp in cps:
+            cp.wait()
+        for part in (0, 1):
+            rows = rows_of[part]
+
+            def step(j, carry, part=part, rows=rows):
+                w = W.at[u, y, j, x, rows, :]
+                w[...] = (
+                    w[...].astype(F32) + ST[2 * part, j].astype(F32) + ST[2 * part + 1, j].astype(F32)
+                ).astype(BF16)
+                return carry
+
+            own = (
+                W[u, y, z, x, rows, :].astype(F32) + ST[2 * part, z].astype(F32) + ST[2 * part + 1, z].astype(F32)
+            )
+            lax.fori_loop(0, 4, step, 0)
+            G3[u, rows, :] = own
+        for part, dst in ((0, ra3), (1, rb3)):
+            for k in (1, 2, 3):
+                rs_send(
+                    u, 4 + 3 * part + k - 1, W.at[u, y, zk[k], x, rows_of[part], :], dst.at[u, k - 1], z_n[k]
+                )
+
+    def rs4(u):
+        for part, dst in ((0, ra3), (1, rb3)):
+            for k in (1, 2, 3):
+                rs_recv(u, 4 + 3 * part + k - 1, dst.at[u, k - 1])
+        a = local(ra3.at[u], ST3.at[0], lsem.at[0])
+        b = local(rb3.at[u], ST3.at[1], lsem.at[1])
+        a.start()
+        b.start()
+        a.wait()
+        b.wait()
+        for part in (0, 1):
+            g = G3[u, rows_of[part], :]
+            for k in range(3):
+                g = g + ST3[part, k].astype(F32)
+            G3[u, rows_of[part], :] = g
+            SQ[...] += jnp.sum((g * g).reshape(6, 8, D), axis=0)
+
+    ag1(0)
+    ag0(2)
+    ag1(1)
+    ag2(0)
+    ag0(3)
+    ag1(2)
+    ag2(1)
+    wait_all(h0)
+    ag3(0)
+    chunks = ((0, WALL), (WALL, RO), (WALL + RO, RO))
+    for r, n in chunks:
+        project(0, 0, r, n)
+    ag0(4)
+    ag1(3)
+    ag2(2)
+    attention(0)
+    cp = out_project(0, lambda r: 0)
+    cp.wait()
+    norm_forward(0, (6, 6), (9, 9), (14, 14), 1)
+    h1 = share_rows(H.at[1])
+    ag0(5)
+    ag1(4)
+    ag2(3)
+    ag3(1)
+    ag3(2)
+    wait_all(h1)
+    for r, n in chunks:
+        project(1, 1 if r < WALL else 2, r, n)
+    ag0(6)
+    ag1(5)
+    ag2(4)
+    attention(1)
+    cp = out_project(1, lambda r: 1 if r < WALL else 2)
+    cp.wait()
+    norm_forward(1, (7, 8), (10, 11), (15, 16), 2)
+    h2 = share_rows(H.at[2])
+    ag1(6)
+    ag2(5)
+    ag3(3)
+    wait_all(h2)
+    feed_up(0)
+    ag2(6)
+    ag3(4)
+    ag3(5)
+    feed_up(1)
+    ag3(6)
+    cp = branch_sum(feed_down)
+    cp.wait()
+    norm_forward(2, (19, 20), (12, 13), (17, 18), None)
+    oc = local(YO, out3, lsem.at[4])
+    oc.start()
+
+    norm_backward(2, True, (12, 13), (3, 4), (8, 9), (13, 14), DYA)
+    wait_all(share_rows(DYA))
+    oc.wait()
+    feed_back(1, DYA)
+    rs1(6)
+    feed_back(0, DYA)
+    rs1(4)
+    cp = branch_sum(feed_hidden_back)
+    feed_up_grad(1)
+    rs1(5)
+    feed_up_grad(0)
+    rs1(3)
+    cp.wait()
+    norm_backward(1, False, (10, 11), (1, 2), (6, 7), (11, 12), DYB)
+    wait_all(share_rows(DYB))
+    for r, n in chunks:
+        grad_mixture(1 if r < WALL else 2, r, n, DYB)
+    attention_back(1)
+    cp = branch_back(lambda r: 1 if r < WALL else 2)
+    attn_grad(1, 2, WALL, ALL, DYB)
+    rs1(2)
+    attn_grad(1, 1, 0, WALL, DYB)
+    rs1(1)
+    cp.wait()
+    norm_backward(0, False, (9, 9), (0, 0), (5, 5), (10, 10), DYA)
+    dy0 = share_rows(DYA)
+    rs2(6)
+    rs2(4)
+    wait_all(dy0)
+    for r, n in chunks:
+        grad_mixture(0, r, n, DYA)
+    attention_back(0)
+    rs2(5)
+    cp = branch_back(lambda r: 0)
+    attn_grad(0, 0, 0, ALL, DYA)
+    rs1(0)
+    cp.wait()
+
+    def finish(oo, rr, s):
+        XS[oo, :] += YO[oo, :] + YR[oo, :].astype(F32)
+
+    over_own(finish)
+    gc = local(XS, gx, lsem.at[4])
+    gc.start()
+
+    def vsend(k, src, dst, dev):
+        cp = remote(src, dst, vs.at[k], vr.at[k], dev)
+        cp.start()
+        return cp
+
+    def total(k, buf, slot, zbuf, out):
+        cp = vsend(k, buf.at[0], slot.at[0], y_n)
+        cp.wait()
+        buf[1] = buf[0] + slot[0]
+        cp = vsend(k + 1, buf.at[1], slot.at[1], x_n)
+        cp.wait()
+        zbuf[z] = buf[1] + slot[1]
+        cps = [vsend(k + 1 + j, zbuf.at[z], zbuf.at[z], z_n[j]) for j in (1, 2, 3)]
+        for cp in cps:
+            cp.wait()
+        out[c] = zbuf[0] + zbuf[1] + zbuf[2] + zbuf[3]
+        vsend(k + 5, out.at[c], out.at[c], core_n).wait()
+
+    SQ[...] = jnp.zeros_like(SQ)
+    rs2(3)
+    rs3(6)
+    rs2(2)
+    rs3(4)
+    VR[2] = VG[...]
+    total(0, VR.at[pl.ds(2, 2)], VR, VZ, vgo)
+    rs3(5)
+    rs2(1)
+    rs3(3)
+    rs4(6)
+    rs2(0)
+    rs3(2)
+    rs4(4)
+    rs3(1)
+    rs4(5)
+    rs3(0)
+    rs4(3)
+    rs4(2)
+    rs4(1)
+    rs4(0)
+    g = local(G3, g32, lsem.at[0])
+    g.start()
+    SR[2] = jnp.full((8, 128), jnp.sum(SQ[...]), F32)
+    total(6, SR.at[pl.ds(2, 2)], SR, SZ, sqo)
+    for cp in rs_sends:
+        cp.wait_send()
+    g.wait()
+    gc.wait()
+
+
+def fused(sh_a, sh_f, xin, cot, vec, km):
+    anywhere = pl.BlockSpec(memory_space=pl.ANY)
+    vmem = pl.BlockSpec(memory_space=pltpu.VMEM)
+    s = jax.ShapeDtypeStruct
+    dma = pltpu.SemaphoreType.DMA
+    outs = [
+        (s((OWN, D), F32), anywhere),
+        (s((OWN, D), F32), anywhere),
+        (s((NU, 96, D), F32), anywhere),
+        (s((2, 32, D), F32), vmem),
+        (s((2, 8, 128), F32), vmem),
+        (s((NU, 4, 2, 48, D), BF16), anywhere),
+        (s((NU, 4, 48, D), BF16), anywhere),
+        (s((NU, 3, 48, D), BF16), anywhere),
+        (s((NU, 2, 4, 48, D), BF16), anywhere),
+        (s((NU, 4, 48, D), BF16), anywhere),
+        (s((NU, 3, 48, D), BF16), anywhere),
+    ]
+    scratch = [
+        pltpu.VMEM((NU, 2, 4, 2, 96, D), BF16),
+        pltpu.VMEM((3, ALL, D), BF16),
+        pltpu.VMEM((ALL, D), BF16),
+        pltpu.VMEM((ALL, D), BF16),
+        pltpu.VMEM((3, OWN, D), F32),
+        pltpu.VMEM((OWN, D), F32),
+        pltpu.VMEM((OWN, D), F32),
+        pltpu.VMEM((OWN, D), BF16),
+        pltpu.VMEM((OWN, D), BF16),
+        pltpu.VMEM((2, ALL, 384), BF16),
+        pltpu.VMEM((2, ALL, 384), BF16),
+        pltpu.VMEM((2, ALL, 384), BF16),
+        pltpu.VMEM((2, 2, ALL, 256), BF16),
+        pltpu.VMEM((2, 8 * 3 * 4 * LP, 128), BF16),
+        pltpu.VMEM((2, 8 * 3 * 4 * RP, 128), BF16),
+        pltpu.VMEM((2, ALL, D), BF16),
+        pltpu.VMEM((2, ALL, D), BF16),
+        pltpu.VMEM((2, ALL, 640), BF16),
+        pltpu.VMEM((1, ALL, 384), BF16),
+        pltpu.VMEM((NU, 96, D), F32),
+        pltpu.VMEM((4, 4, 48, D), BF16),
+        pltpu.VMEM((2, 3, 48, D), BF16),
+        pltpu.VMEM((32, D), F32),
+        pltpu.VMEM((4, 32, D), F32),
+        pltpu.VMEM((4, 32, D), F32),
+        pltpu.VMEM((8, D), F32),
+        pltpu.VMEM((4, 8, 128), F32),
+        pltpu.VMEM((4, 8, 128), F32),
+        dma((5,)),
+        dma((18,)),
+        dma((18,)),
+        dma((NU, 2, 16)),
+        dma((NU, 2, 16)),
+        dma((NU, 10)),
+        dma((NU, 10)),
+        dma((12,)),
+        dma((12,)),
+    ]
+    return pl.pallas_call(
+        kernel,
+        out_shape=[o[0] for o in outs],
+        in_specs=[anywhere, anywhere, anywhere, vmem, vmem, vmem],
+        out_specs=[o[1] for o in outs],
+        scratch_shapes=scratch,
+        compiler_params=pltpu.CompilerParams(
+            collective_id=0, has_side_effects=True, vmem_limit_bytes=62 * 1024 * 1024
+        ),
+    )(sh_a, sh_f, xin, cot, vec, km)
+
+
+def adam_update(master, first, second, grad, rate):
+    first = BETA_FIRST * first + (1.0 - BETA_FIRST) * grad
+    second = BETA_SECOND * second + (1.0 - BETA_SECOND) * grad * grad
+    first_hat = first / (1.0 - BETA_FIRST**STEP)
+    second_hat = second / (1.0 - BETA_SECOND**STEP)
+    fresh = master - rate * (first_hat / (jnp.sqrt(second_hat) + ADAM_EPSILON) + WEIGHT_DECAY * master)
+    return (fresh, first, second)
+
+
+def fast_body(
+    lang_in, vis_in, word_lengths, lang_cot, vis_cot,
+    attn_master, attn_first, attn_second, ffn_master, ffn_first, ffn_second,
+    vectors, vector_first, vector_second,
+):
+    t = lax.axis_index("tensor")
+    y, c = t // 2, t % 2
+    items, words, width = lang_in.shape
+    regions = vis_in.shape[1]
+    head = attn_master.shape[3]
+
+    def rows(word_part, region_part):
+        w = jnp.pad(word_part, ((0, 0), (0, LP - words), (0, 0))).reshape(WO, width)
+        r = jnp.pad(region_part, ((0, 0), (0, RP - regions), (0, 0))).reshape(RO, width)
+        return jnp.concatenate([w, r], axis=0)
+
+    def unrows(v):
+        w = v[:WO].reshape(items, LP, width)[:, :words]
+        r = v[WO:].reshape(items, RP, width)[:, :regions]
+        return w, r
+
+    low = attn_master.astype(BF16)
+    wq, wk, wv, wo = (low[:, j] for j in range(4))
+    sh_a = jnp.concatenate([wq, wk[..., 128:], wk[..., :128], wv, wo[..., 128:], wo[..., :128]], axis=-1)
+    sh_f = ffn_master.astype(BF16).reshape(4, *ffn_master.shape[2:])
+    own_len = lax.dynamic_slice_in_dim(word_lengths, t * items, items)
+    sib_len = lax.dynamic_slice_in_dim(word_lengths, (2 * y + 1 - c) * items, items)
+    keep = jnp.arange(words, dtype=jnp.int32)[None, :] < own_len[:, None]
+    xin = rows(lang_in, vis_in)
+    cot = rows(jnp.where(keep[:, :, None], lang_cot, 0), vis_cot)
+    lens = jnp.concatenate([own_len, sib_len])
+    km = (jnp.arange(LP, dtype=jnp.int32)[None, :] < lens[:, None]).astype(F32).reshape(8, 2 * LP)
+    km = jnp.pad(km, ((0, 0), (0, 128 - 2 * LP)))
+    mine = lambda v: jnp.where(c == 0, v[..., 0, :], v[..., 1, :])
+    heads = mine(vectors[0:6].reshape(2, 3, 2, 2, head))
+    zero = jnp.zeros_like(heads[0])
+    bias = jnp.concatenate([heads[0], zero, heads[1], zero], axis=-1).reshape(6, width)
+    hidden = mine(vectors[21:29].reshape(2, 2, 2, width)).reshape(4, width)
+    vec = jnp.concatenate([vectors, jnp.zeros((3, width), F32), bias, hidden], axis=0)
+    vec = jnp.pad(vec, ((0, 48 - vec.shape[0]), (0, 0)))
+
+    outs = fused(sh_a, sh_f, xin, cot, vec, km)
+    out3, gx, g32, vg, sq = outs[:5]
+
+    lang_out, vis_out = unrows(out3)
+    lang_grad, vis_grad = unrows(gx)
+    ga = g32[:3]
+    attn_share = jnp.stack(
+        [
+            ga[..., 0:192],
+            jnp.concatenate([ga[..., 256:384], ga[..., 192:256]], axis=-1),
+            ga[..., 384:576],
+            jnp.concatenate([ga[..., 640:768], ga[..., 576:640]], axis=-1),
+        ],
+        axis=1,
+    )
+    ffn_share = g32[3:].reshape(ffn_master.shape)
+    both = vg[0] + vg[1]
+    packs = vg[:, 15:21].reshape(2, 3, 2, width)
+    pick = lambda v: v.transpose(1, 2, 0, 3).reshape(3, width)
+    hid = vg[:, 21:25].reshape(2, 2, 2, width).transpose(1, 2, 0, 3).reshape(8, width)
+    vector_total = jnp.concatenate(
+        [pick(packs[..., 0:192]), pick(packs[..., 384:576]), both[10:13], both[0:5], both[5:10], both[13:15], hid],
+        axis=0,
+    )
+    square_total = sq[0, 0, 0] + sq[1, 0, 0]
+    grad_norm = jnp.sqrt(square_total + jnp.sum(vector_total * vector_total))
+    clip_scale = CLIP_NORM / jnp.maximum(grad_norm, CLIP_NORM)
+    vector_clipped = vector_total * clip_scale
+    attn_new, attn_first_new, attn_second_new = adam_update(
+        attn_master, attn_first, attn_second, attn_share * clip_scale, RATE_MATRIX
+    )
+    ffn_new, ffn_first_new, ffn_second_new = adam_update(
+        ffn_master, ffn_first, ffn_second, ffn_share * clip_scale, RATE_MATRIX
+    )
+    vector_new, vector_first_new, vector_second_new = adam_update(
+        vectors, vector_first, vector_second, vector_clipped, RATE_VECTOR
+    )
+    return (
+        lang_out, vis_out, lang_grad, vis_grad,
+        attn_new, attn_first_new, attn_second_new, attn_new.astype(BF16),
+        ffn_new, ffn_first_new, ffn_second_new, ffn_new.astype(BF16),
+        vector_new, vector_first_new, vector_second_new, vector_clipped[19:21], grad_norm,
+    )
 
 
 def normalize(inputs, norm_gain, norm_shift):
@@ -207,18 +1049,7 @@
     )
 
 
-def adam_update(master, first, second, grad, rate):
-    first = BETA_FIRST * first + (1.0 - BETA_FIRST) * grad
-    second = BETA_SECOND * second + (1.0 - BETA_SECOND) * grad * grad
-    first_hat = first / (1.0 - BETA_FIRST**STEP)
-    second_hat = second / (1.0 - BETA_SECOND**STEP)
-    fresh = master - rate * (
-        first_hat / (jnp.sqrt(second_hat) + ADAM_EPSILON) + WEIGHT_DECAY * master
-    )
-    return (fresh, first, second)
-
-
-def body(
+def general_body(
     lang_in,
     vis_in,
     word_lengths,
@@ -489,8 +1320,9 @@
 
 
 def solution(mesh):
+    tuned = dict(mesh.shape) == {"dp": 8, "tensor": 4}
     return jax.shard_map(
-        body,
+        fast_body if tuned else general_body,
         mesh=mesh,
         in_specs=(
             P(("dp", "tensor"), None, None),

time: 1150 us -> 431 us (0.37)
  waiting for transfers between devices: 507 us -> 0 us
  Pallas kernels: 0 us -> 387 us
  local copies, waits for them, and re-layouts: 224 us -> 24.9 us
  matrix products: 175 us -> 0 us
  blocking collectives: 110 us -> 0 us
  other arithmetic: 95.9 us -> 9.9 us
  between operations: 21.1 us -> 4.81 us
    pallas_call x0 -> x1, Pallas kernels: none -> 387 us  [fused(): pl.pallas_call(kernel, out_shape=[o[0] for o in outs], in_specs=[anywhere...]
    dot_general x88 -> x0, matrix products: 175 us -> none  [the longest x20 61.1 us: product(): return jnp.dot(left_rows, right_matrix, preferred_element_type=jnp.float32)]
    all_gather x8 -> x0, waiting for transfers between devices: 150 us -> none  [the longest x1 70.7 us: body(): lax.all_gather(attn_master.astype(jnp.bfloat16), 'dp', axis=2, tiled=True)]
    reduce_scatter x7 -> x0, waiting for transfers between devices: 124 us -> none  [the longest x3 73.1 us: collect(): lax.psum_scatter(region_terms.astype(jnp.bfloat16), 'tensor', scatter_dim...]
    psum x1 -> x0, waiting for transfers between devices: 119 us -> none  [body(): vector_total = lax.psum(vector_grad, ('dp', 'tensor'))]
    unnamed x30 -> x0, waiting for transfers between devices: 115 us -> none
    unnamed x458 -> x46, local copies, waits for them, and re-layouts: 94.9 us -> 12.9 us
    all_gather x6 -> x0, blocking collectives: 69.6 us -> none  [the longest x3 38.9 us: fetch_rows(): lax.all_gather(word_grads.astype(jnp.bfloat16), 'tensor', axis=0, tiled=T...]
  transfers between devices with their start and end apart: 23 -> 0, of which waited for: 13 -> 0; matrix products, arithmetic and copies ran while one was open for 35% -> 0% of each run, Pallas kernels for 0% -> 0%
where the time goes in v1:
time: 431 us; the launch traced here: 427 us
  Pallas kernels  387 us (90%)
  local copies, waits for them, and re-layouts  24.9 us (6%)
  other arithmetic  9.9 us (2%)
  between operations  4.81 us (1%)
    pallas_call x1, Pallas kernels, fused(): pl.pallas_call(kernel, out_shape=[o[0] for o in outs], in_specs=[anywhere...  387 us
    unnamed x46, local copies, waits for them, and re-layouts  12.9 us

profile of v1, /device:TPU:0, one launch (start us, length us, event | category | flops | bytes accessed | tf_op | source)
XLA Modules:
  0.0 426.6 jit_solution(4727337589300942047)
XLA Ops:
  0.7 0.8 fusion.14
  1.6 0.1 lt.55
  1.7 0.1 concatenate.46
  1.8 0.1 concatenate.45
  1.9 0.1 lt.59
  2.0 0.6 pad_convert_fusion.km
  2.6 0.8 slice.162
  3.5 0.7 slice.157
  4.3 0.1 reshape.142
  4.5 1.0 pad_maximum_fusion.2
  5.5 0.7 pad.28.vec
  6.2 0.1 broadcast_select_fusion
  6.5 0.8 copy-done.11
  7.3 0.1 copy.136
  7.5 0.1 copy.138
  7.6 1.2 pad_maximum_fusion
  8.9 0.6 copy-done
  9.4 0.9 convert_element_type.27
  10.5 0.9 concatenate.38.sh_a
  11.4 386.9 %shard_map.269 = (f32[512,768]{1,0:T(8,128)}, f32[512,768]{1,0:T(8,128)}, f32[7,96,768]{2,1,0:T(8,128)}, f32[2,32,768]{2,1,0:T(8,128)}, f32[2,8,128]{2,1,0:T(8,1...) custom-call(bf16[3,96,768]{2,1,0:T(8,128)(2,1)} %concatenate.38.sh_a, ...), custom_call_target="tpu_custom_call" | custom-call | tf_op jit(solution)/shard_map/pallas_call | solution.py:756
  398.4 1.3 fusion.13
  400.9 0.9 slice.192
  401.9 0.9 slice.181
  402.8 1.0 slice_add_fusion
  403.8 0.1 reshape.150
  403.9 0.1 reshape.149
  404.0 0.7 concatenate.50
  404.7 0.6 multiply_reduce_fusion
  406.1 0.8 multiply_subtract_fusion.2
  406.9 0.6 slice.218
  407.5 1.2 fusion.9
  408.7 1.0 fusion.8
  409.9 1.2 copy.132
  411.1 0.9 copy.131
  412.2 1.2 copy.134
  413.3 0.9 copy.133
  414.4 0.1 slice_multiply_fusion
  414.5 1.1 copy-done.7
  415.5 0.4 copy-done.3
  415.9 0.4 copy-done.6
  416.3 0.9 fusion.6
  417.2 0.9 copy.126
  418.1 1.1 copy.123
  419.2 1.1 copy.124
  420.3 1.1 copy.125
  421.3 0.6 copy-done.8
  421.9 0.4 copy-done.9
  422.3 2.6 fusion.4
  (70 shorter events, 1.2 us)
Async XLA Ops:
  0.7 5.5 %copy-start.13 = (bf16[8,20,768]{2,0,1:T(8,128)(2,1)S(1)}, bf16[8,20,768]{2,0,1:T(8,128)(2,1)}, u32[]{:S(2)}) copy-start(bf16[8,20,768]{2,0,1:T(8,128)(2,1)} %param.17) | copy-start | bytes 737284
  4.4 2.0 copy-start.14
  6.3 1.0 copy-start.11
  6.4 1.0 copy-start.12
  7.6 1.8 copy-start
  8.8 1.5 copy-start.2
  398.3 7.7 %copy-start.10 = (f32[29,768]{1,0:T(8,128)S(1)}, f32[29,768]{1,0:T(8,128)}, u32[]{:S(2)}) copy-start(f32[29,768]{1,0:T(8,128)} %param.25) | copy-start | bytes 267268
  398.4 7.7 %copy-start.15 = (f32[29,768]{1,0:T(8,128)S(1)}, f32[29,768]{1,0:T(8,128)}, u32[]{:S(2)}) copy-start(f32[29,768]{1,0:T(8,128)} %param.26) | copy-start | bytes 267268
  398.4 7.7 %copy-start.16 = (f32[29,768]{1,0:T(8,128)S(1)}, f32[29,768]{1,0:T(8,128)}, u32[]{:S(2)}) copy-start(f32[29,768]{1,0:T(8,128)} %param.27) | copy-start | bytes 267268
  407.5 2.3 copy-start.5
  409.9 2.1 copy-start.4
  412.1 2.1 copy-start.1
  414.3 1.3 copy-start.7
  414.3 1.6 copy-start.3
  414.3 1.9 copy-start.6
  420.2 1.7 copy-start.8
  420.2 2.0 copy-start.9

commit v2 on v0

--- a/solution.py
+++ b/solution.py
@@ -1,12 +1,14 @@
+import functools
+
 import jax
 import jax.numpy as jnp
 from jax import lax
+from jax.experimental import pallas as pl
+from jax.experimental.pallas import tpu as pltpu
 from jax.sharding import PartitionSpec as P
 
 HD = 64
 STEP = 10
-
-
 NORM_EPSILON = 1e-06
 MASKED = -1000000000.0
 BETA_FIRST = 0.5
@@ -16,6 +18,1246 @@
 RATE_MATRIX = 0.03
 RATE_VECTOR = 0.3
 CLIP_NORM = 1.0
+
+MESH = pl.DeviceIdType.MESH
+F32 = jnp.float32
+BF16 = jnp.bfloat16
+
+LP, RP = 24, 40
+WO, RO = 8 * LP, 8 * RP
+WALL, ALL = 2 * WO, 2 * WO + 2 * RO
+OWN = WO + RO
+D = 768
+NU = 7
+SEGS = ((0, 0, WO), (WO, WALL, RO))
+CH = 64
+VMEM_BYTES = 62 * 1024 * 1024
+
+
+def nn(a, b):
+    return jnp.dot(a, b, preferred_element_type=F32)
+
+
+def nt(a, b):
+    return lax.dot_general(a, b, (((1,), (1,)), ((), ())), preferred_element_type=F32)
+
+
+def tn(a, b):
+    return lax.dot_general(a, b, (((0,), (0,)), ((), ())), preferred_element_type=F32)
+
+
+def low_lanes(rows):
+    return lax.broadcasted_iota(jnp.int32, (rows, 128), 1) < HD
+
+
+def swap(v):
+    return pltpu.roll(v, HD, 1)
+
+
+def kernel(
+    lang_in, vis_in, lang_cot, vis_cot, lengths, attn_w, ffn_w, vec,
+    out3, gx, g32, vgo, sqo, ra1, ra2, ra3, rb1, rb2, rb3, rz,
+    W, H, DYA, DYB, Z, XS, YO, YS, YR, Q, K, V, F, PW, PR, A, GP, E, DO, G3, ST, ST3, VG, VR, VZ, SQ, SP, SZ, BIAS,
+    lsem, osem, gsem, cs, cr, ags, agr, rss, rsr, vs, vr, ps, pr,
+):
+    d = lax.axis_index("dp")
+    t = lax.axis_index("tensor")
+    z, x = d // 2, d % 2
+    y, c = t // 2, t % 2
+    oy, ox = 1 - y, 1 - x
+
+    def at(zz, xx, yy, cc):
+        return (zz * 2 + xx, yy * 2 + cc)
+
+    core_n, y_n, x_n = at(z, x, y, 1 - c), at(z, x, oy, c), at(z, ox, y, c)
+    zk = [(z + k) % 4 for k in range(4)]
+    z_n = [at(zk[k], x, y, c) for k in range(4)]
+    flips = [(i, j, k) for i in (0, 1) for j in (0, 1) for k in (0, 1)][1:]
+    plane = [at(z, (x + i) % 2, (y + j) % 2, (c + k) % 2) for i, j, k in flips]
+
+    barrier = pltpu.get_barrier_semaphore()
+    partners = plane + z_n[1:]
+    for p in partners:
+        pl.semaphore_signal(barrier, inc=1, device_id=p, device_id_type=MESH)
+    pl.semaphore_wait(barrier, len(partners))
+
+    def remote(src, dst, ss, rs, dev):
+        return pltpu.make_async_remote_copy(
+            src_ref=src, dst_ref=dst, send_sem=ss, recv_sem=rs, device_id=dev, device_id_type=MESH
+        )
+
+    def local(src, dst, sem):
+        return pltpu.make_async_copy(src, dst, sem)
+
+    rows_of = (pl.ds(0, 48), pl.ds(48, 48))
+
+    def shard(u, part, dy, dx, dz):
+        return W.at[u, y if dy == 0 else oy, zk[dz], x if dx == 0 else ox, rows_of[part], :]
+
+    def sid(dy, dx, dz):
+        return dy * 8 + dx * 4 + dz
+
+    ag_sends = {}
+
+    def ag_send(u, part, dy, dx, dz, way):
+        src = shard(u, part, dy, dx, dz)
+        if way == "x":
+            there, dev = sid(dy, 1 - dx, dz), x_n
+        elif way == "y":
+            there, dev = sid(1 - dy, dx, dz), y_n
+        else:
+            there, dev = sid(dy, dx, (dz - way) % 4), z_n[way]
+        n = ag_sends.setdefault((u, part), [])
+        cp = remote(src, src, ags.at[u, part, len(n)], agr.at[u, part, there], dev)
+        cp.start()
+        n.append(cp)
+
+    def ag_recv(u, part, dy, dx, dz):
+        src = shard(u, part, dy, dx, dz)
+        remote(src, src, ags.at[u, part, 15], agr.at[u, part, sid(dy, dx, dz)], x_n).wait_recv()
+
+    def ag_first(u):
+        for part in (0, 1):
+            for k in (1, 3, 2):
+                ag_send(u, part, 0, 0, 0, k)
+            ag_send(u, part, 0, 0, 0, "x")
+            ag_send(u, part, 0, 0, 0, "y")
+
+    def ag_pass(u, part, k):
+        ag_recv(u, part, 0, 0, k)
+        ag_send(u, part, 0, 0, k, "x")
+        ag_send(u, part, 0, 0, k, "y")
+
+    def ag_turn(u, part, k):
+        if part == 0:
+            ag_recv(u, 0, 0, 1, k)
+            ag_send(u, 0, 0, 1, k, "y")
+        else:
+            ag_recv(u, 1, 1, 0, k)
+            ag_send(u, 1, 1, 0, k, "x")
+
+    def ag_first_m(u):
+        ag_send(u, 0, 0, 0, 0, "x")
+        ag_send(u, 1, 0, 0, 0, "y")
+        for part in (0, 1):
+            for k in (1, 3, 2):
+                ag_send(u, part, 0, 0, 0, k)
+        ag_send(u, 0, 0, 0, 0, "y")
+        ag_send(u, 1, 0, 0, 0, "x")
+
+    def ag_spread(u, part):
+        dy, dx = ((0, 1), (1, 0))[part]
+        ag_recv(u, part, dy, dx, 0)
+        for k in (1, 3, 2, "yx"[part]):
+            ag_send(u, part, dy, dx, 0, k)
+
+    def ag_cross(u, part, q, k):
+        dy, dx = ((0, q), (q, 0))[part]
+        ag_recv(u, part, dy, dx, k)
+        ag_send(u, part, dy, dx, k, "yx"[part])
+
+    def ag_last(u):
+        for k in (0, 1, 3, 2):
+            for dx in (0, 1):
+                ag_recv(u, 0, 1, dx, k)
+            for dy in (0, 1):
+                ag_recv(u, 1, dy, 1, k)
+        for part in (0, 1):
+            for cp in ag_sends[(u, part)]:
+                cp.wait_send()
+
+    core_count = [0]
+
+    def core_copy(src, dst):
+        i = core_count[0]
+        core_count[0] += 1
+        cp = remote(src, dst, cs.at[i], cr.at[i], core_n)
+        cp.start()
+        return cp
+
+    def share_rows(ref, s):
+        o, r, n = SEGS[s]
+        return core_copy(ref.at[pl.ds(r, n)], ref.at[pl.ds(r + n, n)])
+
+    def wait_all(cps):
+        for cp in cps:
+            cp.wait()
+
+    def branch_sum(s, terms):
+        o, r, n = SEGS[s]
+        YS[o : o + n, :] = terms(r + n, n).astype(BF16)
+        cp = core_copy(YS.at[pl.ds(o, n)], YR.at[pl.ds(o, n)])
+        YO[o : o + n, :] = terms(r, n)
+        return cp
+
+    own_f = [local(ffn_w.at[i // 2, i % 2], Z.at[0, pl.ds(96 * i, 96)], lsem.at[i]) for i in range(4)]
+    for cp in own_f:
+        cp.start()
+
+    def pack(u):
+        q, k, v, o = (attn_w[u, j] for j in range(4))
+        w = W.at[u, y, z, x]
+        for base, a, b in ((0, q, k), (384, v, o)):
+            w[:, base : base + 128] = a[:, 0:128].astype(BF16)
+            w[:, base + 128 : base + 256] = jnp.concatenate([a[:, 128:192], b[:, 128:192]], axis=1).astype(BF16)
+            w[:, base + 256 : base + 384] = b[:, 0:128].astype(BF16)
+
+    for u in range(3):
+        pack(u)
+    for i, cp in enumerate(own_f):
+        cp.wait()
+        W[3 + i, y, z, x] = Z[0, 96 * i : 96 * i + 96, :].astype(BF16)
+
+    def items_of(s):
+        return (lang_in, lang_cot, 20, LP) if s == 0 else (vis_in, vis_cot, 36, RP)
+
+    def load_rows(s, src, count, pad, masked):
+        o, r, n = SEGS[s]
+        XS[o : o + n, :] = jnp.zeros((n, D), F32)
+        for p in range(0, count, 4):
+            v = jnp.swapaxes(src[p : p + 4].astype(F32), 0, 1)
+            for i in range(8):
+                w = v[i]
+                if masked:
+                    w = jnp.where(place + p < lengths[t * 8 + i], w, 0.0)
+                XS[o + i * pad + p : o + i * pad + p + 4, :] = w
+
+    place = lax.broadcasted_iota(jnp.int32, (4, D), 0)
+
+    def load_cot(s):
+        _, src, count, pad = items_of(s)
+        load_rows(s, src, count, pad, s == 0)
+
+    lane4 = lax.broadcasted_iota(jnp.int32, (1, 384), 1)
+    held = {}
+
+    def got(name):
+        if name in held:
+            held.pop(name).wait()
+
+    def load_input():
+        for s, (o, r, n) in enumerate(SEGS):
+            src, _, count, pad = items_of(s)
+            load_rows(s, src, count, pad, False)
+            for j in range(n // 64):
+                H[0, r + j * 64 : r + j * 64 + 64, :] = XS[o + j * 64 : o + j * 64 + 64, :].astype(BF16)
+            held["h0", s] = share_rows(H.at[0], s)
+        VG[...] = jnp.zeros_like(VG)
+        SQ[...] = jnp.zeros_like(SQ)
+        for b in range(3):
+            for j in range(2):
+                for k, base in ((b, 0), (3 + b, 384)):
+                    v = vec[k : k + 1, j * 384 : j * 384 + 384]
+                    v = jnp.where(c == 0, v, pltpu.roll(v, 192, 1))
+                    BIAS[2 * b + j : 2 * b + j + 1, base : base + 384] = jnp.where(lane4 < 192, v, 0.0)
+
+    def item_rows(n, half):
+        r = lax.broadcasted_iota(jnp.int32, (2 * n, 128), 0)
+        return ((r >= half) & (r < n)) | (r >= n + half)
+
+    lane_w = lax.broadcasted_iota(jnp.int32, (1, 128), 1)
+    item_w = lane_w >= LP
+    item_r = lane_w >= RP
+    good_r = (lane_w < 36) | ((lane_w >= RP) & (lane_w < RP + 36))
+    one = lambda m: jnp.where(m, 1.0, 0.0)
+    ir_w, ir_r = one(item_rows(2 * LP, LP)), one(item_rows(2 * RP, RP))
+    mask_wr = ((ir_w == one(item_r)) & good_r)[:, : 2 * RP]
+    mask_rr = ((ir_r == one(item_r)) & good_r)[:, : 2 * RP]
+    mask_ww = (ir_w == one(item_w))[:, : 2 * LP]
+    mask_rw = (ir_r == one(item_w))[:, : 2 * LP]
+
+    lane_k = lane_w[:, : 2 * LP]
+
+    def word_keys(i):
+        first = y * 16 + jnp.where(i < 4, c, 1 - c) * 8 + 2 * (i % 4)
+        a, b = lengths[first], lengths[first + 1]
+        return (lane_k < a) | ((lane_k >= LP) & (lane_k < b + LP))
+
+    def weights_of(u, yy, a, b):
+        return W[u, yy, :, :, :, a:b].reshape(D, b - a)
+
+    def project(sec, u, r, n):
+        h = H[sec, r : r + n, :]
+        r0 = nn(h, weights_of(u, 0, 0, 640)) + BIAS[2 * u : 2 * u + 1, 0:640]
+        r1 = nn(h, weights_of(u, 1, 0, 640)) + BIAS[2 * u + 1 : 2 * u + 2, 0:640]
+        lo = low_lanes(n)
+        rr = pl.ds(r, n)
+        Q[sec, rr, 0:128] = r0[:, 0:128].astype(BF16)
+        Q[sec, rr, 128:256] = r1[:, 0:128].astype(BF16)
+        m0, m1 = r0[:, 128:256], r1[:, 128:256]
+        Q[sec, rr, 256:384] = jnp.where(lo, m0, swap(m1)).astype(BF16)
+        K[sec, rr, 256:384] = jnp.where(lo, swap(m0), m1).astype(BF16)
+        K[sec, rr, 0:128] = r0[:, 256:384].astype(BF16)
+        K[sec, rr, 128:256] = r1[:, 256:384].astype(BF16)
+        V[sec, rr, 0:128] = r0[:, 384:512].astype(BF16)
+        V[sec, rr, 128:256] = r1[:, 384:512].astype(BF16)
+        V[sec, rr, 256:384] = jnp.where(lo, r0[:, 512:640], swap(r1[:, 512:640])).astype(BF16)
+
+    def stacked(ref, sec, rows, n, w):
+        v = ref[sec, rows, w * 128 : w * 128 + 128]
+        lo = low_lanes(n)
+        zero = jnp.zeros_like(v)
+        return jnp.concatenate([jnp.where(lo, v, zero), jnp.where(lo, zero, v)], axis=0)
+
+    def attend(sec, i, qr, nq, kr, nk, mask, pref):
+        lo = low_lanes(nq)
+        for w in range(3):
+            cols = slice(w * 128, w * 128 + 128)
+            s = nt(stacked(Q, sec, qr, nq, w), K[sec, kr, cols]) * (HD**-0.5)
+            s = jnp.where(mask, s, MASKED)
+            e = jnp.exp(s - jnp.max(s, axis=1, keepdims=True))
+            p = (e / jnp.sum(e, axis=1, keepdims=True)).astype(BF16)
+            pref[sec, pl.ds(pl.multiple_of((i * 3 + w) * 2 * nq, 32), 2 * nq), 0:nk] = p
+            o = nn(p, V[sec, kr, cols])
+            o = jnp.where(lo, o[:nq], o[nq:])
+            if w < 2:
+                F[sec, w, qr, 128:256] = o.astype(BF16)
+            else:
+                zero = jnp.zeros_like(o)
+                F[sec, 0, qr, 0:128] = jnp.where(lo, zero, swap(o)).astype(BF16)
+                F[sec, 1, qr, 0:128] = jnp.where(lo, zero, o).astype(BF16)
+
+    def pair_rows(i):
+        return (
+            pl.ds(pl.multiple_of(i * 2 * LP, 16), 2 * LP),
+            pl.ds(pl.multiple_of(WALL + i * 2 * RP, 16), 2 * RP),
+        )
+
+    def attention(sec, s, first=0, last=8):
+        def pair(i, carry):
+            wr, rr = pair_rows(i)
+            if sec == 0:
+                attend(0, i, wr, 2 * LP, rr, 2 * RP, mask_wr, PW)
+                attend(0, i, rr, 2 * RP, wr, 2 * LP, mask_rw & word_keys(i), PR)
+            elif s == 0:
+                attend(1, i, wr, 2 * LP, wr, 2 * LP, mask_ww & word_keys(i), PW)
+            else:
+                attend(1, i, rr, 2 * RP, rr, 2 * RP, mask_rr, PR)
+            return carry
+
+        lax.fori_loop(first, last, pair, 0)
+
+    def out_project(sec, s, u):
+        def terms(r, n):
+            return nt(F[sec, 0, r : r + n, :], weights_of(u, 0, 512, 768)) + nt(
+                F[sec, 1, r : r + n, :], weights_of(u, 1, 512, 768)
+            )
+
+        return branch_sum(s, terms)
+
+    def over_own(fn, s):
+        o, r, n = SEGS[s]
+
+        def step(j, carry):
+            fn(pl.ds(pl.multiple_of(o + j * CH, CH), CH), pl.ds(pl.multiple_of(r + j * CH, CH), CH))
+            return carry
+
+        lax.fori_loop(0, n // CH, step, 0)
+
+    def stats(v):
+        mean = jnp.mean(v, axis=1, keepdims=True)
+        cen = v - mean
+        rstd = lax.rsqrt(jnp.mean(cen * cen, axis=1, keepdims=True) + NORM_EPSILON)
+        return cen * rstd, rstd
+
+    def row(k):
+        return vec[k : k + 1, :]
+
+    def norm_forward(s, zi, bias, gain, shift, nxt):
+        def fn(oo, rr):
+            v = YO[oo, :] + YR[oo, :].astype(F32) + row(bias) + XS[oo, :]
+            Z[zi, oo, :] = v
+            xh, _ = stats(v)
+            out = xh * row(gain) + row(shift)
+            if nxt is None:
+                YO[oo, :] = out
+            else:
+                XS[oo, :] = out
+                H[nxt, rr, :] = out.astype(BF16)
+
+        over_own(fn, s)
+
+    def norm_backward(s, zi, first, gain, row_g, row_s, row_b, DY):
+        def fn(oo, rr):
+            dout = XS[oo, :]
+            if not first:
+                dout = dout + YO[oo, :] + YR[oo, :].astype(F32)
+            xh, rstd = stats(Z[zi, oo, :])
+            dx = dout * row(gain)
+            dz = rstd * (
+                dx - jnp.mean(dx, axis=1, keepdims=True) - xh * jnp.mean(dx * xh, axis=1, keepdims=True)
+            )
+            VG[row_g : row_g + 1, :] += jnp.sum(dout * xh, axis=0, keepdims=True)
+            VG[row_s : row_s + 1, :] += jnp.sum(dout, axis=0, keepdims=True)
+            VG[row_b : row_b + 1, :] += jnp.sum(dz, axis=0, keepdims=True)
+            XS[oo, :] = dz
+            DY[rr, :] = dz.astype(BF16)
+
+        over_own(fn, s)
+
+    def gate_rows(n, y2, r, o):
+        def step(j, carry):
+            u = YO[pl.ds(pl.multiple_of(o + j * 16, 16), 16), :]
+            rr = pl.ds(pl.multiple_of(r + j * 16, 16), 16)
+            half = 0.5 * (1.0 + lax.erf(u * (0.5**0.5)))
+            A[y2, rr, :] = (u * half).astype(BF16)
+            GP[y2, rr, :] = (half + u * (jnp.exp(-0.5 * u * u) * 0.3989422804014327)).astype(BF16)
+            return carry
+
+        lax.fori_loop(0, n // 16, step, 0)
+
+    STREAM = ((0, WO), (WALL, RO))
+
+    def feed_up(s, j):
+        o, r0, n = SEGS[s]
+        r, y2 = r0 + (j // 2) * n, j % 2
+        hidden = vec[pl.ds(21 + 4 * s + 2 * y2 + c, 1), :]
+        YO[o : o + n, :] = nn(H[2, r : r + n, :], weights_of(3 + 2 * s, y2, 0, D)) + hidden
+        gate_rows(n, y2, r, o)
+
+    def feed_down(r, n):
+        u = 4 if r < WALL else 6
+        return nt(A[0, r : r + n, :], weights_of(u, 0, 0, D)) + nt(A[1, r : r + n, :], weights_of(u, 1, 0, D))
+
+    def put_grad(u, yy, m, value):
+        W[u, yy, 2 * m : 2 * m + 2, :, :, :] = value.astype(BF16).reshape(2, 2, 96, D)
+
+    def feed_back(s, y2, DY):
+        r0, n = STREAM[s]
+        r1 = r0 + 2 * n
+        u2 = 4 + 2 * s
+        total = jnp.zeros((1, D), F32)
+        for half in range(2):
+            du = nt_rows_gate(DY, u2, y2, r0 + half * n, n)
+            total = total + jnp.sum(du.astype(F32), axis=0, keepdims=True)
+        k = 21 + 2 * s + y2
+        VG[k : k + 1, :] = total
+        for m in range(2):
+            put_grad(u2, y2, m, tn(DY[r0:r1, m * 384 : m * 384 + 384], A[y2, r0:r1, :]))
+
+    def nt_rows_gate(DY, u2, y2, r, n):
+        da = nn(DY[r : r + n, :], weights_of(u2, y2, 0, D))
+        du = (da * GP[y2, r : r + n, :].astype(F32)).astype(BF16)
+        GP[y2, r : r + n, :] = du
+        return du
+
+    def feed_hidden_back(r, n):
+        u = 3 if r < WALL else 5
+        return nt(GP[0, r : r + n, :], weights_of(u, 0, 0, D)) + nt(GP[1, r : r + n, :], weights_of(u, 1, 0, D))
+
+    def feed_up_grad(s):
+        r0, n = STREAM[s]
+        r1 = r0 + 2 * n
+        for y2 in range(2):
+            for m in range(2):
+                put_grad(3 + 2 * s, y2, m, tn(H[2, r0:r1, m * 384 : m * 384 + 384], GP[y2, r0:r1, :]))
+
+    def grad_mixture(u, r, n, DY):
+        dy = DY[r : r + n, :]
+        r0 = nn(dy, weights_of(u, 0, 512, 768))
+        r1 = nn(dy, weights_of(u, 1, 512, 768))
+        rr = pl.ds(r, n)
+        DO[0, rr, 0:128] = r0[:, 128:256].astype(BF16)
+        DO[0, rr, 128:256] = r1[:, 128:256].astype(BF16)
+        DO[0, rr, 256:384] = jnp.where(low_lanes(n), swap(r0[:, 0:128]), r1[:, 0:128]).astype(BF16)
+
+    def attend_back(sec, i, qr, nq, kr, nk, pref):
+        lo = low_lanes(nq)
+        dqs, dks, dvs = [], [], []
+        for w in range(3):
+            cols = slice(w * 128, w * 128 + 128)
+            p = pref[sec, pl.ds(pl.multiple_of((i * 3 + w) * 2 * nq, 32), 2 * nq), 0:nk]
+            dos = stacked(DO, 0, qr, nq, w)
+            dp = nt(dos, V[sec, kr, cols])
+            pf = p.astype(F32)
+            ds = (pf * (dp - jnp.sum(pf * dp, axis=1, keepdims=True))).astype(BF16)
+            dq = nn(ds, K[sec, kr, cols]) * (HD**-0.5)
+            dqs.append(jnp.where(lo, dq[:nq], dq[nq:]))
+            dks.append(tn(ds, stacked(Q, sec, qr, nq, w)) * (HD**-0.5))
+            dvs.append(tn(p, dos))
+        return dqs, dks, dvs
+
+    def put_pack(rows, n, dqs, dks, dvs):
+        lo = low_lanes(n)
+        zero = jnp.zeros((n, 128), F32)
+        for w in range(2):
+            E[w, rows, 0:128] = dqs[w].astype(BF16)
+            E[w, rows, 256:384] = dks[w].astype(BF16)
+            E[w, rows, 384:512] = dvs[w].astype(BF16)
+        E[0, rows, 128:256] = jnp.where(lo, dqs[2], swap(dks[2])).astype(BF16)
+        E[1, rows, 128:256] = jnp.where(lo, swap(dqs[2]), dks[2]).astype(BF16)
+        E[0, rows, 512:640] = jnp.where(lo, dvs[2], zero).astype(BF16)
+        E[1, rows, 512:640] = jnp.where(lo, swap(dvs[2]), zero).astype(BF16)
+
+    def attention_back(sec, s, first=0, last=8):
+        def pair(i, carry):
+            wr, rr = pair_rows(i)
+            if sec == 0:
+                qw, kr_, vr_ = attend_back(0, i, wr, 2 * LP, rr, 2 * RP, PW)
+                qr_, kw, vw = attend_back(0, i, rr, 2 * RP, wr, 2 * LP, PR)
+                put_pack(wr, 2 * LP, qw, kw, vw)
+                put_pack(rr, 2 * RP, qr_, kr_, vr_)
+            elif s == 0:
+                put_pack(wr, 2 * LP, *attend_back(1, i, wr, 2 * LP, wr, 2 * LP, PW))
+            else:
+                put_pack(rr, 2 * RP, *attend_back(1, i, rr, 2 * RP, rr, 2 * RP, PR))
+            return carry
+
+        lax.fori_loop(first, last, pair, 0)
+
+    def branch_back(s, u):
+        def terms(r, n):
+            return nt(E[0, r : r + n, :], weights_of(u, 0, 0, 640)) + nt(E[1, r : r + n, :], weights_of(u, 1, 0, 640))
+
+        return branch_sum(s, terms)
+
+    def attn_grad(sec, u, r0, r1, DY, sides=(0, 1)):
+        for yy in sides:
+            k = 15 + 2 * u + yy
+            VG[k : k + 1, 0:640] = jnp.sum(E[yy, r0:r1, :].astype(F32), axis=0, keepdims=True)
+            for m in range(2):
+                mc = slice(m * 384, m * 384 + 384)
+                a = tn(H[sec, r0:r1, mc], E[yy, r0:r1, :])
+                b = tn(DY[r0:r1, mc], F[sec, yy, r0:r1, :])
+                put_grad(u, yy, m, jnp.concatenate([a[:, 0:512], a[:, 512:640] + b[:, 0:128], b[:, 128:256]], axis=1))
+
+    top, bot = rows_of
+    rs_sends = []
+
+    def rs_send(u, k, src, dst, dev):
+        cp = remote(src, dst, rss.at[u, k], rsr.at[u, k], dev)
+        cp.start()
+        rs_sends.append(cp)
+
+    def rs_recv(u, k, dst):
+        remote(dst, dst, rss.at[u, k], rsr.at[u, k], x_n).wait_recv()
+
+    def rs1(u):
+        for k, (xx, yy) in enumerate(((ox, oy), (x, y))):
+            rs_send(u, k, W.at[u, oy, :, xx, top, :], ra1.at[u, :, xx], y_n)
+            rs_send(u, 2 + k, W.at[u, yy, :, ox, bot, :], rb1.at[u, yy], x_n)
+
+    def add_in(dst, stage):
+        def step(j, carry):
+            dst(j)[...] = (dst(j)[...].astype(F32) + stage[j].astype(F32)).astype(BF16)
+            return carry
+
+        lax.fori_loop(0, 4, step, 0)
+
+    def rs2_m(u, part):
+        cps = []
+        for q in (0, 1):
+            rs_recv(u, 2 * part + q, (ra1.at[u, :, (ox, x)[q]], rb1.at[u, (oy, y)[q]])[part])
+        for q in (0, 1):
+            cps.append(local((ra1.at[u, :, q], rb1.at[u, q])[part], ST.at[q], lsem.at[q]))
+            cps[-1].start()
+        for q in (0, 1):
+            cps[q].wait()
+            if part == 0:
+                add_in(lambda j: W.at[u, y, j, q, top, :], ST.at[q])
+            else:
+                add_in(lambda j: W.at[u, q, j, x, bot, :], ST.at[q])
+        for k in (1, 3, 2):
+            src = (W.at[u, y, zk[k], :, top, :], W.at[u, :, zk[k], x, bot, :])[part]
+            rs_send(u, 5 + 3 * part + k, src, rz.at[u, part, k - 1], z_n[k])
+
+    def rs3_m(u, part):
+        for k in (1, 3, 2):
+            rs_recv(u, 5 + 3 * part + k, rz.at[u, part, k - 1])
+        cps = [local(rz.at[u, part, :, q], ST3.at[q], lsem.at[2 + q]) for q in (0, 1)]
+        for cp in cps:
+            cp.start()
+        for cp in cps:
+            cp.wait()
+        rows = rows_of[part]
+
+        def total(yy, xx, q):
+            g = W[u, yy, z, xx, rows, :].astype(F32)
+            for k in range(3):
+                g = g + ST3[q, k].astype(F32)
+            return g
+
+        if part == 0:
+            W[u, y, z, ox, rows, :] = total(y, ox, ox).astype(BF16)
+            rs_send(u, 4, W.at[u, y, z, ox, rows, :], ra3.at[u, 0], x_n)
+        else:
+            W[u, oy, z, x, rows, :] = total(oy, x, oy).astype(BF16)
+            rs_send(u, 5, W.at[u, oy, z, x, rows, :], rb3.at[u, 0], y_n)
+        G3[u, rows, :] = total(y, x, (x, y)[part])
+
+    def rs4_m(u):
+        cps = []
+        for part, dst in ((0, ra3), (1, rb3)):
+            rs_recv(u, 4 + part, dst.at[u, 0])
+            cps.append(local(dst.at[u, 0], ST3.at[part, 0], lsem.at[part]))
+            cps[-1].start()
+        for cp in cps:
+            cp.wait()
+        return rs_end(u, 1)
+
+    def rs2(u, part):
+        src, k = ((ra1.at[u, :, ox], 0), (rb1.at[u, oy], 2))[part]
+        rs_recv(u, k, src)
+        cp = local(src, ST.at[part], lsem.at[part])
+        cp.start()
+        cp.wait()
+        if part == 0:
+            add_in(lambda j: W.at[u, y, j, ox, top, :], ST.at[0])
+            rs_send(u, 4, W.at[u, y, :, ox, top, :], ra2.at[u], x_n)
+        else:
+            add_in(lambda j: W.at[u, oy, j, x, bot, :], ST.at[1])
+            rs_send(u, 5, W.at[u, oy, :, x, bot, :], rb2.at[u], y_n)
+
+    def rs3(u, part):
+        cps = []
+        for i, (k, src) in enumerate((((1, ra1.at[u, :, x]), (4, ra2.at[u])), ((3, rb1.at[u, y]), (5, rb2.at[u])))[part]):
+            rs_recv(u, k, src)
+            cps.append(local(src, ST.at[2 + i], lsem.at[2 + i]))
+            cps[-1].start()
+        for cp in cps:
+            cp.wait()
+        rows = rows_of[part]
+
+        def step(j, carry):
+            w = W.at[u, y, j, x, rows, :]
+            w[...] = (w[...].astype(F32) + ST[2, j].astype(F32) + ST[3, j].astype(F32)).astype(BF16)
+            return carry
+
+        own = W[u, y, z, x, rows, :].astype(F32) + ST[2, z].astype(F32) + ST[3, z].astype(F32)
+        lax.fori_loop(0, 4, step, 0)
+        G3[u, rows, :] = own
+        for k in (1, 3, 2):
+            rs_send(u, 5 + 3 * part + k, W.at[u, y, zk[k], x, rows, :], (ra3, rb3)[part].at[u, k - 1], z_n[k])
+
+    def rs4(u):
+        cps = []
+        for part, dst in ((0, ra3), (1, rb3)):
+            for k in (1, 3, 2):
+                rs_recv(u, 5 + 3 * part + k, dst.at[u, k - 1])
+            cps.append(local(dst.at[u], ST3.at[part], lsem.at[part]))
+            cps[-1].start()
+        for cp in cps:
+            cp.wait()
+        return rs_end(u, 3)
+
+    def rs_end(u, terms):
+        for part in (0, 1):
+            g = G3[u, rows_of[part], :]
+            for k in range(terms):
+                g = g + ST3[part, k].astype(F32)
+            G3[u, rows_of[part], :] = g
+            SQ[...] += jnp.sum((g * g).reshape(6, 8, D), axis=0)
+        cp = local(G3.at[u], g32.at[u], gsem.at[u])
+        cp.start()
+        return cp
+
+    def vsend(k, src, dst, dev):
+        cp = remote(src, dst, vs.at[k], vr.at[k], dev)
+        cp.start()
+        return cp
+
+    pending = []
+
+    def vec1():
+        VR[2] = VG[...]
+        pending.append(vsend(0, VR.at[2], VR.at[0], y_n))
+
+    def vec2():
+        pending.pop().wait()
+        VR[3] = VR[2] + VR[0]
+        pending.append(vsend(1, VR.at[3], VR.at[1], x_n))
+
+    def vec3():
+        pending.pop().wait()
+        VZ[z] = VR[3] + VR[1]
+        for j in (1, 2, 3):
+            pending.append(vsend(1 + j, VZ.at[z], VZ.at[z], z_n[j]))
+
+    def vec4():
+        while pending:
+            pending.pop().wait()
+        vgo[c] = VZ[0] + VZ[1] + VZ[2] + VZ[3]
+        pending.append(vsend(5, vgo.at[c], vgo.at[c], core_n))
+
+    def squares():
+        me = y * 4 + x * 2 + c
+        SP[me] = jnp.full((8, 128), jnp.sum(SQ[...]), F32)
+        cps = []
+        for i, dev in enumerate(plane):
+            cp = remote(SP.at[me], SP.at[me], ps.at[i], pr.at[i], dev)
+            cp.start()
+            cps.append(cp)
+        for cp in cps:
+            cp.wait()
+        total = SP[0]
+        for i in range(1, 8):
+            total = total + SP[i]
+        SZ[z] = total
+        cps = []
+        for j in (1, 2, 3):
+            cp = remote(SZ.at[z], SZ.at[z], ps.at[6 + j], pr.at[6 + j], z_n[j])
+            cp.start()
+            cps.append(cp)
+        for cp in cps:
+            cp.wait()
+        sqo[...] = SZ[0] + SZ[1] + SZ[2] + SZ[3]
+
+    chunks = ((0, WALL), (WALL, RO), (WALL + RO, RO))
+
+    def do_pj0(j):
+        got(("h0", 0))
+        got(("h0", 1))
+        project(0, 0, *chunks[j])
+
+    def do_at0(j):
+        attention(0, 0, 4 * j, 4 * j + 4)
+
+    def do_op0(s):
+        held["y1", s] = out_project(0, s, 0)
+
+    def do_nf0(s):
+        got(("y1", s))
+        norm_forward(s, 0, 6, 9, 14, 1)
+        held["h1", s] = share_rows(H.at[1], s)
+
+    def do_pj1(s, j):
+        got(("h1", s))
+        _, r, n = SEGS[s]
+        project(1, 1 + s, r + j * n, n)
+
+    def do_at1(s):
+        attention(1, s)
+
+    def do_op1(s):
+        held["y2", s] = out_project(1, s, 1 + s)
+
+    def do_nf1(s):
+        got(("y2", s))
+        norm_forward(s, 1, 7 + s, 10 + s, 15 + s, 2)
+        held["h2", s] = share_rows(H.at[2], s)
+
+    def do_fu(s, j):
+        got(("h2", s))
+        feed_up(s, j)
+
+    def do_fd(s):
+        held["f", s] = branch_sum(s, feed_down)
+
+    def do_n3(s):
+        got(("f", s))
+        norm_forward(s, 2, 19 + s, 12 + s, 17 + s, None)
+        o, r, n = SEGS[s]
+        held["out", s] = local(YO.at[pl.ds(o, n)], out3.at[pl.ds(o, n)], osem.at[s])
+        held["out", s].start()
+        load_cot(s)
+        norm_backward(s, 2, True, 12 + s, 3 + s, 8 + s, 13 + s, DYA)
+        held["dy3", s] = share_rows(DYA, s)
+
+    def do_fb(s, j):
+        got(("dy3", s))
+        feed_back(s, j, DYA)
+        if j == 1:
+            rs1(4 + 2 * s)
+
+    def do_fh(s):
+        got(("out", s))
+        held["dh2", s] = branch_sum(s, feed_hidden_back)
+
+    def do_fg(s):
+        feed_up_grad(s)
+        rs1(3 + 2 * s)
+
+    def do_sb(s):
+        got(("dh2", s))
+        norm_backward(s, 1, False, 10 + s, 1 + s, 6 + s, 11 + s, DYB)
+        held["dy2", s] = share_rows(DYB, s)
+
+    def do_gm(s, j):
+        got(("dy2", s))
+        _, r, n = SEGS[s]
+        grad_mixture(1 + s, r + j * n, n, DYB)
+
+    def do_ab(s, j):
+        if s == 1:
+            attention_back(1, s, 4 * j, 4 * j + 4)
+        else:
+            attention_back(1, s)
+
+    def do_be(s):
+        held["dh1", s] = branch_back(s, 1 + s)
+
+    def do_ag(s):
+        _, r, n = SEGS[s]
+        attn_grad(1, 1 + s, r, r + 2 * n, DYB)
+        rs1(1 + s)
+
+    def do_cb(s):
+        got(("dh1", s))
+        norm_backward(s, 0, False, 9, 0, 5, 10, DYA)
+        held["dy1", s] = share_rows(DYA, s)
+
+    def do_gm0(j):
+        got(("dy1", 0))
+        got(("dy1", 1))
+        grad_mixture(0, *chunks[j], DYA)
+
+    def do_ab0(j):
+        attention_back(0, 0, 4 * j, 4 * j + 4)
+
+    def do_be0(s):
+        held["dh0", s] = branch_back(s, 0)
+
+    def do_ag0(j):
+        attn_grad(0, 0, 0, ALL, DYA, (j,))
+        if j == 1:
+            rs1(0)
+
+    def do_fin(s):
+        got(("dh0", s))
+
+        def finish(oo, rr):
+            XS[oo, :] += YO[oo, :] + YR[oo, :].astype(F32)
+
+        over_own(finish, s)
+        o, r, n = SEGS[s]
+        held["gx", s] = local(XS.at[pl.ds(o, n)], gx.at[pl.ds(o, n)], osem.at[s])
+        held["gx", s].start()
+
+    ag_first(0)
+    load_input()
+    ag_first(2)
+    ag_turn(0, 1, 0)
+    ag_pass(0, 1, 1)
+    ag_first_m(5)
+    ag_turn(0, 0, 0)
+    ag_pass(0, 0, 1)
+    ag_pass(0, 0, 3)
+    ag_turn(0, 1, 1)
+    ag_pass(0, 1, 2)
+    ag_first(6)
+    ag_pass(0, 1, 3)
+    ag_turn(0, 0, 3)
+    ag_turn(0, 0, 1)
+    ag_pass(2, 1, 1)
+    ag_pass(2, 0, 3)
+    ag_pass(0, 0, 2)
+    ag_pass(2, 0, 2)
+    ag_turn(0, 1, 3)
+    ag_turn(2, 0, 3)
+    ag_turn(0, 1, 2)
+    ag_turn(0, 0, 2)
+    ag_pass(2, 1, 3)
+    ag_cross(5, 1, 0, 1)
+    ag_pass(2, 0, 1)
+    ag_last(0)
+    ag_pass(2, 1, 2)
+    ag_cross(5, 0, 0, 2)
+    ag_cross(5, 0, 0, 3)
+    ag_cross(5, 1, 0, 2)
+    ag_turn(6, 1, 0)
+    ag_turn(2, 0, 2)
+    do_pj0(2)
+    do_pj0(0)
+    ag_spread(5, 1)
+    ag_turn(2, 1, 0)
+    ag_cross(5, 0, 0, 1)
+    do_pj0(1)
+    do_at0(0)
+    ag_pass(6, 0, 1)
+    ag_pass(6, 1, 1)
+    ag_pass(6, 0, 3)
+    ag_pass(6, 0, 2)
+    ag_cross(5, 1, 0, 3)
+    ag_turn(2, 1, 1)
+    ag_pass(6, 1, 3)
+    ag_turn(2, 0, 1)
+    ag_first(1)
+    ag_turn(6, 0, 3)
+    ag_spread(5, 0)
+    ag_turn(6, 0, 2)
+    ag_turn(2, 0, 0)
+    ag_pass(6, 1, 2)
+    ag_cross(5, 1, 1, 1)
+    ag_turn(1, 1, 0)
+    ag_first_m(3)
+    ag_turn(2, 1, 3)
+    do_at0(1)
+    do_op0(1)
+    ag_spread(3, 1)
+    do_nf0(1)
+    ag_turn(6, 0, 1)
+    ag_turn(2, 1, 2)
+    ag_pass(1, 1, 2)
+    ag_pass(1, 0, 1)
+    ag_cross(5, 0, 1, 3)
+    ag_pass(1, 0, 2)
+    ag_pass(1, 0, 3)
+    ag_cross(5, 1, 1, 3)
+    ag_turn(1, 1, 2)
+    ag_last(2)
+    ag_turn(6, 0, 0)
+    do_pj1(1, 1)
+    ag_pass(1, 1, 3)
+    do_pj1(1, 0)
+    ag_cross(5, 0, 1, 1)
+    ag_cross(5, 0, 1, 2)
+    ag_turn(6, 1, 2)
+    ag_cross(5, 1, 1, 2)
+    do_at1(1)
+    ag_turn(6, 1, 3)
+    do_op1(1)
+    ag_turn(1, 0, 2)
+    ag_turn(1, 1, 3)
+    ag_turn(6, 1, 1)
+    ag_turn(1, 0, 0)
+    ag_cross(3, 0, 0, 1)
+    do_nf1(1)
+    ag_first(4)
+    ag_last(5)
+    ag_turn(1, 0, 3)
+    do_fu(1, 0)
+    ag_cross(3, 0, 0, 3)
+    do_fu(1, 1)
+    ag_turn(1, 0, 1)
+    ag_pass(1, 1, 1)
+    do_op0(0)
+    ag_spread(3, 0)
+    ag_turn(4, 0, 0)
+    ag_cross(3, 1, 0, 2)
+    ag_last(6)
+    ag_cross(3, 1, 1, 1)
+    ag_cross(3, 1, 0, 3)
+    do_fu(1, 2)
+    do_fu(1, 3)
+    ag_turn(4, 1, 0)
+    do_fd(1)
+    ag_turn(1, 1, 1)
+    ag_pass(4, 1, 3)
+    ag_pass(4, 0, 1)
+    ag_pass(4, 0, 3)
+    ag_cross(3, 0, 0, 2)
+    do_nf0(0)
+    ag_cross(3, 1, 0, 1)
+    do_n3(1)
+    ag_pass(4, 1, 2)
+    do_fb(1, 0)
+    ag_cross(3, 0, 1, 1)
+    ag_turn(4, 1, 3)
+    do_fb(1, 1)
+    ag_last(1)
+    do_fh(1)
+    do_pj1(0, 1)
+    do_pj1(0, 0)
+    ag_cross(3, 0, 1, 3)
+    ag_turn(4, 0, 1)
+    ag_cross(3, 0, 1, 2)
+    do_at1(0)
+    ag_pass(4, 1, 1)
+    do_sb(1)
+    do_gm(1, 1)
+    do_gm(1, 0)
+    ag_pass(4, 0, 2)
+    do_fg(1)
+    do_op1(0)
+    rs2_m(6, 0)
+    rs2_m(6, 1)
+    ag_cross(3, 1, 1, 2)
+    do_ab(1, 0)
+    do_ab(1, 1)
+    do_be(1)
+    ag_turn(4, 0, 2)
+    ag_turn(4, 1, 1)
+    do_nf1(0)
+    ag_cross(3, 1, 1, 3)
+    ag_turn(4, 1, 2)
+    ag_turn(4, 0, 3)
+    do_ag(1)
+    ag_last(3)
+    do_fu(0, 0)
+    do_fu(0, 1)
+    do_fu(0, 2)
+    ag_last(4)
+    rs2_m(5, 1)
+    do_fu(0, 3)
+    do_fd(0)
+    rs2(2, 0)
+    rs2(2, 1)
+    do_n3(0)
+    rs2_m(5, 0)
+    do_fb(0, 0)
+    do_fb(0, 1)
+    do_fh(0)
+    do_sb(0)
+    rs3(2, 1)
+    do_fg(0)
+    do_cb(1)
+    do_gm(0, 1)
+    rs3_m(6, 1)
+    do_gm(0, 0)
+    do_ab(0, 0)
+    rs2(4, 0)
+    do_be(0)
+    do_cb(0)
+    rs3(2, 0)
+    do_gm0(0)
+    do_ag(0)
+    do_gm0(2)
+    rs2(4, 1)
+    rs2_m(3, 1)
+    rs2_m(3, 0)
+    do_gm0(1)
+    do_ab0(0)
+    do_ab0(1)
+    do_be0(0)
+    rs2(1, 0)
+    rs2(1, 1)
+    do_be0(1)
+    do_ag0(0)
+    rs3(4, 1)
+    rs3(1, 1)
+    rs3_m(6, 0)
+    do_ag0(1)
+    held["g", 6] = rs4_m(6)
+    vec1()
+    rs3_m(3, 0)
+    rs3(1, 0)
+    rs3_m(5, 0)
+    rs2(0, 1)
+    do_fin(1)
+    rs3(4, 0)
+    vec2()
+    rs2(0, 0)
+    rs3_m(5, 1)
+    vec3()
+    do_fin(0)
+    held["g", 2] = rs4(2)
+    rs3(0, 1)
+    rs3(0, 0)
+    held["g", 1] = rs4(1)
+    rs3_m(3, 1)
+    vec4()
+    held["g", 5] = rs4_m(5)
+    held["g", 3] = rs4_m(3)
+    held["g", 4] = rs4(4)
+    held["g", 0] = rs4(0)
+    squares()
+    for cp in rs_sends:
+        cp.wait_send()
+    pending.pop().wait()
+    for name in list(held):
+        got(name)
+
+
+def fused(args):
+    anywhere = pl.BlockSpec(memory_space=pl.ANY)
+    vmem = pl.BlockSpec(memory_space=pltpu.VMEM)
+    s = jax.ShapeDtypeStruct
+    dma = pltpu.SemaphoreType.DMA
+    outs = [
+        (s((OWN, D), F32), anywhere),
+        (s((OWN, D), F32), anywhere),
+        (s((NU, 96, D), F32), anywhere),
+        (s((2, 32, D), F32), vmem),
+        (s((8, 128), F32), vmem),
+        (s((NU, 4, 2, 48, D), BF16), anywhere),
+        (s((NU, 4, 48, D), BF16), anywhere),
+        (s((NU, 3, 48, D), BF16), anywhere),
+        (s((NU, 2, 4, 48, D), BF16), anywhere),
+        (s((NU, 4, 48, D), BF16), anywhere),
+        (s((NU, 3, 48, D), BF16), anywhere),
+        (s((NU, 2, 3, 2, 48, D), BF16), anywhere),
+    ]
+    scratch = [
+        pltpu.VMEM((NU, 2, 4, 2, 96, D), BF16),
+        pltpu.VMEM((3, ALL, D), BF16),
+        pltpu.VMEM((ALL, D), BF16),
+        pltpu.VMEM((ALL, D), BF16),
+        pltpu.VMEM((3, OWN, D), F32),
+        pltpu.VMEM((OWN, D), F32),
+        pltpu.VMEM((OWN, D), F32),
+        pltpu.VMEM((OWN, D), BF16),
+        pltpu.VMEM((OWN, D), BF16),
+        pltpu.VMEM((2, ALL, 384), BF16),
+        pltpu.VMEM((2, ALL, 384), BF16),
+        pltpu.VMEM((2, ALL, 384), BF16),
+        pltpu.VMEM((2, 2, ALL, 256), BF16),
+        pltpu.VMEM((2, 8 * 3 * 4 * LP, 128), BF16),
+        pltpu.VMEM((2, 8 * 3 * 4 * RP, 128), BF16),
+        pltpu.VMEM((2, ALL, D), BF16),
+        pltpu.VMEM((2, ALL, D), BF16),
+        pltpu.VMEM((2, ALL, 640), BF16),
+        pltpu.VMEM((1, ALL, 384), BF16),
+        pltpu.VMEM((NU, 96, D), F32),
+        pltpu.VMEM((4, 4, 48, D), BF16),
+        pltpu.VMEM((2, 3, 48, D), BF16),
+        pltpu.VMEM((32, D), F32),
+        pltpu.VMEM((4, 32, D), F32),
+        pltpu.VMEM((4, 32, D), F32),
+        pltpu.VMEM((8, D), F32),
+        pltpu.VMEM((8, 8, 128), F32),
+        pltpu.VMEM((4, 8, 128), F32),
+        pltpu.VMEM((8, D), F32),
+        dma((4,)),
+        dma((3,)),
+        dma((NU,)),
+        dma((26,)),
+        dma((26,)),
+        dma((NU, 2, 16)),
+        dma((NU, 2, 16)),
+        dma((NU, 12)),
+        dma((NU, 12)),
+        dma((6,)),
+        dma((6,)),
+        dma((10,)),
+        dma((10,)),
+    ]
+    smem = pl.BlockSpec(memory_space=pltpu.SMEM)
+    return pl.pallas_call(
+        kernel,
+        out_shape=[o[0] for o in outs],
+        in_specs=[vmem, vmem, vmem, vmem, smem, vmem, anywhere, vmem],
+        out_specs=[o[1] for o in outs],
+        scratch_shapes=scratch,
+        compiler_params=pltpu.CompilerParams(
+            collective_id=0, has_side_effects=True, vmem_limit_bytes=VMEM_BYTES
+        ),
+    )(*args)
+
+
+def adam_update(master, first, second, grad, rate):
+    first = BETA_FIRST * first + (1.0 - BETA_FIRST) * grad
+    second = BETA_SECOND * second + (1.0 - BETA_SECOND) * grad * grad
+    first_hat = first / (1.0 - BETA_FIRST**STEP)
+    second_hat = second / (1.0 - BETA_SECOND**STEP)
+    fresh = master - rate * (first_hat / (jnp.sqrt(second_hat) + ADAM_EPSILON) + WEIGHT_DECAY * master)
+    return (fresh, first, second)
+
+
+def update_kernel(
+    vg, sq, vec, vec_m, vec_v, out3, gx, g32, aw, am, av, fw, fm, fv,
+    lang_out, vis_out, lang_grad, vis_grad, aw_o, am_o, av_o, ac_o, fw_o, fm_o, fv_o, fc_o,
+    vec_o, vec_mo, vec_vo, bias_o, norm_o,
+    G, AW, AM, AV, AC, FW, FM, FV, FC, S0, S1, L0, L1, V0, V1, VT, gs, isem, osem, ssem,
+):
+    def go(src, dst, sem):
+        cp = pltpu.make_async_copy(src, dst, sem)
+        cp.start()
+        return cp
+
+    streams = [go(out3, S0, ssem.at[0]), go(gx, S1, ssem.at[1])]
+    grads = [go(g32.at[u], G.at[u], gs.at[u]) for u in range(NU)]
+    loads = []
+    for u in range(NU):
+        if u < 3:
+            refs = ((aw.at[u], AW.at[u]), (am.at[u], AM.at[u]), (av.at[u], AV.at[u]))
+        else:
+            i = (u - 3) // 2, (u - 3) % 2
+            refs = tuple((a.at[i[0], i[1]], b.at[i[0], i[1]]) for a, b in ((fw, FW), (fm, FM), (fv, FV)))
+        loads.append([go(a, b, isem.at[u, k]) for k, (a, b) in enumerate(refs)])
+
+    lane = lax.broadcasted_iota(jnp.int32, (1, 384), 1)
+    for b in range(3):
+        for j in range(2):
+            k = 15 + 2 * b + j
+            for base, line in ((0, b), (384, 3 + b)):
+                v0, v1 = vg[0, k : k + 1, base : base + 384], vg[1, k : k + 1, base : base + 384]
+                VT[line : line + 1, j * 384 : j * 384 + 384] = jnp.where(lane < 192, v0, pltpu.roll(v1, 192, 1))
+    for line, k, n in ((6, 10, 3), (9, 0, 10), (19, 13, 2)):
+        VT[line : line + n, :] = vg[0, k : k + n, :] + vg[1, k : k + n, :]
+    for i in range(4):
+        for core in range(2):
+            VT[21 + 2 * i + core : 22 + 2 * i + core, :] = vg[core, 21 + i : 22 + i, :]
+    total = VT[0:29, :]
+    squares = jnp.sum(jnp.sum(total * total, axis=1, keepdims=True), axis=0, keepdims=True) + sq[0:1, 0:1]
+    norm = jnp.sqrt(squares)
+    clip = CLIP_NORM / jnp.maximum(norm, CLIP_NORM)
+    norm_o[...] = jnp.broadcast_to(norm, (8, 128))
+    clipped = total * clip
+    bias_o[...] = clipped[19:21, :]
+    vec_o[...], vec_mo[...], vec_vo[...] = adam_update(vec[...], vec_m[...], vec_v[...], clipped, RATE_VECTOR)
+
+    outs = []
+    for k, (src, L, V, lo, vo) in enumerate(((S0, L0, V0, lang_out, vis_out), (S1, L1, V1, lang_grad, vis_grad))):
+        streams[k].wait()
+        for M, base, count, pad in ((L, 0, 20, LP), (V, WO, 36, RP)):
+            for p in range(0, count, 4):
+                rows = jnp.stack([src[base + i * pad + p : base + i * pad + p + 4, :] for i in range(8)])
+                M[p : p + 4] = jnp.swapaxes(rows, 0, 1)
+        outs += [go(L, lo, ssem.at[2 + 2 * k]), go(V, vo, ssem.at[3 + 2 * k])]
+
+    for u in range(NU):
+        grads[u].wait()
+        for cp in loads[u]:
+            cp.wait()
+        if u < 3:
+            g = G.at[u]
+            parts = (
+                g[:, 0:192],
+                jnp.concatenate([g[:, 256:384], swap(g[:, 128:256])[:, 0:64]], axis=1),
+                g[:, 384:576],
+                jnp.concatenate([g[:, 640:768], swap(g[:, 512:640])[:, 0:64]], axis=1),
+            )
+            for j in range(4):
+                new, m, v = adam_update(AW[u, j], AM[u, j], AV[u, j], parts[j] * clip, RATE_MATRIX)
+                AW[u, j], AM[u, j], AV[u, j], AC[u, j] = new, m, v, new.astype(BF16)
+            refs = ((AW.at[u], aw_o.at[u]), (AM.at[u], am_o.at[u]), (AV.at[u], av_o.at[u]), (AC.at[u], ac_o.at[u]))
+        else:
+            s, j = (u - 3) // 2, (u - 3) % 2
+
+            def step(i, carry, s=s, j=j, u=u):
+                r = pl.ds(pl.multiple_of(i * 16, 16), 16)
+                new, m, v = adam_update(FW[s, j, r, :], FM[s, j, r, :], FV[s, j, r, :], G[u, r, :] * clip, RATE_MATRIX)
+                FW[s, j, r, :] = new
+                FM[s, j, r, :] = m
+                FV[s, j, r, :] = v
+                FC[s, j, r, :] = new.astype(BF16)
+                return carry
+
+            lax.fori_loop(0, 6, step, 0)
+            refs = tuple(
+                (a.at[s, j], b.at[s, j]) for a, b in ((FW, fw_o), (FM, fm_o), (FV, fv_o), (FC, fc_o))
+            )
+        outs += [go(a, b, osem.at[u, k]) for k, (a, b) in enumerate(refs)]
+    for cp in outs:
+        cp.wait()
+
+
+def fast_body(
+    lang_in, vis_in, word_lengths, lang_cot, vis_cot,
+    attn_master, attn_first, attn_second, ffn_master, ffn_first, ffn_second,
+    vectors, vector_first, vector_second,
+):
+    lang_in, vis_in, lang_cot, vis_cot = (a.swapaxes(0, 1) for a in (lang_in, vis_in, lang_cot, vis_cot))
+    out3, gx, g32, vg, sq = fused(
+        (lang_in, vis_in, lang_cot, vis_cot, word_lengths, attn_master, ffn_master, vectors)
+    )[:5]
+    anywhere = pl.BlockSpec(memory_space=pl.ANY)
+    vmem = pl.BlockSpec(memory_space=pltpu.VMEM)
+    like = lambda a, dtype=F32: jax.ShapeDtypeStruct(a.shape, dtype)
+    streams, matrices = [lang_in, vis_in] * 2, [attn_master] * 4 + [ffn_master] * 4
+    types = [F32, F32, F32, BF16] * 2
+    scratch = [pltpu.VMEM((NU, 96, D), F32)]
+    scratch += [pltpu.VMEM(a.shape, dt) for a, dt in zip(matrices, types)]
+    scratch += [pltpu.VMEM((OWN, D), F32)] * 2
+    scratch += [pltpu.VMEM(a.shape, F32) for a in (lang_in, lang_in, vis_in, vis_in)]
+    scratch += [pltpu.VMEM((32, D), F32)]
+    dma = pltpu.SemaphoreType.DMA
+    scratch += [dma((NU,)), dma((NU, 3)), dma((NU, 4)), dma((6,))]
+    outs = pl.pallas_call(
+        update_kernel,
+        out_shape=[like(a) for a in streams]
+        + [like(a, dt) for a, dt in zip(matrices, types)]
+        + [like(vectors)] * 3
+        + [jax.ShapeDtypeStruct((2, D), F32), jax.ShapeDtypeStruct((8, 128), F32)],
+        in_specs=[vmem] * 5 + [anywhere] * 9,
+        out_specs=[anywhere] * 12 + [vmem] * 5,
+        scratch_shapes=scratch,
+        compiler_params=pltpu.CompilerParams(vmem_limit_bytes=48 * 1024 * 1024),
+    )(
+        vg, sq, vectors, vector_first, vector_second, out3, gx, g32,
+        attn_master, attn_first, attn_second, ffn_master, ffn_first, ffn_second,
+    )
+    return (*(a.swapaxes(0, 1) for a in outs[:4]), *outs[4:16], outs[16][0, 0])
 
 
 def normalize(inputs, norm_gain, norm_shift):
@@ -207,18 +1449,7 @@
     )
 
 
-def adam_update(master, first, second, grad, rate):
-    first = BETA_FIRST * first + (1.0 - BETA_FIRST) * grad
-    second = BETA_SECOND * second + (1.0 - BETA_SECOND) * grad * grad
-    first_hat = first / (1.0 - BETA_FIRST**STEP)
-    second_hat = second / (1.0 - BETA_SECOND**STEP)
-    fresh = master - rate * (
-        first_hat / (jnp.sqrt(second_hat) + ADAM_EPSILON) + WEIGHT_DECAY * master
-    )
-    return (fresh, first, second)
-
-
-def body(
+def general_body(
     lang_in,
     vis_in,
     word_lengths,
@@ -489,8 +1720,9 @@
 
 
 def solution(mesh):
+    tuned = dict(mesh.shape) == {"dp": 8, "tensor": 4}
     return jax.shard_map(
-        body,
+        fast_body if tuned else general_body,
         mesh=mesh,
         in_specs=(
             P(("dp", "tensor"), None, None),

time: 1150 us -> 323 us (0.28)
  waiting for transfers between devices: 507 us -> 0 us
  Pallas kernels: 0 us -> 311 us
  local copies, waits for them, and re-layouts: 224 us -> 5.93 us
  matrix products: 175 us -> 0 us
  blocking collectives: 110 us -> 0 us
  other arithmetic: 95.9 us -> 0 us
  between operations: 21.1 us -> 0.94 us
    pallas_call x0 -> x2, Pallas kernels: none -> 311 us  [the longest x1 304 us: fused(): pl.pallas_call(kernel, out_shape=[o[0] for o in outs], in_specs=[vmem, vm...]
    dot_general x88 -> x0, matrix products: 175 us -> none  [the longest x20 61.1 us: product(): return jnp.dot(left_rows, right_matrix, preferred_element_type=jnp.float32)]
    all_gather x8 -> x0, waiting for transfers between devices: 150 us -> none  [the longest x1 70.7 us: body(): lax.all_gather(attn_master.astype(jnp.bfloat16), 'dp', axis=2, tiled=True)]
    reduce_scatter x7 -> x0, waiting for transfers between devices: 124 us -> none  [the longest x3 73.1 us: collect(): lax.psum_scatter(region_terms.astype(jnp.bfloat16), 'tensor', scatter_dim...]
    psum x1 -> x0, waiting for transfers between devices: 119 us -> none  [body(): vector_total = lax.psum(vector_grad, ('dp', 'tensor'))]
    unnamed x30 -> x0, waiting for transfers between devices: 115 us -> none
    unnamed x458 -> x18, local copies, waits for them, and re-layouts: 94.9 us -> 5.42 us
    all_gather x6 -> x0, blocking collectives: 69.6 us -> none  [the longest x3 38.9 us: fetch_rows(): lax.all_gather(word_grads.astype(jnp.bfloat16), 'tensor', axis=0, tiled=T...]
  transfers between devices with their start and end apart: 23 -> 0, of which waited for: 13 -> 0; matrix products, arithmetic and copies ran while one was open for 35% -> 0% of each run, Pallas kernels for 0% -> 0%
where the time goes in v2:
time: 323 us; the launch traced here: 318 us
  Pallas kernels  311 us (96%)
  local copies, waits for them, and re-layouts  5.93 us (2%)
    pallas_call x1, Pallas kernels, fused(): pl.pallas_call(kernel, out_shape=[o[0] for o in outs], in_specs=[vmem, vm...  304 us
    pallas_call x1, Pallas kernels, fast_body(): pl.pallas_call(update_kernel, out_shape=[like(a) for a in streams] + [lik...  7.68 us

profile of v2, /device:TPU:0, one launch (start us, length us, event | category | flops | bytes accessed | tf_op | source)
XLA Modules:
  0.0 318.4 jit_solution(15815736379752867241)
XLA Ops:
  0.7 0.0 copy-start
  0.7 0.0 copy-start.4
  0.7 0.0 copy-start.6
  0.7 0.0 copy-start.7
  0.7 303.8 %shard_map.269 = (f32[512,768]{1,0:T(8,128)}, f32[512,768]{1,0:T(8,128)}, f32[7,96,768]{2,1,0:T(8,128)}, f32[2,32,768]{2,1,0:T(8,128)}, f32[8,128]{1,0:T(8,128)}...) custom-call(bf16[20,8,768]{2,1,0:T(8,128)(2,1)} %bitcast.11, ...), custom_call_target="tpu_custom_call" | custom-call | tf_op jit(solution)/shard_map/pallas_call | solution.py:1115
  304.5 0.0 copy-done
  304.5 0.0 copy-done.4
  304.5 0.0 copy-done.6
  304.5 0.0 copy-done.7
  304.6 0.0 copy-start.1
  304.6 1.3 copy-done.1
  305.8 0.0 copy-start.2
  305.8 1.3 copy-done.2
  307.1 0.0 copy-start.3
  307.1 1.3 copy-done.3
  308.4 0.0 copy-start.5
  308.4 0.9 copy-done.5
  309.3 0.0 copy-start.8
  309.3 0.7 copy-done.8
  310.0 7.7 %shard_map.270 = (f32[20,8,768]{2,1,0:T(8,128)}, f32[36,8,768]{2,1,0:T(8,128)}, f32[20,8,768]{2,1,0:T(8,128)}, f32[36,8,768]{2,1,0:T(8,128)}, f32[3,4,96,192]{3,...) custom-call(f32[2,32,768]{2,1,0:T(8,128)S(1)} %copy-done.5, ...), custom_call_target="tpu_custom_call" | custom-call | tf_op jit(solution)/shard_map/pallas_call | solution.py:1246
  317.7 0.5 slice.3
Async XLA Ops:
  0.7 303.9 %copy-start = (f32[3,4,96,192]{3,2,1,0:T(8,128)S(1)}, f32[3,4,96,192]{3,2,1,0:T(8,128)}, u32[]{:S(2)}) copy-start(f32[3,4,96,192]{3,2,1,0:T(8,128)} %aw.1) | copy-start | bytes 2654212
  0.7 303.9 %copy-start.4 = (f32[29,768]{1,0:T(8,128)S(1)}, f32[29,768]{1,0:T(8,128)}, u32[]{:S(2)}) copy-start(f32[29,768]{1,0:T(8,128)} %vec.3) | copy-start | bytes 267268
  0.7 303.9 %copy-start.6 = (f32[29,768]{1,0:T(8,128)S(1)}, f32[29,768]{1,0:T(8,128)}, u32[]{:S(2)}) copy-start(f32[29,768]{1,0:T(8,128)} %vec_m.1) | copy-start | bytes 267268
  0.7 303.9 %copy-start.7 = (f32[29,768]{1,0:T(8,128)S(1)}, f32[29,768]{1,0:T(8,128)}, u32[]{:S(2)}) copy-start(f32[29,768]{1,0:T(8,128)} %vec_v.1) | copy-start | bytes 267268
  304.6 1.3 copy-start.1
  305.8 1.3 copy-start.2
  307.1 1.3 copy-start.3
  308.4 0.9 copy-start.5
  309.3 0.7 copy-start.8

commit v3 on v2

--- a/solution.py
+++ b/solution.py
@@ -72,6 +72,11 @@
     core_n, y_n, x_n = at(z, x, y, 1 - c), at(z, x, oy, c), at(z, ox, y, c)
     zk = [(z + k) % 4 for k in range(4)]
     z_n = [at(zk[k], x, y, c) for k in range(4)]
+    half = z // 2
+    near, mid, far = z + 1 - 2 * (z % 2), 2 - half, 3 - 3 * half
+    inner = z % 3 != 0
+    zr = [z, near, mid, far]
+    mid_role = jnp.where(inner, 2, 3)
     flips = [(i, j, k) for i in (0, 1) for j in (0, 1) for k in (0, 1)][1:]
     plane = [at(z, (x + i) % 2, (y + j) % 2, (c + k) % 2) for i, j, k in flips]
 
@@ -92,7 +97,7 @@
     rows_of = (pl.ds(0, 48), pl.ds(48, 48))
 
     def shard(u, part, dy, dx, dz):
-        return W.at[u, y if dy == 0 else oy, zk[dz], x if dx == 0 else ox, rows_of[part], :]
+        return W.at[u, y if dy == 0 else oy, zr[dz], x if dx == 0 else ox, rows_of[part], :]
 
     def sid(dy, dx, dz):
         return dy * 8 + dx * 4 + dz
@@ -101,70 +106,78 @@
 
     def ag_send(u, part, dy, dx, dz, way):
         src = shard(u, part, dy, dx, dz)
-        if way == "x":
-            there, dev = sid(dy, 1 - dx, dz), x_n
-        elif way == "y":
-            there, dev = sid(1 - dy, dx, dz), y_n
-        else:
-            there, dev = sid(dy, dx, (dz - way) % 4), z_n[way]
+        there, dev = {
+            "x": (sid(dy, 1 - dx, dz), x_n),
+            "y": (sid(1 - dy, dx, dz), y_n),
+            "near": (sid(dy, dx, 1), at(near, x, y, c)),
+            "mid": (sid(dy, dx, 0) + mid_role, at(mid, x, y, c)),
+            "relay": (sid(dy, dx, dz), at(near, x, y, c)),
+        }[way]
         n = ag_sends.setdefault((u, part), [])
         cp = remote(src, src, ags.at[u, part, len(n)], agr.at[u, part, there], dev)
-        cp.start()
-        n.append(cp)
+        n.append((cp, way == "relay"))
+        if way == "relay":
+            pl.when(inner)(cp.start)
+        else:
+            cp.start()
 
     def ag_recv(u, part, dy, dx, dz):
         src = shard(u, part, dy, dx, dz)
-        remote(src, src, ags.at[u, part, 15], agr.at[u, part, sid(dy, dx, dz)], x_n).wait_recv()
+        remote(src, src, ags.at[u, part, 17], agr.at[u, part, sid(dy, dx, dz)], x_n).wait_recv()
 
     def ag_first(u):
         for part in (0, 1):
-            for k in (1, 3, 2):
-                ag_send(u, part, 0, 0, 0, k)
-            ag_send(u, part, 0, 0, 0, "x")
-            ag_send(u, part, 0, 0, 0, "y")
+            for way in ("mid", "near", "x", "y"):
+                ag_send(u, part, 0, 0, 0, way)
+
+    def ag_relay(u, part, dy, dx, k):
+        if k >= 2:
+            ag_send(u, part, dy, dx, k, "relay")
 
     def ag_pass(u, part, k):
         ag_recv(u, part, 0, 0, k)
+        ag_relay(u, part, 0, 0, k)
         ag_send(u, part, 0, 0, k, "x")
         ag_send(u, part, 0, 0, k, "y")
 
     def ag_turn(u, part, k):
-        if part == 0:
-            ag_recv(u, 0, 0, 1, k)
-            ag_send(u, 0, 0, 1, k, "y")
-        else:
-            ag_recv(u, 1, 1, 0, k)
-            ag_send(u, 1, 1, 0, k, "x")
+        dy, dx = ((0, 1), (1, 0))[part]
+        ag_recv(u, part, dy, dx, k)
+        ag_send(u, part, dy, dx, k, "yx"[part])
 
     def ag_first_m(u):
         ag_send(u, 0, 0, 0, 0, "x")
         ag_send(u, 1, 0, 0, 0, "y")
         for part in (0, 1):
-            for k in (1, 3, 2):
-                ag_send(u, part, 0, 0, 0, k)
+            ag_send(u, part, 0, 0, 0, "mid")
+            ag_send(u, part, 0, 0, 0, "near")
         ag_send(u, 0, 0, 0, 0, "y")
         ag_send(u, 1, 0, 0, 0, "x")
 
     def ag_spread(u, part):
         dy, dx = ((0, 1), (1, 0))[part]
         ag_recv(u, part, dy, dx, 0)
-        for k in (1, 3, 2, "yx"[part]):
-            ag_send(u, part, dy, dx, 0, k)
+        for way in ("mid", "near", "yx"[part]):
+            ag_send(u, part, dy, dx, 0, way)
 
     def ag_cross(u, part, q, k):
         dy, dx = ((0, q), (q, 0))[part]
         ag_recv(u, part, dy, dx, k)
+        ag_relay(u, part, dy, dx, k)
         ag_send(u, part, dy, dx, k, "yx"[part])
 
     def ag_last(u):
-        for k in (0, 1, 3, 2):
+        for k in range(4):
             for dx in (0, 1):
                 ag_recv(u, 0, 1, dx, k)
             for dy in (0, 1):
                 ag_recv(u, 1, dy, 1, k)
         for part in (0, 1):
-            for cp in ag_sends[(u, part)]:
-                cp.wait_send()
+            for cp, relayed in ag_sends[(u, part)]:
+                if relayed:
+                    pl.when(inner)(cp.wait_send)
+                else:
+                    cp.wait_send()
 
     core_count = [0]
 
@@ -190,7 +203,7 @@
         YO[o : o + n, :] = terms(r, n)
         return cp
 
-    own_f = [local(ffn_w.at[i // 2, i % 2], Z.at[0, pl.ds(96 * i, 96)], lsem.at[i]) for i in range(4)]
+    own_f = [local(ffn_w.at[i // 2, i % 2], Z.at[2, pl.ds(96 * i, 96)], lsem.at[i]) for i in range(4)]
     for cp in own_f:
         cp.start()
 
@@ -202,11 +215,12 @@
             w[:, base + 128 : base + 256] = jnp.concatenate([a[:, 128:192], b[:, 128:192]], axis=1).astype(BF16)
             w[:, base + 256 : base + 384] = b[:, 0:128].astype(BF16)
 
-    for u in range(3):
-        pack(u)
-    for i, cp in enumerate(own_f):
-        cp.wait()
-        W[3 + i, y, z, x] = Z[0, 96 * i : 96 * i + 96, :].astype(BF16)
+    def own_weights(u):
+        if u < 3:
+            pack(u)
+        else:
+            own_f[u - 3].wait()
+            W[u, y, z, x] = Z[2, 96 * (u - 3) : 96 * (u - 2), :].astype(BF16)
 
     def items_of(s):
         return (lang_in, lang_cot, 20, LP) if s == 0 else (vis_in, vis_cot, 36, RP)
@@ -511,8 +525,8 @@
 
         return branch_sum(s, terms)
 
-    def attn_grad(sec, u, r0, r1, DY, sides=(0, 1)):
-        for yy in sides:
+    def attn_grad(sec, u, r0, r1, DY):
+        for yy in range(2):
             k = 15 + 2 * u + yy
             VG[k : k + 1, 0:640] = jnp.sum(E[yy, r0:r1, :].astype(F32), axis=0, keepdims=True)
             for m in range(2):
@@ -521,7 +535,46 @@
                 b = tn(DY[r0:r1, mc], F[sec, yy, r0:r1, :])
                 put_grad(u, yy, m, jnp.concatenate([a[:, 0:512], a[:, 512:640] + b[:, 0:128], b[:, 128:256]], axis=1))
 
+    def cross_grad(j, DY):
+        for yy in range(2):
+            if j == 0:
+                k = 15 + yy
+                VG[k : k + 1, 0:640] = jnp.sum(E[yy].astype(F32), axis=0, keepdims=True)
+            for m in range(2):
+                mc = slice(m * 384, m * 384 + 384)
+                if j == 0:
+                    g = tn(H[0, :, mc], E[yy, :, 0:384])
+                else:
+                    a = tn(H[0, :, mc], E[yy, :, 384:640])
+                    b = tn(DY[:, mc], F[0, yy])
+                    g = jnp.concatenate([a[:, 0:128], a[:, 128:256] + b[:, 0:128], b[:, 128:256]], axis=1)
+                W[0, yy, 2 * m : 2 * m + 2, :, :, j * 384 : j * 384 + 384] = g.astype(BF16).reshape(2, 2, 96, 384)
+
     top, bot = rows_of
+    def real(u):
+        return u % NU
+
+    def cols(u):
+        return {0: pl.ds(0, 384), 7: pl.ds(384, 384)}.get(u, pl.ds(0, D))
+
+    def here(u):
+        return pl.ds(0, 384) if u in (0, 7) else pl.ds(0, D)
+
+    def slab(u, yy, zz, xx, rows):
+        return W.at[real(u), yy, zz, xx, rows, cols(u)]
+
+    every = slice(None)
+
+    def slot(ref, u, *index):
+        rest = (every,) * (len(ref.shape) - 2 - len(index))
+        return ref.at[(real(u), *index, *rest, cols(u))]
+
+    def stage(u, i):
+        return ST.at[i, :, :, here(u)]
+
+    def stage3(u, i):
+        return ST3.at[i, :, :, here(u)]
+
     rs_sends = []
 
     def rs_send(u, k, src, dst, dev):
@@ -534,120 +587,103 @@
 
     def rs1(u):
         for k, (xx, yy) in enumerate(((ox, oy), (x, y))):
-            rs_send(u, k, W.at[u, oy, :, xx, top, :], ra1.at[u, :, xx], y_n)
-            rs_send(u, 2 + k, W.at[u, yy, :, ox, bot, :], rb1.at[u, yy], x_n)
-
-    def add_in(dst, stage):
-        def step(j, carry):
-            dst(j)[...] = (dst(j)[...].astype(F32) + stage[j].astype(F32)).astype(BF16)
-            return carry
-
-        lax.fori_loop(0, 4, step, 0)
-
-    def rs2_m(u, part):
-        cps = []
-        for q in (0, 1):
-            rs_recv(u, 2 * part + q, (ra1.at[u, :, (ox, x)[q]], rb1.at[u, (oy, y)[q]])[part])
-        for q in (0, 1):
-            cps.append(local((ra1.at[u, :, q], rb1.at[u, q])[part], ST.at[q], lsem.at[q]))
-            cps[-1].start()
-        for q in (0, 1):
-            cps[q].wait()
-            if part == 0:
-                add_in(lambda j: W.at[u, y, j, q, top, :], ST.at[q])
-            else:
-                add_in(lambda j: W.at[u, q, j, x, bot, :], ST.at[q])
-        for k in (1, 3, 2):
-            src = (W.at[u, y, zk[k], :, top, :], W.at[u, :, zk[k], x, bot, :])[part]
-            rs_send(u, 5 + 3 * part + k, src, rz.at[u, part, k - 1], z_n[k])
-
-    def rs3_m(u, part):
-        for k in (1, 3, 2):
-            rs_recv(u, 5 + 3 * part + k, rz.at[u, part, k - 1])
-        cps = [local(rz.at[u, part, :, q], ST3.at[q], lsem.at[2 + q]) for q in (0, 1)]
+            rs_send(u, k, slab(u, oy, every, xx, top), slot(ra1, u, every, xx), y_n)
+            rs_send(u, 2 + k, slab(u, yy, every, ox, bot), slot(rb1, u, yy), x_n)
+
+    def fetch(u, pairs):
+        cps = [local(src, dst, lsem.at[i]) for i, (src, dst) in enumerate(pairs)]
         for cp in cps:
             cp.start()
         for cp in cps:
             cp.wait()
+
+    def add_in(dst, *stages):
+        def step(j, carry):
+            total = dst(j)[...].astype(F32)
+            for st in stages:
+                total = total + st[j].astype(F32)
+            dst(j)[...] = total.astype(BF16)
+            return carry
+
+        lax.fori_loop(0, 4, step, 0)
+
+    def first_arrival(u, part, q):
+        return slot(ra1, u, every, q) if part == 0 else slot(rb1, u, q)
+
+    def rs2_m(u, part):
+        for q in (0, 1):
+            rs_recv(u, 2 * part + q, first_arrival(u, part, ((ox, x), (oy, y))[part][q]))
+        fetch(u, [(first_arrival(u, part, q), stage(u, q)) for q in (0, 1)])
+        for q in (0, 1):
+            add_in(lambda j: slab(u, y, j, q, top) if part == 0 else slab(u, q, j, x, bot), stage(u, q))
+        for k in (1, 3, 2):
+            src = slab(u, y, zk[k], every, top) if part == 0 else slab(u, every, zk[k], x, bot)
+            rs_send(u, 5 + 3 * part + k, src, slot(rz, u, part, k - 1), z_n[k])
+
+    def rs3_m(u, part):
+        for k in (1, 3, 2):
+            rs_recv(u, 5 + 3 * part + k, slot(rz, u, part, k - 1))
+        fetch(u, [(slot(rz, u, part, every, q), stage3(u, q)) for q in (0, 1)])
+
+        def total(ref, q):
+            g = ref[...].astype(F32)
+            for k in range(3):
+                g = g + ST3[q, k, :, here(u)].astype(F32)
+            return g
+
         rows = rows_of[part]
-
-        def total(yy, xx, q):
-            g = W[u, yy, z, xx, rows, :].astype(F32)
-            for k in range(3):
-                g = g + ST3[q, k].astype(F32)
-            return g
-
+        other, q, dst, dev = ((slab(u, y, z, ox, rows), ox, ra3, x_n), (slab(u, oy, z, x, rows), oy, rb3, y_n))[part]
+        other[...] = total(other, q).astype(BF16)
+        rs_send(u, 4 + part, other, slot(dst, u, 0), dev)
+        G3[real(u), rows, cols(u)] = total(slab(u, y, z, x, rows), (x, y)[part])
+
+    def rs4_m(u):
+        for part, dst in ((0, ra3), (1, rb3)):
+            rs_recv(u, 4 + part, slot(dst, u, 0))
+        fetch(u, [(slot(dst, u, 0), ST3.at[part, 0, :, here(u)]) for part, dst in ((0, ra3), (1, rb3))])
+        return rs_end(u, 1)
+
+    def rs2(u, part):
+        q = (ox, oy)[part]
+        src = first_arrival(u, part, q)
+        rs_recv(u, 2 * part, src)
+        fetch(u, [(src, stage(u, part))])
         if part == 0:
-            W[u, y, z, ox, rows, :] = total(y, ox, ox).astype(BF16)
-            rs_send(u, 4, W.at[u, y, z, ox, rows, :], ra3.at[u, 0], x_n)
+            add_in(lambda j: slab(u, y, j, ox, top), stage(u, 0))
+            rs_send(u, 4, slab(u, y, every, ox, top), slot(ra2, u), x_n)
         else:
-            W[u, oy, z, x, rows, :] = total(oy, x, oy).astype(BF16)
-            rs_send(u, 5, W.at[u, oy, z, x, rows, :], rb3.at[u, 0], y_n)
-        G3[u, rows, :] = total(y, x, (x, y)[part])
-
-    def rs4_m(u):
-        cps = []
-        for part, dst in ((0, ra3), (1, rb3)):
-            rs_recv(u, 4 + part, dst.at[u, 0])
-            cps.append(local(dst.at[u, 0], ST3.at[part, 0], lsem.at[part]))
-            cps[-1].start()
-        for cp in cps:
-            cp.wait()
-        return rs_end(u, 1)
-
-    def rs2(u, part):
-        src, k = ((ra1.at[u, :, ox], 0), (rb1.at[u, oy], 2))[part]
-        rs_recv(u, k, src)
-        cp = local(src, ST.at[part], lsem.at[part])
-        cp.start()
-        cp.wait()
-        if part == 0:
-            add_in(lambda j: W.at[u, y, j, ox, top, :], ST.at[0])
-            rs_send(u, 4, W.at[u, y, :, ox, top, :], ra2.at[u], x_n)
-        else:
-            add_in(lambda j: W.at[u, oy, j, x, bot, :], ST.at[1])
-            rs_send(u, 5, W.at[u, oy, :, x, bot, :], rb2.at[u], y_n)
+            add_in(lambda j: slab(u, oy, j, x, bot), stage(u, 1))
+            rs_send(u, 5, slab(u, oy, every, x, bot), slot(rb2, u), y_n)
 
     def rs3(u, part):
-        cps = []
-        for i, (k, src) in enumerate((((1, ra1.at[u, :, x]), (4, ra2.at[u])), ((3, rb1.at[u, y]), (5, rb2.at[u])))[part]):
+        sources = (first_arrival(u, part, (x, y)[part]), slot((ra2, rb2)[part], u))
+        for k, src in zip((2 * part + 1, 4 + part), sources):
             rs_recv(u, k, src)
-            cps.append(local(src, ST.at[2 + i], lsem.at[2 + i]))
-            cps[-1].start()
-        for cp in cps:
-            cp.wait()
+        fetch(u, [(src, stage(u, 2 + i)) for i, src in enumerate(sources)])
         rows = rows_of[part]
-
-        def step(j, carry):
-            w = W.at[u, y, j, x, rows, :]
-            w[...] = (w[...].astype(F32) + ST[2, j].astype(F32) + ST[3, j].astype(F32)).astype(BF16)
-            return carry
-
-        own = W[u, y, z, x, rows, :].astype(F32) + ST[2, z].astype(F32) + ST[3, z].astype(F32)
-        lax.fori_loop(0, 4, step, 0)
-        G3[u, rows, :] = own
+        own = slab(u, y, z, x, rows)[...].astype(F32)
+        for i in (2, 3):
+            own = own + ST[i, z, :, here(u)].astype(F32)
+        add_in(lambda j: slab(u, y, j, x, rows), stage(u, 2), stage(u, 3))
+        G3[real(u), rows, cols(u)] = own
         for k in (1, 3, 2):
-            rs_send(u, 5 + 3 * part + k, W.at[u, y, zk[k], x, rows, :], (ra3, rb3)[part].at[u, k - 1], z_n[k])
+            rs_send(u, 5 + 3 * part + k, slab(u, y, zk[k], x, rows), slot((ra3, rb3)[part], u, k - 1), z_n[k])
 
     def rs4(u):
-        cps = []
         for part, dst in ((0, ra3), (1, rb3)):
             for k in (1, 3, 2):
-                rs_recv(u, 5 + 3 * part + k, dst.at[u, k - 1])
-            cps.append(local(dst.at[u], ST3.at[part], lsem.at[part]))
-            cps[-1].start()
-        for cp in cps:
-            cp.wait()
+                rs_recv(u, 5 + 3 * part + k, slot(dst, u, k - 1))
+        fetch(u, [(slot(dst, u), stage3(u, part)) for part, dst in ((0, ra3), (1, rb3))])
         return rs_end(u, 3)
 
     def rs_end(u, terms):
         for part in (0, 1):
-            g = G3[u, rows_of[part], :]
+            g = G3[real(u), rows_of[part], cols(u)]
             for k in range(terms):
-                g = g + ST3[part, k].astype(F32)
-            G3[u, rows_of[part], :] = g
-            SQ[...] += jnp.sum((g * g).reshape(6, 8, D), axis=0)
-        cp = local(G3.at[u], g32.at[u], gsem.at[u])
+                g = g + ST3[part, k, :, here(u)].astype(F32)
+            G3[real(u), rows_of[part], cols(u)] = g
+            SQ[:, cols(u)] += jnp.sum((g * g).reshape(6, 8, g.shape[1]), axis=0)
+        cp = local(G3.at[real(u), :, cols(u)], g32.at[real(u), :, cols(u)], gsem.at[u])
         cp.start()
         return cp
 
@@ -808,9 +844,8 @@
         held["dh0", s] = branch_back(s, 0)
 
     def do_ag0(j):
-        attn_grad(0, 0, 0, ALL, DYA, (j,))
-        if j == 1:
-            rs1(0)
+        cross_grad(j, DYA)
+        rs1(7 * j)
 
     def do_fin(s):
         got(("dh0", s))
@@ -823,223 +858,235 @@
         held["gx", s] = local(XS.at[pl.ds(o, n)], gx.at[pl.ds(o, n)], osem.at[s])
         held["gx", s].start()
 
+    own_weights(0)
     ag_first(0)
+    own_weights(5)
+    own_weights(6)
+    own_weights(2)
+    ag_first(2)
+    own_weights(3)
+    ag_first_m(5)
     load_input()
-    ag_first(2)
+    ag_first_m(6)
+    ag_pass(0, 0, 3)
+    ag_spread(5, 0)
+    ag_pass(0, 0, 2)
+    ag_spread(6, 0)
+    ag_turn(0, 0, 0)
+    own_weights(1)
+    ag_spread(6, 1)
+    ag_pass(2, 1, 2)
+    ag_turn(0, 0, 3)
+    ag_pass(2, 0, 2)
+    ag_spread(5, 1)
+    ag_pass(0, 0, 1)
+    ag_pass(2, 1, 1)
+    ag_pass(2, 1, 3)
+    ag_pass(0, 1, 2)
     ag_turn(0, 1, 0)
+    own_weights(4)
+    ag_pass(0, 1, 3)
+    ag_first_m(1)
     ag_pass(0, 1, 1)
-    ag_first_m(5)
-    ag_turn(0, 0, 0)
-    ag_pass(0, 0, 1)
-    ag_pass(0, 0, 3)
+    ag_turn(2, 1, 2)
+    ag_cross(5, 1, 0, 3)
+    ag_cross(6, 0, 0, 1)
+    ag_turn(0, 1, 2)
+    ag_first_m(3)
+    ag_turn(0, 1, 3)
+    ag_turn(0, 0, 2)
     ag_turn(0, 1, 1)
-    ag_pass(0, 1, 2)
-    ag_first(6)
-    ag_pass(0, 1, 3)
-    ag_turn(0, 0, 3)
+    ag_pass(2, 0, 1)
     ag_turn(0, 0, 1)
-    ag_pass(2, 1, 1)
     ag_pass(2, 0, 3)
-    ag_pass(0, 0, 2)
-    ag_pass(2, 0, 2)
-    ag_turn(0, 1, 3)
+    ag_cross(5, 1, 0, 1)
+    ag_cross(5, 1, 1, 1)
+    ag_cross(5, 0, 0, 2)
+    ag_spread(1, 0)
+    ag_cross(1, 0, 0, 2)
+    ag_spread(3, 1)
+    ag_turn(2, 0, 0)
+    ag_cross(5, 0, 1, 2)
+    ag_cross(6, 1, 0, 1)
+    ag_cross(6, 1, 0, 2)
+    ag_spread(3, 0)
+    ag_last(0)
+    do_pj0(1)
+    ag_first_m(4)
+    ag_turn(2, 0, 2)
+    ag_turn(2, 1, 1)
+    ag_cross(5, 0, 0, 3)
+    ag_turn(2, 0, 1)
     ag_turn(2, 0, 3)
-    ag_turn(0, 1, 2)
-    ag_turn(0, 0, 2)
-    ag_pass(2, 1, 3)
-    ag_cross(5, 1, 0, 1)
-    ag_pass(2, 0, 1)
-    ag_last(0)
-    ag_pass(2, 1, 2)
-    ag_cross(5, 0, 0, 2)
-    ag_cross(5, 0, 0, 3)
-    ag_cross(5, 1, 0, 2)
-    ag_turn(6, 1, 0)
-    ag_turn(2, 0, 2)
     do_pj0(2)
     do_pj0(0)
-    ag_spread(5, 1)
+    ag_cross(5, 0, 1, 3)
+    ag_cross(6, 1, 1, 3)
     ag_turn(2, 1, 0)
+    ag_turn(2, 1, 3)
+    ag_cross(1, 1, 0, 2)
+    do_at0(0)
     ag_cross(5, 0, 0, 1)
-    do_pj0(1)
-    do_at0(0)
-    ag_pass(6, 0, 1)
-    ag_pass(6, 1, 1)
-    ag_pass(6, 0, 3)
-    ag_pass(6, 0, 2)
-    ag_cross(5, 1, 0, 3)
-    ag_turn(2, 1, 1)
-    ag_pass(6, 1, 3)
-    ag_turn(2, 0, 1)
-    ag_first(1)
-    ag_turn(6, 0, 3)
-    ag_spread(5, 0)
-    ag_turn(6, 0, 2)
-    ag_turn(2, 0, 0)
-    ag_pass(6, 1, 2)
-    ag_cross(5, 1, 1, 1)
-    ag_turn(1, 1, 0)
-    ag_first_m(3)
-    ag_turn(2, 1, 3)
+    ag_cross(3, 0, 0, 3)
     do_at0(1)
+    ag_cross(5, 1, 0, 2)
+    ag_cross(5, 0, 1, 1)
+    ag_cross(3, 1, 0, 2)
+    ag_cross(1, 1, 0, 3)
     do_op0(1)
-    ag_spread(3, 1)
+    ag_cross(6, 0, 1, 2)
+    ag_cross(6, 0, 1, 1)
+    ag_cross(6, 1, 1, 1)
+    ag_spread(1, 1)
+    ag_cross(4, 0, 0, 1)
+    ag_cross(3, 1, 1, 1)
     do_nf0(1)
-    ag_turn(6, 0, 1)
-    ag_turn(2, 1, 2)
-    ag_pass(1, 1, 2)
-    ag_pass(1, 0, 1)
-    ag_cross(5, 0, 1, 3)
-    ag_pass(1, 0, 2)
-    ag_pass(1, 0, 3)
+    ag_cross(3, 0, 0, 2)
+    ag_cross(6, 0, 0, 3)
+    ag_cross(1, 0, 1, 1)
+    ag_last(2)
+    do_pj1(1, 0)
+    ag_cross(5, 1, 1, 2)
     ag_cross(5, 1, 1, 3)
-    ag_turn(1, 1, 2)
-    ag_last(2)
-    ag_turn(6, 0, 0)
     do_pj1(1, 1)
-    ag_pass(1, 1, 3)
-    do_pj1(1, 0)
-    ag_cross(5, 0, 1, 1)
-    ag_cross(5, 0, 1, 2)
-    ag_turn(6, 1, 2)
-    ag_cross(5, 1, 1, 2)
     do_at1(1)
-    ag_turn(6, 1, 3)
+    ag_cross(3, 1, 1, 2)
+    ag_cross(3, 1, 0, 1)
+    ag_cross(6, 1, 0, 3)
+    ag_cross(1, 0, 1, 3)
     do_op1(1)
-    ag_turn(1, 0, 2)
-    ag_turn(1, 1, 3)
-    ag_turn(6, 1, 1)
-    ag_turn(1, 0, 0)
+    ag_cross(1, 1, 1, 3)
+    do_nf1(1)
+    ag_spread(4, 1)
+    ag_cross(6, 1, 1, 2)
+    ag_cross(6, 0, 0, 2)
+    do_op0(0)
+    ag_last(5)
+    ag_cross(1, 1, 0, 1)
+    ag_spread(4, 0)
     ag_cross(3, 0, 0, 1)
-    do_nf1(1)
-    ag_first(4)
-    ag_last(5)
-    ag_turn(1, 0, 3)
     do_fu(1, 0)
-    ag_cross(3, 0, 0, 3)
     do_fu(1, 1)
-    ag_turn(1, 0, 1)
-    ag_pass(1, 1, 1)
-    do_op0(0)
-    ag_spread(3, 0)
-    ag_turn(4, 0, 0)
-    ag_cross(3, 1, 0, 2)
-    ag_last(6)
-    ag_cross(3, 1, 1, 1)
-    ag_cross(3, 1, 0, 3)
+    ag_cross(4, 1, 0, 1)
+    ag_cross(6, 0, 1, 3)
+    ag_cross(1, 0, 1, 2)
+    ag_cross(1, 1, 1, 1)
     do_fu(1, 2)
     do_fu(1, 3)
-    ag_turn(4, 1, 0)
+    ag_cross(3, 0, 1, 2)
+    ag_cross(3, 0, 1, 1)
+    ag_cross(1, 1, 1, 2)
+    ag_last(6)
     do_fd(1)
-    ag_turn(1, 1, 1)
-    ag_pass(4, 1, 3)
-    ag_pass(4, 0, 1)
-    ag_pass(4, 0, 3)
-    ag_cross(3, 0, 0, 2)
     do_nf0(0)
-    ag_cross(3, 1, 0, 1)
+    ag_cross(1, 0, 0, 1)
+    ag_cross(4, 1, 0, 3)
+    ag_cross(4, 1, 1, 3)
+    ag_cross(1, 0, 0, 3)
     do_n3(1)
-    ag_pass(4, 1, 2)
+    ag_cross(3, 1, 1, 3)
+    ag_cross(3, 0, 1, 3)
+    ag_cross(4, 0, 0, 3)
+    ag_cross(4, 1, 1, 1)
+    ag_last(1)
+    ag_cross(3, 1, 0, 3)
+    do_pj1(0, 0)
     do_fb(1, 0)
-    ag_cross(3, 0, 1, 1)
-    ag_turn(4, 1, 3)
     do_fb(1, 1)
-    ag_last(1)
+    ag_cross(4, 0, 1, 2)
+    ag_cross(4, 1, 1, 2)
+    ag_cross(4, 0, 0, 2)
     do_fh(1)
+    ag_cross(4, 1, 0, 2)
+    ag_cross(4, 0, 1, 3)
     do_pj1(0, 1)
-    do_pj1(0, 0)
-    ag_cross(3, 0, 1, 3)
-    ag_turn(4, 0, 1)
-    ag_cross(3, 0, 1, 2)
     do_at1(0)
-    ag_pass(4, 1, 1)
     do_sb(1)
+    ag_cross(4, 0, 1, 1)
+    do_op1(0)
+    ag_last(3)
+    do_nf1(0)
+    do_fg(1)
+    rs2_m(6, 1)
+    do_gm(1, 0)
     do_gm(1, 1)
-    do_gm(1, 0)
-    ag_pass(4, 0, 2)
-    do_fg(1)
-    do_op1(0)
-    rs2_m(6, 0)
-    rs2_m(6, 1)
-    ag_cross(3, 1, 1, 2)
-    do_ab(1, 0)
-    do_ab(1, 1)
-    do_be(1)
-    ag_turn(4, 0, 2)
-    ag_turn(4, 1, 1)
-    do_nf1(0)
-    ag_cross(3, 1, 1, 3)
-    ag_turn(4, 1, 2)
-    ag_turn(4, 0, 3)
-    do_ag(1)
-    ag_last(3)
     do_fu(0, 0)
     do_fu(0, 1)
+    rs2_m(6, 0)
     do_fu(0, 2)
+    do_fu(0, 3)
     ag_last(4)
-    rs2_m(5, 1)
-    do_fu(0, 3)
     do_fd(0)
-    rs2(2, 0)
-    rs2(2, 1)
     do_n3(0)
-    rs2_m(5, 0)
     do_fb(0, 0)
     do_fb(0, 1)
+    rs2_m(5, 0)
+    do_ab(1, 0)
     do_fh(0)
+    rs2(4, 1)
+    rs2_m(5, 1)
+    do_fg(0)
     do_sb(0)
-    rs3(2, 1)
-    do_fg(0)
+    do_ab(1, 1)
+    rs2(4, 0)
+    do_be(1)
+    do_ag(1)
+    do_gm(0, 0)
+    do_gm(0, 1)
     do_cb(1)
-    do_gm(0, 1)
-    rs3_m(6, 1)
-    do_gm(0, 0)
     do_ab(0, 0)
-    rs2(4, 0)
     do_be(0)
+    rs2_m(3, 1)
     do_cb(0)
-    rs3(2, 0)
+    do_ag(0)
+    rs3(4, 0)
+    rs2_m(3, 0)
+    rs2(2, 0)
     do_gm0(0)
-    do_ag(0)
+    do_gm0(1)
     do_gm0(2)
-    rs2(4, 1)
-    rs2_m(3, 1)
-    rs2_m(3, 0)
-    do_gm0(1)
+    rs3(4, 1)
+    rs2(2, 1)
     do_ab0(0)
     do_ab0(1)
     do_be0(0)
     rs2(1, 0)
+    rs3_m(3, 1)
+    rs3_m(5, 1)
+    rs3_m(5, 0)
+    do_be0(1)
+    rs3(2, 0)
     rs2(1, 1)
-    do_be0(1)
+    rs3(2, 1)
     do_ag0(0)
-    rs3(4, 1)
+    do_ag0(1)
     rs3(1, 1)
+    rs3_m(3, 0)
     rs3_m(6, 0)
-    do_ag0(1)
+    rs3_m(6, 1)
+    rs2(7, 1)
+    held["g", 2] = rs4(2)
+    rs3(1, 0)
+    rs2(7, 0)
+    rs2(0, 0)
+    rs2(0, 1)
+    vec1()
+    held["g", 3] = rs4_m(3)
+    rs3(7, 0)
+    held["g", 4] = rs4(4)
+    do_fin(0)
     held["g", 6] = rs4_m(6)
-    vec1()
-    rs3_m(3, 0)
-    rs3(1, 0)
-    rs3_m(5, 0)
-    rs2(0, 1)
+    rs3(7, 1)
+    held["g", 5] = rs4_m(5)
+    vec2()
+    held["g", 1] = rs4(1)
+    rs3(0, 0)
+    rs3(0, 1)
+    vec3()
     do_fin(1)
-    rs3(4, 0)
-    vec2()
-    rs2(0, 0)
-    rs3_m(5, 1)
-    vec3()
-    do_fin(0)
-    held["g", 2] = rs4(2)
-    rs3(0, 1)
-    rs3(0, 0)
-    held["g", 1] = rs4(1)
-    rs3_m(3, 1)
+    held["g", 7] = rs4(7)
+    held["g", 0] = rs4(0)
     vec4()
-    held["g", 5] = rs4_m(5)
-    held["g", 3] = rs4_m(3)
-    held["g", 4] = rs4(4)
-    held["g", 0] = rs4(0)
     squares()
     for cp in rs_sends:
         cp.wait_send()
@@ -1099,13 +1146,13 @@
         pltpu.VMEM((8, D), F32),
         dma((4,)),
         dma((3,)),
-        dma((NU,)),
+        dma((NU + 1,)),
         dma((26,)),
         dma((26,)),
+        dma((NU, 2, 18)),
         dma((NU, 2, 16)),
-        dma((NU, 2, 16)),
-        dma((NU, 12)),
-        dma((NU, 12)),
+        dma((NU + 1, 12)),
+        dma((NU + 1, 12)),
         dma((6,)),
         dma((6,)),
         dma((10,)),
@@ -1231,8 +1278,8 @@
     out3, gx, g32, vg, sq = fused(
         (lang_in, vis_in, lang_cot, vis_cot, word_lengths, attn_master, ffn_master, vectors)
     )[:5]
-    anywhere = pl.BlockSpec(memory_space=pl.ANY)
     vmem = pl.BlockSpec(memory_space=pltpu.VMEM)
+    hbm = pl.BlockSpec(memory_space=pltpu.HBM)
     like = lambda a, dtype=F32: jax.ShapeDtypeStruct(a.shape, dtype)
     streams, matrices = [lang_in, vis_in] * 2, [attn_master] * 4 + [ffn_master] * 4
     types = [F32, F32, F32, BF16] * 2
@@ -1249,10 +1296,10 @@
         + [like(a, dt) for a, dt in zip(matrices, types)]
         + [like(vectors)] * 3
         + [jax.ShapeDtypeStruct((2, D), F32), jax.ShapeDtypeStruct((8, 128), F32)],
-        in_specs=[vmem] * 5 + [anywhere] * 9,
-        out_specs=[anywhere] * 12 + [vmem] * 5,
+        in_specs=[vmem] * 5 + [hbm] * 9,
+        out_specs=[hbm] * 12 + [vmem] * 5,
         scratch_shapes=scratch,
-        compiler_params=pltpu.CompilerParams(vmem_limit_bytes=48 * 1024 * 1024),
+        compiler_params=pltpu.CompilerParams(vmem_limit_bytes=VMEM_BYTES),
     )(
         vg, sq, vectors, vector_first, vector_second, out3, gx, g32,
         attn_master, attn_first, attn_second, ffn_master, ffn_first, ffn_second,

time: 323 us -> 306 us (0.947)
  Pallas kernels: 311 us -> 299 us
  local copies, waits for them, and re-layouts: 5.93 us -> 1.19 us
    pallas_call x1, Pallas kernels: 304 us -> 288 us  [fused(): pl.pallas_call(kernel, out_shape=[o[0] for o in outs], in_specs=[vmem, vm...]
    unnamed x18 -> x0, local copies, waits for them, and re-layouts: 5.42 us -> none
where the time goes in v3:
time: 306 us; the launch traced here: 301 us
  Pallas kernels  299 us (98%)
    pallas_call x1, Pallas kernels, fused(): pl.pallas_call(kernel, out_shape=[o[0] for o in outs], in_specs=[vmem, vm...  288 us
    pallas_call x1, Pallas kernels, fast_body(): pl.pallas_call(update_kernel, out_shape=[like(a) for a in streams] + [lik...  10.6 us

profile of v3, /device:TPU:0, one launch (start us, length us, event | category | flops | bytes accessed | tf_op | source)
XLA Modules:
  0.0 301.1 jit_solution(4240167155067433359)
XLA Ops:
  0.7 288.5 %shard_map.269 = (f32[512,768]{1,0:T(8,128)}, f32[512,768]{1,0:T(8,128)}, f32[7,96,768]{2,1,0:T(8,128)}, f32[2,32,768]{2,1,0:T(8,128)}, f32[8,128]{1,0:T(8,128)}...) custom-call(bf16[20,8,768]{2,1,0:T(8,128)(2,1)} %bitcast.11, ...), custom_call_target="tpu_custom_call" | custom-call | tf_op jit(solution)/shard_map/pallas_call | solution.py:1162
  289.1 10.6 %shard_map.270 = (f32[20,8,768]{2,1,0:T(8,128)}, f32[36,8,768]{2,1,0:T(8,128)}, f32[20,8,768]{2,1,0:T(8,128)}, f32[36,8,768]{2,1,0:T(8,128)}, f32[3,4,96,192]{3,...) custom-call(f32[2,32,768]{2,1,0:T(8,128)} %get-tuple-element.39.vg, ...), custom_call_target="tpu_custom_call" | custom-call | tf_op jit(solution)/shard_map/pallas_call | solution.py:1293
  299.7 1.2 slice.3

commit v4 on v3

--- a/solution.py
+++ b/solution.py
@@ -31,6 +31,8 @@
 NU = 7
 SEGS = ((0, 0, WO), (WO, WALL, RO))
 CH = 64
+REDUCE = "ZZZMMMMZ"
+SLOTS = 6
 VMEM_BYTES = 62 * 1024 * 1024
 
 
@@ -56,9 +58,9 @@
 
 def kernel(
     lang_in, vis_in, lang_cot, vis_cot, lengths, attn_w, ffn_w, vec,
-    out3, gx, g32, vgo, sqo, ra1, ra2, ra3, rb1, rb2, rb3, rz,
-    W, H, DYA, DYB, Z, XS, YO, YS, YR, Q, K, V, F, PW, PR, A, GP, E, DO, G3, ST, ST3, VG, VR, VZ, SQ, SP, SZ, BIAS,
-    lsem, osem, gsem, cs, cr, ags, agr, rss, rsr, vs, vr, ps, pr,
+    out3, gx, g32, vgo, sqo, ra1, ra2, rb1, rb2, rn, re, rc, rf,
+    W, H, DYA, DYB, Z, XS, YO, YS, YR, Q, K, V, F, PW, PR, A, GP, E, DO, G3, ST, VG, VR, VZ, SQ, SP, SZ, BIAS,
+    lsem, wsem, osem, gsem, cs, cr, ags, agr, rss, rsr, vs, vr, ps, pr,
 ):
     d = lax.axis_index("dp")
     t = lax.axis_index("tensor")
@@ -203,7 +205,7 @@
         YO[o : o + n, :] = terms(r, n)
         return cp
 
-    own_f = [local(ffn_w.at[i // 2, i % 2], Z.at[2, pl.ds(96 * i, 96)], lsem.at[i]) for i in range(4)]
+    own_f = [local(ffn_w.at[i // 2, i % 2], Z.at[2, pl.ds(96 * i, 96)], wsem.at[i]) for i in range(4)]
     for cp in own_f:
         cp.start()
 
@@ -349,7 +351,7 @@
                 attend(1, i, rr, 2 * RP, rr, 2 * RP, mask_rr, PR)
             return carry
 
-        lax.fori_loop(first, last, pair, 0)
+        lax.fori_loop(first, last, pair, 0, unroll=2 if sec == 0 else 4)
 
     def out_project(sec, s, u):
         def terms(r, n):
@@ -517,7 +519,7 @@
                 put_pack(rr, 2 * RP, *attend_back(1, i, rr, 2 * RP, rr, 2 * RP, PR))
             return carry
 
-        lax.fori_loop(first, last, pair, 0)
+        lax.fori_loop(first, last, pair, 0, unroll=2 if sec == 0 else 4)
 
     def branch_back(s, u):
         def terms(r, n):
@@ -566,21 +568,26 @@
     every = slice(None)
 
     def slot(ref, u, *index):
+        if any(ref is r for r in (rn, re, rc)) and not kind_m(u):
+            index = (*index, 0)
         rest = (every,) * (len(ref.shape) - 2 - len(index))
         return ref.at[(real(u), *index, *rest, cols(u))]
 
+    def kind_m(u):
+        return REDUCE[u] == "M"
+
     def stage(u, i):
         return ST.at[i, :, :, here(u)]
 
-    def stage3(u, i):
-        return ST3.at[i, :, :, here(u)]
-
     rs_sends = []
 
-    def rs_send(u, k, src, dst, dev):
-        cp = remote(src, dst, rss.at[u, k], rsr.at[u, k], dev)
-        cp.start()
-        rs_sends.append(cp)
+    def rs_send(u, k, src, dst, dev, when=None, arrives=None):
+        cp = remote(src, dst, rss.at[u, k], rsr.at[u, k if arrives is None else arrives], dev)
+        if when is None:
+            cp.start()
+        else:
+            pl.when(when)(cp.start)
+        rs_sends.append((cp, when))
 
     def rs_recv(u, k, dst):
         remote(dst, dst, rss.at[u, k], rsr.at[u, k], x_n).wait_recv()
@@ -590,12 +597,33 @@
             rs_send(u, k, slab(u, oy, every, xx, top), slot(ra1, u, every, xx), y_n)
             rs_send(u, 2 + k, slab(u, yy, every, ox, bot), slot(rb1, u, yy), x_n)
 
-    def fetch(u, pairs):
-        cps = [local(src, dst, lsem.at[i]) for i, (src, dst) in enumerate(pairs)]
+    free = list(range(SLOTS))
+    fetched = {}
+
+    def fetch(name, copies, when=None):
+        taken, cps = [], []
+        for group in copies:
+            n = free.pop(0)
+            taken.append(n)
+            for k, (src, at_, count) in enumerate(group):
+                dst = ST.at[n, at_, :, here(name[1])] if count == 0 else ST.at[n, pl.ds(at_, count), :, here(name[1])]
+                cp = local(src, dst, lsem.at[n, k])
+                cps.append(cp)
+                if when is None:
+                    cp.start()
+                else:
+                    pl.when(when)(cp.start)
+        fetched[name] = (taken, cps, when)
+
+    def staged(*name):
+        taken, cps, when = fetched.pop(name)
         for cp in cps:
-            cp.start()
-        for cp in cps:
-            cp.wait()
+            if when is None:
+                cp.wait()
+            else:
+                pl.when(when)(cp.wait)
+        free.extend(taken)
+        return taken
 
     def add_in(dst, *stages):
         def step(j, carry):
@@ -610,77 +638,126 @@
     def first_arrival(u, part, q):
         return slot(ra1, u, every, q) if part == 0 else slot(rb1, u, q)
 
-    def rs2_m(u, part):
+    def rs_over_z(u, part, pick):
+        near_dev = at(near, x, y, c)
+        rs_send(u, 6 + part, pick(near), slot(rn, u, part), near_dev)
+        for role, place in ((0, mid), (1, far)):
+            rs_send(u, 8 + 2 * part + role, pick(place), slot(re, u, part, role), near_dev, jnp.logical_not(inner))
+
+    def rs_relay(u, part, pick):
+        for role, place in ((0, mid), (1, far)):
+            dev = at(place, x, y, c)
+            rs_send(u, (12, 14)[role] + part, pick(place), slot(rc, u, part), dev, inner, 12 + part)
+
+    def picker(u, part):
+        if kind_m(u):
+            return lambda place: slab(u, y, place, every, top) if part == 0 else slab(u, every, place, x, bot)
+        return lambda place: slab(u, y, place, x, rows_of[part])
+
+    def f5(u, part):
+        def waits():
+            for role in (0, 1):
+                rs_recv(u, 8 + 2 * part + role, slot(re, u, part, role))
+
+        pl.when(inner)(waits)
+        n = 2 if kind_m(u) else 0
+        fetch(("5", u, part), [[(slot(re, u, part, role), 2 * role, n) for role in (0, 1)]], inner)
+
+    def rs5(u, part):
+        (n,) = staged("5", u, part)
+
+        def add():
+            for role, place in ((0, mid), (1, far)):
+                for q in range(2 if kind_m(u) else 1):
+                    if kind_m(u):
+                        ref = slab(u, y, place, q, top) if part == 0 else slab(u, q, place, x, bot)
+                    else:
+                        ref = slab(u, y, place, x, rows_of[part])
+                    ref[...] = (ref[...].astype(F32) + ST[n, 2 * role + q, :, here(u)].astype(F32)).astype(BF16)
+
+        pl.when(inner)(add)
+        rs_relay(u, part, picker(u, part))
+
+    def f2_m(u, part):
         for q in (0, 1):
             rs_recv(u, 2 * part + q, first_arrival(u, part, ((ox, x), (oy, y))[part][q]))
-        fetch(u, [(first_arrival(u, part, q), stage(u, q)) for q in (0, 1)])
-        for q in (0, 1):
-            add_in(lambda j: slab(u, y, j, q, top) if part == 0 else slab(u, q, j, x, bot), stage(u, q))
-        for k in (1, 3, 2):
-            src = slab(u, y, zk[k], every, top) if part == 0 else slab(u, every, zk[k], x, bot)
-            rs_send(u, 5 + 3 * part + k, src, slot(rz, u, part, k - 1), z_n[k])
+        fetch(("2", u, part), [[(first_arrival(u, part, q), 0, 4)] for q in (0, 1)])
+
+    def rs2_m(u, part):
+        for q, n in enumerate(staged("2", u, part)):
+            add_in(lambda j: slab(u, y, j, q, top) if part == 0 else slab(u, q, j, x, bot), stage(u, n))
+        rs_over_z(u, part, picker(u, part))
+
+    def f3_m(u, part):
+        rs_recv(u, 6 + part, slot(rn, u, part))
+        rs_recv(u, 12 + part, slot(rc, u, part))
+        fetch(("3", u, part), [[(slot(rn, u, part), 0, 2), (slot(rc, u, part), 2, 2)]])
 
     def rs3_m(u, part):
-        for k in (1, 3, 2):
-            rs_recv(u, 5 + 3 * part + k, slot(rz, u, part, k - 1))
-        fetch(u, [(slot(rz, u, part, every, q), stage3(u, q)) for q in (0, 1)])
+        (n,) = staged("3", u, part)
 
         def total(ref, q):
-            g = ref[...].astype(F32)
-            for k in range(3):
-                g = g + ST3[q, k, :, here(u)].astype(F32)
-            return g
+            return ref[...].astype(F32) + ST[n, q, :, here(u)].astype(F32) + ST[n, 2 + q, :, here(u)].astype(F32)
 
         rows = rows_of[part]
-        other, q, dst, dev = ((slab(u, y, z, ox, rows), ox, ra3, x_n), (slab(u, oy, z, x, rows), oy, rb3, y_n))[part]
+        other, q, dev = ((slab(u, y, z, ox, rows), ox, x_n), (slab(u, oy, z, x, rows), oy, y_n))[part]
         other[...] = total(other, q).astype(BF16)
-        rs_send(u, 4 + part, other, slot(dst, u, 0), dev)
+        rs_send(u, 4 + part, other, slot(rf, u, part), dev)
         G3[real(u), rows, cols(u)] = total(slab(u, y, z, x, rows), (x, y)[part])
 
+    def f4_m(u):
+        for part in (0, 1):
+            rs_recv(u, 4 + part, slot(rf, u, part))
+        fetch(("4", u), [[(slot(rf, u, part), part, 0) for part in (0, 1)]])
+
     def rs4_m(u):
-        for part, dst in ((0, ra3), (1, rb3)):
-            rs_recv(u, 4 + part, slot(dst, u, 0))
-        fetch(u, [(slot(dst, u, 0), ST3.at[part, 0, :, here(u)]) for part, dst in ((0, ra3), (1, rb3))])
         return rs_end(u, 1)
 
+    def f2(u, part):
+        src = first_arrival(u, part, (ox, oy)[part])
+        rs_recv(u, 2 * part, src)
+        fetch(("2", u, part), [[(src, 0, 4)]])
+
     def rs2(u, part):
-        q = (ox, oy)[part]
-        src = first_arrival(u, part, q)
-        rs_recv(u, 2 * part, src)
-        fetch(u, [(src, stage(u, part))])
+        (n,) = staged("2", u, part)
         if part == 0:
-            add_in(lambda j: slab(u, y, j, ox, top), stage(u, 0))
+            add_in(lambda j: slab(u, y, j, ox, top), stage(u, n))
             rs_send(u, 4, slab(u, y, every, ox, top), slot(ra2, u), x_n)
         else:
-            add_in(lambda j: slab(u, oy, j, x, bot), stage(u, 1))
+            add_in(lambda j: slab(u, oy, j, x, bot), stage(u, n))
             rs_send(u, 5, slab(u, oy, every, x, bot), slot(rb2, u), y_n)
 
-    def rs3(u, part):
+    def f3(u, part):
         sources = (first_arrival(u, part, (x, y)[part]), slot((ra2, rb2)[part], u))
         for k, src in zip((2 * part + 1, 4 + part), sources):
             rs_recv(u, k, src)
-        fetch(u, [(src, stage(u, 2 + i)) for i, src in enumerate(sources)])
+        fetch(("3", u, part), [[(src, 0, 4)] for src in sources])
+
+    def rs3(u, part):
+        a, b = staged("3", u, part)
         rows = rows_of[part]
         own = slab(u, y, z, x, rows)[...].astype(F32)
-        for i in (2, 3):
-            own = own + ST[i, z, :, here(u)].astype(F32)
-        add_in(lambda j: slab(u, y, j, x, rows), stage(u, 2), stage(u, 3))
+        for n in (a, b):
+            own = own + ST[n, z, :, here(u)].astype(F32)
+        add_in(lambda j: slab(u, y, j, x, rows), stage(u, a), stage(u, b))
         G3[real(u), rows, cols(u)] = own
-        for k in (1, 3, 2):
-            rs_send(u, 5 + 3 * part + k, slab(u, y, zk[k], x, rows), slot((ra3, rb3)[part], u, k - 1), z_n[k])
+        rs_over_z(u, part, picker(u, part))
+
+    def f4(u):
+        for part in (0, 1):
+            rs_recv(u, 6 + part, slot(rn, u, part))
+            rs_recv(u, 12 + part, slot(rc, u, part))
+        fetch(("4", u), [[(slot(ref, u, part), 2 * part + k, 0) for part in (0, 1) for k, ref in enumerate((rn, rc))]])
 
     def rs4(u):
-        for part, dst in ((0, ra3), (1, rb3)):
-            for k in (1, 3, 2):
-                rs_recv(u, 5 + 3 * part + k, slot(dst, u, k - 1))
-        fetch(u, [(slot(dst, u), stage3(u, part)) for part, dst in ((0, ra3), (1, rb3))])
-        return rs_end(u, 3)
+        return rs_end(u, 2)
 
     def rs_end(u, terms):
+        (n,) = staged("4", u)
         for part in (0, 1):
             g = G3[real(u), rows_of[part], cols(u)]
             for k in range(terms):
-                g = g + ST3[part, k, :, here(u)].astype(F32)
+                g = g + ST[n, part * terms + k, :, here(u)].astype(F32)
             G3[real(u), rows_of[part], cols(u)] = g
             SQ[:, cols(u)] += jnp.sum((g * g).reshape(6, 8, g.shape[1]), axis=0)
         cp = local(G3.at[real(u), :, cols(u)], g32.at[real(u), :, cols(u)], gsem.at[u])
@@ -860,236 +937,311 @@
 
     own_weights(0)
     ag_first(0)
-    own_weights(5)
     own_weights(6)
     own_weights(2)
-    ag_first(2)
+    ag_first_m(2)
+    own_weights(5)
+    ag_first_m(5)
+    ag_spread(5, 1)
+    ag_pass(0, 1, 1)
+    ag_pass(0, 1, 2)
     own_weights(3)
-    ag_first_m(5)
+    ag_pass(0, 0, 2)
+    ag_spread(5, 0)
+    ag_turn(0, 0, 0)
+    ag_spread(2, 0)
+    own_weights(4)
+    ag_turn(0, 1, 0)
+    ag_turn(0, 1, 1)
+    ag_pass(0, 0, 1)
+    ag_first_m(6)
+    own_weights(1)
+    ag_cross(2, 1, 0, 2)
+    ag_spread(2, 1)
+    ag_cross(2, 1, 0, 3)
+    ag_cross(2, 0, 0, 1)
     load_input()
-    ag_first_m(6)
+    ag_cross(5, 1, 1, 1)
+    ag_cross(2, 1, 0, 1)
+    ag_first(1)
+    ag_pass(0, 1, 3)
+    ag_cross(2, 0, 1, 1)
+    ag_spread(6, 0)
+    ag_cross(2, 0, 1, 2)
+    ag_first_m(3)
     ag_pass(0, 0, 3)
-    ag_spread(5, 0)
-    ag_pass(0, 0, 2)
-    ag_spread(6, 0)
-    ag_turn(0, 0, 0)
-    own_weights(1)
+    ag_cross(6, 1, 0, 2)
+    ag_cross(2, 0, 0, 2)
+    ag_cross(5, 1, 1, 2)
+    ag_turn(0, 0, 1)
+    ag_cross(5, 0, 0, 3)
+    ag_turn(0, 0, 2)
     ag_spread(6, 1)
-    ag_pass(2, 1, 2)
+    ag_turn(0, 1, 3)
     ag_turn(0, 0, 3)
-    ag_pass(2, 0, 2)
-    ag_spread(5, 1)
-    ag_pass(0, 0, 1)
-    ag_pass(2, 1, 1)
-    ag_pass(2, 1, 3)
-    ag_pass(0, 1, 2)
-    ag_turn(0, 1, 0)
-    own_weights(4)
-    ag_pass(0, 1, 3)
-    ag_first_m(1)
-    ag_pass(0, 1, 1)
-    ag_turn(2, 1, 2)
+    ag_turn(0, 1, 2)
+    ag_cross(5, 0, 1, 3)
+    ag_spread(3, 0)
     ag_cross(5, 1, 0, 3)
-    ag_cross(6, 0, 0, 1)
-    ag_turn(0, 1, 2)
-    ag_first_m(3)
-    ag_turn(0, 1, 3)
-    ag_turn(0, 0, 2)
-    ag_turn(0, 1, 1)
-    ag_pass(2, 0, 1)
-    ag_turn(0, 0, 1)
-    ag_pass(2, 0, 3)
-    ag_cross(5, 1, 0, 1)
-    ag_cross(5, 1, 1, 1)
+    ag_spread(3, 1)
+    ag_cross(6, 1, 0, 1)
     ag_cross(5, 0, 0, 2)
-    ag_spread(1, 0)
-    ag_cross(1, 0, 0, 2)
-    ag_spread(3, 1)
-    ag_turn(2, 0, 0)
-    ag_cross(5, 0, 1, 2)
-    ag_cross(6, 1, 0, 1)
-    ag_cross(6, 1, 0, 2)
-    ag_spread(3, 0)
     ag_last(0)
-    do_pj0(1)
-    ag_first_m(4)
-    ag_turn(2, 0, 2)
-    ag_turn(2, 1, 1)
-    ag_cross(5, 0, 0, 3)
-    ag_turn(2, 0, 1)
-    ag_turn(2, 0, 3)
+    ag_cross(2, 0, 0, 3)
+    do_pj0(0)
+    ag_cross(6, 0, 1, 1)
+    ag_cross(2, 1, 1, 2)
+    ag_cross(5, 1, 1, 3)
+    ag_pass(1, 0, 3)
+    ag_pass(1, 1, 1)
+    ag_pass(1, 0, 1)
+    ag_cross(5, 0, 1, 1)
     do_pj0(2)
-    do_pj0(0)
-    ag_cross(5, 0, 1, 3)
-    ag_cross(6, 1, 1, 3)
-    ag_turn(2, 1, 0)
-    ag_turn(2, 1, 3)
-    ag_cross(1, 1, 0, 2)
-    do_at0(0)
-    ag_cross(5, 0, 0, 1)
-    ag_cross(3, 0, 0, 3)
-    do_at0(1)
-    ag_cross(5, 1, 0, 2)
-    ag_cross(5, 0, 1, 1)
-    ag_cross(3, 1, 0, 2)
-    ag_cross(1, 1, 0, 3)
-    do_op0(1)
-    ag_cross(6, 0, 1, 2)
-    ag_cross(6, 0, 1, 1)
     ag_cross(6, 1, 1, 1)
-    ag_spread(1, 1)
-    ag_cross(4, 0, 0, 1)
-    ag_cross(3, 1, 1, 1)
-    do_nf0(1)
     ag_cross(3, 0, 0, 2)
     ag_cross(6, 0, 0, 3)
-    ag_cross(1, 0, 1, 1)
+    ag_cross(5, 1, 0, 1)
+    do_pj0(1)
+    ag_cross(2, 0, 1, 3)
+    do_at0(0)
+    ag_cross(2, 1, 1, 1)
+    ag_cross(6, 0, 0, 1)
+    ag_first_m(4)
+    ag_pass(1, 0, 2)
+    ag_turn(1, 0, 3)
+    do_at0(1)
+    ag_cross(2, 1, 1, 3)
+    ag_cross(6, 1, 0, 3)
+    ag_turn(1, 0, 1)
+    do_op0(1)
+    ag_spread(4, 0)
+    do_nf0(1)
+    ag_cross(5, 0, 1, 2)
+    ag_cross(6, 1, 1, 3)
+    ag_cross(5, 0, 0, 1)
+    ag_cross(5, 1, 0, 2)
     ag_last(2)
+    ag_cross(4, 0, 0, 1)
+    do_pj1(1, 1)
+    ag_cross(6, 0, 1, 3)
     do_pj1(1, 0)
-    ag_cross(5, 1, 1, 2)
-    ag_cross(5, 1, 1, 3)
-    do_pj1(1, 1)
+    ag_turn(1, 1, 0)
     do_at1(1)
-    ag_cross(3, 1, 1, 2)
+    ag_pass(1, 1, 3)
+    do_op1(1)
+    do_op0(0)
+    ag_cross(4, 1, 0, 1)
+    ag_cross(6, 0, 1, 2)
+    ag_turn(1, 0, 2)
     ag_cross(3, 1, 0, 1)
-    ag_cross(6, 1, 0, 3)
-    ag_cross(1, 0, 1, 3)
-    do_op1(1)
-    ag_cross(1, 1, 1, 3)
+    ag_cross(6, 0, 0, 2)
     do_nf1(1)
+    ag_cross(6, 1, 1, 2)
+    ag_turn(1, 0, 0)
+    ag_pass(1, 1, 2)
+    ag_cross(3, 0, 1, 1)
+    ag_cross(3, 0, 0, 1)
     ag_spread(4, 1)
-    ag_cross(6, 1, 1, 2)
-    ag_cross(6, 0, 0, 2)
-    do_op0(0)
     ag_last(5)
-    ag_cross(1, 1, 0, 1)
-    ag_spread(4, 0)
-    ag_cross(3, 0, 0, 1)
     do_fu(1, 0)
+    ag_cross(4, 0, 1, 2)
+    ag_cross(3, 1, 1, 1)
     do_fu(1, 1)
-    ag_cross(4, 1, 0, 1)
-    ag_cross(6, 0, 1, 3)
-    ag_cross(1, 0, 1, 2)
-    ag_cross(1, 1, 1, 1)
     do_fu(1, 2)
+    ag_cross(3, 1, 0, 2)
+    ag_cross(3, 1, 0, 3)
     do_fu(1, 3)
+    ag_last(6)
+    ag_cross(4, 1, 0, 2)
+    ag_cross(4, 0, 1, 1)
+    do_fd(1)
+    ag_cross(3, 0, 1, 3)
+    ag_turn(1, 1, 2)
+    ag_cross(3, 1, 1, 3)
+    ag_turn(1, 1, 3)
+    ag_cross(4, 0, 0, 3)
+    ag_turn(1, 1, 1)
+    do_n3(1)
+    ag_cross(4, 1, 0, 3)
     ag_cross(3, 0, 1, 2)
-    ag_cross(3, 0, 1, 1)
-    ag_cross(1, 1, 1, 2)
-    ag_last(6)
-    do_fd(1)
-    do_nf0(0)
-    ag_cross(1, 0, 0, 1)
-    ag_cross(4, 1, 0, 3)
-    ag_cross(4, 1, 1, 3)
-    ag_cross(1, 0, 0, 3)
-    do_n3(1)
-    ag_cross(3, 1, 1, 3)
-    ag_cross(3, 0, 1, 3)
-    ag_cross(4, 0, 0, 3)
+    ag_cross(4, 0, 1, 3)
+    ag_cross(4, 1, 1, 2)
     ag_cross(4, 1, 1, 1)
-    ag_last(1)
-    ag_cross(3, 1, 0, 3)
-    do_pj1(0, 0)
     do_fb(1, 0)
     do_fb(1, 1)
-    ag_cross(4, 0, 1, 2)
-    ag_cross(4, 1, 1, 2)
+    ag_cross(3, 1, 1, 2)
+    do_fh(1)
+    ag_cross(3, 0, 0, 3)
+    ag_cross(4, 1, 1, 3)
+    ag_last(1)
+    do_fg(1)
     ag_cross(4, 0, 0, 2)
-    do_fh(1)
-    ag_cross(4, 1, 0, 2)
-    ag_cross(4, 0, 1, 3)
-    do_pj1(0, 1)
-    do_at1(0)
+    do_nf0(0)
     do_sb(1)
-    ag_cross(4, 0, 1, 1)
-    do_op1(0)
-    ag_last(3)
-    do_nf1(0)
-    do_fg(1)
-    rs2_m(6, 1)
     do_gm(1, 0)
     do_gm(1, 1)
+    do_ab(1, 0)
+    do_pj1(0, 0)
+    f2_m(6, 1)
+    do_pj1(0, 1)
+    rs2_m(6, 1)
+    do_at1(0)
+    do_op1(0)
+    f2_m(6, 0)
+    do_ab(1, 1)
+    do_be(1)
+    rs2_m(6, 0)
+    do_nf1(0)
+    do_ag(1)
+    ag_last(3)
     do_fu(0, 0)
     do_fu(0, 1)
-    rs2_m(6, 0)
+    ag_last(4)
+    f2_m(5, 1)
     do_fu(0, 2)
     do_fu(0, 3)
-    ag_last(4)
     do_fd(0)
+    rs2_m(5, 1)
+    f2(2, 1)
+    f2_m(5, 0)
     do_n3(0)
+    f2(2, 0)
+    rs2(2, 1)
+    rs2_m(5, 0)
+    rs2(2, 0)
+    do_cb(1)
     do_fb(0, 0)
     do_fb(0, 1)
-    rs2_m(5, 0)
-    do_ab(1, 0)
     do_fh(0)
-    rs2(4, 1)
-    rs2_m(5, 1)
     do_fg(0)
     do_sb(0)
-    do_ab(1, 1)
-    rs2(4, 0)
-    do_be(1)
-    do_ag(1)
+    f5(6, 1)
+    rs5(6, 1)
+    f5(5, 1)
+    f3(2, 1)
+    f3(2, 0)
     do_gm(0, 0)
     do_gm(0, 1)
-    do_cb(1)
+    rs3(2, 0)
     do_ab(0, 0)
+    rs3(2, 1)
     do_be(0)
+    do_ag(0)
+    f5(5, 0)
+    f2_m(4, 1)
+    rs5(5, 1)
+    f5(6, 0)
+    do_cb(0)
+    rs5(6, 0)
+    f2_m(4, 0)
+    rs2_m(4, 1)
+    rs5(5, 0)
+    do_gm0(1)
+    rs2_m(4, 0)
+    do_gm0(0)
+    do_gm0(2)
+    do_ab0(0)
+    f5(2, 1)
+    f2_m(3, 0)
+    do_ab0(1)
+    f2(1, 1)
+    rs2_m(3, 0)
+    f3_m(6, 1)
+    f2(1, 0)
+    f5(2, 0)
+    f5(4, 1)
+    rs2(1, 1)
+    rs5(2, 1)
+    f2_m(3, 1)
+    rs2(1, 0)
+    rs5(4, 1)
+    do_be0(1)
+    do_be0(0)
+    do_ag0(0)
+    rs5(2, 0)
+    do_ag0(1)
     rs2_m(3, 1)
-    do_cb(0)
-    do_ag(0)
-    rs3(4, 0)
-    rs2_m(3, 0)
-    rs2(2, 0)
-    do_gm0(0)
-    do_gm0(1)
-    do_gm0(2)
-    rs3(4, 1)
-    rs2(2, 1)
-    do_ab0(0)
-    do_ab0(1)
-    do_be0(0)
-    rs2(1, 0)
-    rs3_m(3, 1)
+    f3(1, 0)
+    rs3(1, 0)
+    f3_m(5, 0)
+    rs3_m(5, 0)
+    f2(0, 1)
+    f5(4, 0)
+    rs3_m(6, 1)
+    f3_m(5, 1)
+    f3(1, 1)
+    f2(0, 0)
+    rs5(4, 0)
+    rs2(0, 0)
     rs3_m(5, 1)
-    rs3_m(5, 0)
-    do_be0(1)
-    rs3(2, 0)
-    rs2(1, 1)
-    rs3(2, 1)
-    do_ag0(0)
-    do_ag0(1)
+    f2(7, 0)
+    f5(3, 0)
+    f3_m(6, 0)
+    rs5(3, 0)
+    rs3_m(6, 0)
+    rs2(7, 0)
+    vec1()
+    f3_m(4, 1)
+    do_fin(0)
     rs3(1, 1)
-    rs3_m(3, 0)
-    rs3_m(6, 0)
-    rs3_m(6, 1)
+    f2(7, 1)
     rs2(7, 1)
-    held["g", 2] = rs4(2)
-    rs3(1, 0)
-    rs2(7, 0)
-    rs2(0, 0)
-    rs2(0, 1)
-    vec1()
-    held["g", 3] = rs4_m(3)
-    rs3(7, 0)
-    held["g", 4] = rs4(4)
-    do_fin(0)
-    held["g", 6] = rs4_m(6)
-    rs3(7, 1)
+    f5(3, 1)
+    f3(0, 0)
+    f4_m(5)
+    rs5(3, 1)
+    f3_m(4, 0)
     held["g", 5] = rs4_m(5)
     vec2()
+    f4_m(6)
+    rs3(0, 0)
+    do_fin(1)
+    f3(7, 1)
+    rs2(0, 1)
+    f5(1, 0)
+    rs3(7, 1)
+    rs3_m(4, 0)
+    rs5(1, 0)
+    f5(1, 1)
+    vec3()
+    f5(0, 0)
+    rs5(1, 1)
+    f3(7, 0)
+    rs5(0, 0)
+    f3(0, 1)
+    rs3(0, 1)
+    held["g", 6] = rs4_m(6)
+    rs3_m(4, 1)
+    f3_m(3, 1)
+    f5(7, 1)
+    rs3(7, 0)
+    f4(1)
+    rs5(7, 1)
+    f5(0, 1)
+    rs5(0, 1)
+    rs3_m(3, 1)
+    f4(2)
     held["g", 1] = rs4(1)
-    rs3(0, 0)
-    rs3(0, 1)
-    vec3()
-    do_fin(1)
+    f3_m(3, 0)
+    f5(7, 0)
+    rs5(7, 0)
+    rs3_m(3, 0)
+    f4(0)
+    vec4()
+    held["g", 2] = rs4(2)
+    f4_m(4)
+    f4_m(3)
+    f4(7)
+    held["g", 0] = rs4(0)
+    held["g", 4] = rs4_m(4)
+    held["g", 3] = rs4_m(3)
     held["g", 7] = rs4(7)
-    held["g", 0] = rs4(0)
-    vec4()
     squares()
-    for cp in rs_sends:
-        cp.wait_send()
+    for cp, when in rs_sends:
+        if when is None:
+            cp.wait_send()
+        else:
+            pl.when(when)(cp.wait_send)
     pending.pop().wait()
     for name in list(held):
         got(name)
@@ -1108,11 +1260,12 @@
         (s((8, 128), F32), vmem),
         (s((NU, 4, 2, 48, D), BF16), anywhere),
         (s((NU, 4, 48, D), BF16), anywhere),
-        (s((NU, 3, 48, D), BF16), anywhere),
         (s((NU, 2, 4, 48, D), BF16), anywhere),
         (s((NU, 4, 48, D), BF16), anywhere),
-        (s((NU, 3, 48, D), BF16), anywhere),
-        (s((NU, 2, 3, 2, 48, D), BF16), anywhere),
+        (s((NU, 2, 2, 48, D), BF16), anywhere),
+        (s((NU, 2, 2, 2, 48, D), BF16), anywhere),
+        (s((NU, 2, 2, 48, D), BF16), anywhere),
+        (s((NU, 2, 48, D), BF16), anywhere),
     ]
     scratch = [
         pltpu.VMEM((NU, 2, 4, 2, 96, D), BF16),
@@ -1135,8 +1288,7 @@
         pltpu.VMEM((2, ALL, 640), BF16),
         pltpu.VMEM((1, ALL, 384), BF16),
         pltpu.VMEM((NU, 96, D), F32),
-        pltpu.VMEM((4, 4, 48, D), BF16),
-        pltpu.VMEM((2, 3, 48, D), BF16),
+        pltpu.VMEM((SLOTS, 4, 48, D), BF16),
         pltpu.VMEM((32, D), F32),
         pltpu.VMEM((4, 32, D), F32),
         pltpu.VMEM((4, 32, D), F32),
@@ -1144,6 +1296,7 @@
         pltpu.VMEM((8, 8, 128), F32),
         pltpu.VMEM((4, 8, 128), F32),
         pltpu.VMEM((8, D), F32),
+        dma((SLOTS, 4)),
         dma((4,)),
         dma((3,)),
         dma((NU + 1,)),
@@ -1151,8 +1304,8 @@
         dma((26,)),
         dma((NU, 2, 18)),
         dma((NU, 2, 16)),
-        dma((NU + 1, 12)),
-        dma((NU + 1, 12)),
+        dma((NU + 1, 16)),
+        dma((NU + 1, 16)),
         dma((6,)),
         dma((6,)),
         dma((10,)),
@@ -1218,7 +1371,7 @@
     squares = jnp.sum(jnp.sum(total * total, axis=1, keepdims=True), axis=0, keepdims=True) + sq[0:1, 0:1]
     norm = jnp.sqrt(squares)
     clip = CLIP_NORM / jnp.maximum(norm, CLIP_NORM)
-    norm_o[...] = jnp.broadcast_to(norm, (8, 128))
+    norm_o[0, 0] = jnp.sum(norm)
     clipped = total * clip
     bias_o[...] = clipped[19:21, :]
     vec_o[...], vec_mo[...], vec_vo[...] = adam_update(vec[...], vec_m[...], vec_v[...], clipped, RATE_VECTOR)
@@ -1295,16 +1448,16 @@
         out_shape=[like(a) for a in streams]
         + [like(a, dt) for a, dt in zip(matrices, types)]
         + [like(vectors)] * 3
-        + [jax.ShapeDtypeStruct((2, D), F32), jax.ShapeDtypeStruct((8, 128), F32)],
+        + [jax.ShapeDtypeStruct((2, D), F32), jax.ShapeDtypeStruct((1, 1), F32)],
         in_specs=[vmem] * 5 + [hbm] * 9,
-        out_specs=[hbm] * 12 + [vmem] * 5,
+        out_specs=[hbm] * 12 + [vmem] * 4 + [pl.BlockSpec(memory_space=pltpu.SMEM)],
         scratch_shapes=scratch,
         compiler_params=pltpu.CompilerParams(vmem_limit_bytes=VMEM_BYTES),
     )(
         vg, sq, vectors, vector_first, vector_second, out3, gx, g32,
         attn_master, attn_first, attn_second, ffn_master, ffn_first, ffn_second,
     )
-    return (*(a.swapaxes(0, 1) for a in outs[:4]), *outs[4:16], outs[16][0, 0])
+    return (*(a.swapaxes(0, 1) for a in outs[:4]), *outs[4:16], outs[16].reshape(()))
 
 
 def normalize(inputs, norm_gain, norm_shift):

time: 306 us -> 290 us (0.948)
  Pallas kernels: 299 us -> 285 us
    pallas_call x1, Pallas kernels: 288 us -> 274 us  [fused(): pl.pallas_call(kernel, out_shape=[o[0] for o in outs], in_specs=[vmem, vm...]
where the time goes in v4:
time: 290 us; the launch traced here: 286 us
  Pallas kernels  285 us (98%)
    pallas_call x1, Pallas kernels, fused(): pl.pallas_call(kernel, out_shape=[o[0] for o in outs], in_specs=[vmem, vm...  274 us
    pallas_call x1, Pallas kernels, fast_body(): pl.pallas_call(update_kernel, out_shape=[like(a) for a in streams] + [lik...  10.6 us

profile of v4, /device:TPU:0, one launch (start us, length us, event | category | flops | bytes accessed | tf_op | source)
XLA Modules:
  0.0 285.5 jit_solution(3663043615652913475)
XLA Ops:
  0.7 274.0 %shard_map.269 = (f32[512,768]{1,0:T(8,128)}, f32[512,768]{1,0:T(8,128)}, f32[7,96,768]{2,1,0:T(8,128)}, f32[2,32,768]{2,1,0:T(8,128)}, f32[8,128]{1,0:T(8,128)}...) custom-call(bf16[20,8,768]{2,1,0:T(8,128)(2,1)} %bitcast.11, ...), custom_call_target="tpu_custom_call" | custom-call | tf_op jit(solution)/shard_map/pallas_call | solution.py:1315
  274.6 10.6 %shard_map.270 = (f32[20,8,768]{2,1,0:T(8,128)}, f32[36,8,768]{2,1,0:T(8,128)}, f32[20,8,768]{2,1,0:T(8,128)}, f32[36,8,768]{2,1,0:T(8,128)}, f32[3,4,96,192]{3,...) custom-call(f32[2,32,768]{2,1,0:T(8,128)} %get-tuple-element.39.vg, ...), custom_call_target="tpu_custom_call" | custom-call | tf_op jit(solution)/shard_map/pallas_call | solution.py:1446

commit v5 on v4

--- a/solution.py
+++ b/solution.py
@@ -937,304 +937,304 @@
 
     own_weights(0)
     ag_first(0)
+    own_weights(5)
+    own_weights(2)
+    load_input()
+    ag_first_m(2)
+    ag_turn(0, 0, 0)
+    ag_first_m(5)
+    ag_pass(0, 1, 1)
+    ag_turn(0, 1, 0)
     own_weights(6)
-    own_weights(2)
-    ag_first_m(2)
-    own_weights(5)
-    ag_first_m(5)
+    ag_pass(0, 0, 2)
+    own_weights(1)
+    ag_pass(0, 1, 2)
+    ag_pass(0, 0, 3)
     ag_spread(5, 1)
-    ag_pass(0, 1, 1)
-    ag_pass(0, 1, 2)
+    ag_pass(0, 0, 1)
+    ag_spread(2, 0)
+    ag_pass(0, 1, 3)
+    ag_spread(2, 1)
+    ag_turn(0, 1, 2)
+    ag_turn(0, 0, 3)
+    ag_cross(2, 0, 0, 2)
+    ag_cross(2, 1, 0, 2)
+    ag_turn(0, 0, 2)
+    own_weights(4)
+    ag_turn(0, 1, 1)
+    ag_cross(2, 0, 0, 1)
+    ag_cross(5, 0, 0, 3)
+    ag_turn(0, 1, 3)
+    ag_turn(0, 0, 1)
+    ag_spread(5, 0)
+    ag_first_m(6)
+    ag_first(1)
+    ag_cross(2, 1, 1, 2)
     own_weights(3)
-    ag_pass(0, 0, 2)
-    ag_spread(5, 0)
-    ag_turn(0, 0, 0)
-    ag_spread(2, 0)
-    own_weights(4)
-    ag_turn(0, 1, 0)
-    ag_turn(0, 1, 1)
-    ag_pass(0, 0, 1)
-    ag_first_m(6)
-    own_weights(1)
-    ag_cross(2, 1, 0, 2)
-    ag_spread(2, 1)
+    ag_cross(2, 1, 0, 1)
+    ag_cross(2, 0, 1, 1)
+    ag_cross(5, 1, 0, 2)
+    ag_cross(2, 0, 0, 3)
+    ag_last(0)
+    ag_cross(5, 0, 1, 1)
+    do_pj0(1)
+    ag_cross(2, 0, 1, 2)
+    ag_cross(6, 0, 0, 1)
+    ag_cross(5, 1, 0, 1)
     ag_cross(2, 1, 0, 3)
-    ag_cross(2, 0, 0, 1)
-    load_input()
+    ag_cross(5, 0, 1, 2)
+    do_pj0(0)
+    ag_cross(5, 0, 0, 1)
+    ag_cross(2, 1, 1, 1)
+    ag_cross(2, 0, 1, 3)
     ag_cross(5, 1, 1, 1)
-    ag_cross(2, 1, 0, 1)
-    ag_first(1)
-    ag_pass(0, 1, 3)
-    ag_cross(2, 0, 1, 1)
+    ag_first_m(3)
+    do_pj0(2)
+    do_at0(0)
+    ag_cross(6, 1, 0, 1)
+    ag_cross(6, 1, 0, 3)
+    ag_pass(1, 1, 1)
+    ag_cross(2, 1, 1, 3)
+    ag_spread(6, 1)
+    do_at0(1)
+    ag_pass(1, 0, 1)
+    do_op0(1)
     ag_spread(6, 0)
-    ag_cross(2, 0, 1, 2)
-    ag_first_m(3)
-    ag_pass(0, 0, 3)
+    ag_cross(5, 1, 1, 3)
+    ag_cross(3, 0, 0, 1)
+    ag_cross(5, 1, 0, 3)
+    do_nf0(1)
+    ag_pass(1, 1, 3)
+    ag_cross(5, 1, 1, 2)
+    ag_last(2)
+    ag_cross(5, 0, 0, 2)
+    do_pj1(1, 1)
+    ag_spread(3, 0)
+    do_pj1(1, 0)
+    ag_turn(1, 0, 1)
+    ag_cross(5, 0, 1, 3)
+    ag_turn(1, 1, 1)
+    ag_turn(1, 1, 0)
+    ag_spread(3, 1)
+    do_at1(1)
+    ag_cross(6, 0, 1, 1)
+    ag_cross(6, 0, 1, 3)
+    ag_turn(1, 1, 3)
+    do_op1(1)
+    ag_cross(6, 0, 0, 3)
+    ag_cross(6, 0, 1, 2)
+    ag_cross(6, 1, 1, 1)
+    do_nf1(1)
+    ag_cross(6, 0, 0, 2)
+    ag_last(5)
+    ag_turn(1, 0, 0)
+    ag_cross(3, 0, 1, 1)
+    ag_cross(6, 1, 1, 3)
+    do_fu(1, 0)
     ag_cross(6, 1, 0, 2)
-    ag_cross(2, 0, 0, 2)
-    ag_cross(5, 1, 1, 2)
-    ag_turn(0, 0, 1)
-    ag_cross(5, 0, 0, 3)
-    ag_turn(0, 0, 2)
-    ag_spread(6, 1)
-    ag_turn(0, 1, 3)
-    ag_turn(0, 0, 3)
-    ag_turn(0, 1, 2)
-    ag_cross(5, 0, 1, 3)
-    ag_spread(3, 0)
-    ag_cross(5, 1, 0, 3)
-    ag_spread(3, 1)
-    ag_cross(6, 1, 0, 1)
-    ag_cross(5, 0, 0, 2)
-    ag_last(0)
-    ag_cross(2, 0, 0, 3)
-    do_pj0(0)
-    ag_cross(6, 0, 1, 1)
-    ag_cross(2, 1, 1, 2)
-    ag_cross(5, 1, 1, 3)
-    ag_pass(1, 0, 3)
-    ag_pass(1, 1, 1)
-    ag_pass(1, 0, 1)
-    ag_cross(5, 0, 1, 1)
-    do_pj0(2)
-    ag_cross(6, 1, 1, 1)
-    ag_cross(3, 0, 0, 2)
-    ag_cross(6, 0, 0, 3)
-    ag_cross(5, 1, 0, 1)
-    do_pj0(1)
-    ag_cross(2, 0, 1, 3)
-    do_at0(0)
-    ag_cross(2, 1, 1, 1)
-    ag_cross(6, 0, 0, 1)
-    ag_first_m(4)
-    ag_pass(1, 0, 2)
-    ag_turn(1, 0, 3)
-    do_at0(1)
-    ag_cross(2, 1, 1, 3)
-    ag_cross(6, 1, 0, 3)
-    ag_turn(1, 0, 1)
-    do_op0(1)
-    ag_spread(4, 0)
-    do_nf0(1)
-    ag_cross(5, 0, 1, 2)
-    ag_cross(6, 1, 1, 3)
-    ag_cross(5, 0, 0, 1)
-    ag_cross(5, 1, 0, 2)
-    ag_last(2)
-    ag_cross(4, 0, 0, 1)
-    do_pj1(1, 1)
-    ag_cross(6, 0, 1, 3)
-    do_pj1(1, 0)
-    ag_turn(1, 1, 0)
-    do_at1(1)
-    ag_pass(1, 1, 3)
-    do_op1(1)
-    do_op0(0)
-    ag_cross(4, 1, 0, 1)
-    ag_cross(6, 0, 1, 2)
-    ag_turn(1, 0, 2)
-    ag_cross(3, 1, 0, 1)
-    ag_cross(6, 0, 0, 2)
-    do_nf1(1)
     ag_cross(6, 1, 1, 2)
-    ag_turn(1, 0, 0)
-    ag_pass(1, 1, 2)
-    ag_cross(3, 0, 1, 1)
-    ag_cross(3, 0, 0, 1)
-    ag_spread(4, 1)
-    ag_last(5)
-    do_fu(1, 0)
-    ag_cross(4, 0, 1, 2)
     ag_cross(3, 1, 1, 1)
     do_fu(1, 1)
+    ag_first_m(4)
     do_fu(1, 2)
-    ag_cross(3, 1, 0, 2)
-    ag_cross(3, 1, 0, 3)
     do_fu(1, 3)
+    ag_pass(1, 1, 2)
+    ag_cross(3, 1, 0, 1)
     ag_last(6)
-    ag_cross(4, 1, 0, 2)
-    ag_cross(4, 0, 1, 1)
+    ag_pass(1, 0, 3)
     do_fd(1)
+    ag_cross(3, 0, 0, 2)
+    ag_pass(1, 0, 2)
+    ag_cross(4, 0, 0, 1)
+    ag_spread(4, 1)
+    ag_spread(4, 0)
+    do_n3(1)
+    ag_cross(4, 1, 0, 3)
+    ag_turn(1, 0, 3)
     ag_cross(3, 0, 1, 3)
     ag_turn(1, 1, 2)
-    ag_cross(3, 1, 1, 3)
-    ag_turn(1, 1, 3)
-    ag_cross(4, 0, 0, 3)
-    ag_turn(1, 1, 1)
-    do_n3(1)
-    ag_cross(4, 1, 0, 3)
+    ag_turn(1, 0, 2)
+    ag_cross(4, 1, 0, 1)
+    do_fb(1, 0)
+    ag_cross(4, 1, 1, 1)
     ag_cross(3, 0, 1, 2)
-    ag_cross(4, 0, 1, 3)
+    do_fb(1, 1)
+    ag_cross(3, 1, 0, 3)
+    ag_cross(3, 1, 0, 2)
+    do_op0(0)
+    do_fh(1)
+    ag_cross(4, 0, 1, 1)
+    do_nf0(0)
+    ag_last(1)
     ag_cross(4, 1, 1, 2)
-    ag_cross(4, 1, 1, 1)
-    do_fb(1, 0)
-    do_fb(1, 1)
     ag_cross(3, 1, 1, 2)
-    do_fh(1)
-    ag_cross(3, 0, 0, 3)
-    ag_cross(4, 1, 1, 3)
-    ag_last(1)
-    do_fg(1)
+    do_sb(1)
+    do_pj1(0, 0)
+    ag_cross(4, 1, 0, 2)
     ag_cross(4, 0, 0, 2)
-    do_nf0(0)
-    do_sb(1)
-    do_gm(1, 0)
-    do_gm(1, 1)
-    do_ab(1, 0)
-    do_pj1(0, 0)
-    f2_m(6, 1)
     do_pj1(0, 1)
-    rs2_m(6, 1)
     do_at1(0)
     do_op1(0)
+    ag_cross(3, 0, 0, 3)
+    do_gm(1, 0)
+    ag_cross(4, 0, 1, 2)
+    do_gm(1, 1)
+    ag_cross(3, 1, 1, 3)
+    do_nf1(0)
+    ag_cross(4, 1, 1, 3)
+    do_fg(1)
     f2_m(6, 0)
+    do_ab(1, 0)
+    rs2_m(6, 0)
     do_ab(1, 1)
-    do_be(1)
-    rs2_m(6, 0)
-    do_nf1(0)
-    do_ag(1)
+    ag_cross(4, 0, 0, 3)
+    f2_m(6, 1)
     ag_last(3)
     do_fu(0, 0)
+    do_be(1)
     do_fu(0, 1)
-    ag_last(4)
-    f2_m(5, 1)
+    ag_cross(4, 0, 1, 3)
+    rs2_m(6, 1)
+    do_ag(1)
     do_fu(0, 2)
     do_fu(0, 3)
+    ag_last(4)
     do_fd(0)
+    f2_m(5, 0)
+    f5(6, 0)
+    f2_m(5, 1)
+    rs2_m(5, 0)
+    do_n3(0)
+    rs5(6, 0)
+    f2(2, 1)
+    f2(2, 0)
     rs2_m(5, 1)
-    f2(2, 1)
-    f2_m(5, 0)
-    do_n3(0)
-    f2(2, 0)
     rs2(2, 1)
-    rs2_m(5, 0)
-    rs2(2, 0)
-    do_cb(1)
     do_fb(0, 0)
     do_fb(0, 1)
     do_fh(0)
+    do_cb(1)
+    do_sb(0)
+    f5(5, 0)
     do_fg(0)
-    do_sb(0)
-    f5(6, 1)
-    rs5(6, 1)
-    f5(5, 1)
+    do_gm(0, 1)
     f3(2, 1)
-    f3(2, 0)
     do_gm(0, 0)
-    do_gm(0, 1)
-    rs3(2, 0)
+    rs5(5, 0)
+    rs3(2, 1)
     do_ab(0, 0)
-    rs3(2, 1)
+    f2_m(4, 1)
+    rs2_m(4, 1)
+    f5(2, 1)
     do_be(0)
     do_ag(0)
-    f5(5, 0)
-    f2_m(4, 1)
+    f2_m(4, 0)
+    do_cb(0)
+    rs2(2, 0)
+    rs5(2, 1)
+    f5(5, 1)
+    f5(6, 1)
+    rs2_m(4, 0)
+    do_gm0(2)
+    do_gm0(0)
+    do_gm0(1)
+    rs5(6, 1)
+    do_ab0(0)
+    f2_m(3, 0)
+    f2_m(3, 1)
     rs5(5, 1)
-    f5(6, 0)
-    do_cb(0)
-    rs5(6, 0)
-    f2_m(4, 0)
-    rs2_m(4, 1)
-    rs5(5, 0)
-    do_gm0(1)
-    rs2_m(4, 0)
-    do_gm0(0)
-    do_gm0(2)
-    do_ab0(0)
-    f5(2, 1)
-    f2_m(3, 0)
+    f5(4, 1)
+    rs2_m(3, 0)
+    f2(1, 1)
+    rs5(4, 1)
+    f5(4, 0)
     do_ab0(1)
-    f2(1, 1)
-    rs2_m(3, 0)
-    f3_m(6, 1)
+    rs2(1, 1)
     f2(1, 0)
-    f5(2, 0)
-    f5(4, 1)
-    rs2(1, 1)
-    rs5(2, 1)
-    f2_m(3, 1)
+    do_be0(0)
+    rs5(4, 0)
     rs2(1, 0)
-    rs5(4, 1)
+    rs2_m(3, 1)
     do_be0(1)
-    do_be0(0)
     do_ag0(0)
-    rs5(2, 0)
+    f3(2, 0)
+    f5(3, 0)
+    f3(1, 1)
+    rs5(3, 0)
     do_ag0(1)
-    rs2_m(3, 1)
+    rs3(1, 1)
     f3(1, 0)
+    f3_m(4, 0)
+    f2(0, 0)
+    rs3(2, 0)
+    f5(3, 1)
+    rs5(3, 1)
     rs3(1, 0)
-    f3_m(5, 0)
-    rs3_m(5, 0)
     f2(0, 1)
-    f5(4, 0)
-    rs3_m(6, 1)
-    f3_m(5, 1)
-    f3(1, 1)
-    f2(0, 0)
-    rs5(4, 0)
+    f5(1, 1)
+    do_fin(0)
+    rs2(0, 1)
     rs2(0, 0)
-    rs3_m(5, 1)
-    f2(7, 0)
-    f5(3, 0)
     f3_m(6, 0)
-    rs5(3, 0)
-    rs3_m(6, 0)
-    rs2(7, 0)
+    do_fin(1)
+    rs5(1, 1)
     vec1()
-    f3_m(4, 1)
-    do_fin(0)
-    rs3(1, 1)
     f2(7, 1)
     rs2(7, 1)
-    f5(3, 1)
+    rs3_m(6, 0)
+    f3_m(4, 1)
+    f5(2, 0)
+    f2(7, 0)
+    f3(0, 1)
+    rs5(2, 0)
+    rs3(0, 1)
     f3(0, 0)
+    vec2()
+    f5(1, 0)
+    rs5(1, 0)
+    f3_m(6, 1)
+    rs2(7, 0)
+    rs3(0, 0)
+    f3_m(5, 0)
+    rs3_m(4, 1)
+    f4(2)
+    f3_m(5, 1)
+    vec3()
+    rs3_m(4, 0)
+    f3_m(3, 0)
+    f5(0, 1)
+    rs3_m(6, 1)
+    rs5(0, 1)
+    rs3_m(5, 0)
+    held["g", 2] = rs4(2)
+    f5(0, 0)
+    rs3_m(3, 0)
+    f3_m(3, 1)
+    rs3_m(5, 1)
+    f3(7, 1)
+    rs3_m(3, 1)
+    rs5(0, 0)
+    f4(1)
+    f3(7, 0)
+    f4_m(6)
+    rs3(7, 1)
+    rs3(7, 0)
+    f5(7, 1)
+    f4_m(4)
     f4_m(5)
-    rs5(3, 1)
-    f3_m(4, 0)
+    f4_m(3)
     held["g", 5] = rs4_m(5)
-    vec2()
-    f4_m(6)
-    rs3(0, 0)
-    do_fin(1)
-    f3(7, 1)
-    rs2(0, 1)
-    f5(1, 0)
-    rs3(7, 1)
-    rs3_m(4, 0)
-    rs5(1, 0)
-    f5(1, 1)
-    vec3()
-    f5(0, 0)
-    rs5(1, 1)
-    f3(7, 0)
-    rs5(0, 0)
-    f3(0, 1)
-    rs3(0, 1)
-    held["g", 6] = rs4_m(6)
-    rs3_m(4, 1)
-    f3_m(3, 1)
-    f5(7, 1)
-    rs3(7, 0)
-    f4(1)
     rs5(7, 1)
-    f5(0, 1)
-    rs5(0, 1)
-    rs3_m(3, 1)
-    f4(2)
+    f5(7, 0)
+    held["g", 4] = rs4_m(4)
     held["g", 1] = rs4(1)
-    f3_m(3, 0)
-    f5(7, 0)
     rs5(7, 0)
-    rs3_m(3, 0)
     f4(0)
     vec4()
-    held["g", 2] = rs4(2)
-    f4_m(4)
-    f4_m(3)
+    held["g", 3] = rs4_m(3)
+    held["g", 6] = rs4_m(6)
     f4(7)
     held["g", 0] = rs4(0)
-    held["g", 4] = rs4_m(4)
-    held["g", 3] = rs4_m(3)
     held["g", 7] = rs4(7)
     squares()
     for cp, when in rs_sends:

time: 290 us -> 282 us (0.972)
  Pallas kernels: 285 us -> 277 us
    pallas_call x1, Pallas kernels: 274 us -> 266 us  [fused(): pl.pallas_call(kernel, out_shape=[o[0] for o in outs], in_specs=[vmem, vm...]
where the time goes in v5:
time: 282 us; the launch traced here: 278 us
  Pallas kernels  277 us (98%)
    pallas_call x1, Pallas kernels, fused(): pl.pallas_call(kernel, out_shape=[o[0] for o in outs], in_specs=[vmem, vm...  266 us
    pallas_call x1, Pallas kernels, fast_body(): pl.pallas_call(update_kernel, out_shape=[like(a) for a in streams] + [lik...  10.6 us

profile of v5, /device:TPU:0, one launch (start us, length us, event | category | flops | bytes accessed | tf_op | source)
XLA Modules:
  0.0 277.8 jit_solution(3407953929685272058)
XLA Ops:
  0.7 266.2 %shard_map.269 = (f32[512,768]{1,0:T(8,128)}, f32[512,768]{1,0:T(8,128)}, f32[7,96,768]{2,1,0:T(8,128)}, f32[2,32,768]{2,1,0:T(8,128)}, f32[8,128]{1,0:T(8,128)}...) custom-call(bf16[20,8,768]{2,1,0:T(8,128)(2,1)} %bitcast.11, ...), custom_call_target="tpu_custom_call" | custom-call | tf_op jit(solution)/shard_map/pallas_call | solution.py:1315
  266.9 10.6 %shard_map.270 = (f32[20,8,768]{2,1,0:T(8,128)}, f32[36,8,768]{2,1,0:T(8,128)}, f32[20,8,768]{2,1,0:T(8,128)}, f32[36,8,768]{2,1,0:T(8,128)}, f32[3,4,96,192]{3,...) custom-call(f32[2,32,768]{2,1,0:T(8,128)} %get-tuple-element.39.vg, ...), custom_call_target="tpu_custom_call" | custom-call | tf_op jit(solution)/shard_map/pallas_call | solution.py:1446

commit v6 on v5

--- a/solution.py
+++ b/solution.py
@@ -939,302 +939,302 @@
     ag_first(0)
     own_weights(5)
     own_weights(2)
-    load_input()
     ag_first_m(2)
-    ag_turn(0, 0, 0)
-    ag_first_m(5)
-    ag_pass(0, 1, 1)
     ag_turn(0, 1, 0)
     own_weights(6)
+    ag_pass(0, 0, 1)
+    ag_first_m(5)
+    ag_spread(2, 0)
+    ag_pass(0, 1, 1)
+    ag_spread(2, 1)
+    ag_pass(0, 0, 3)
+    load_input()
+    ag_pass(0, 1, 3)
     ag_pass(0, 0, 2)
+    ag_cross(2, 1, 0, 3)
+    ag_turn(0, 0, 0)
     own_weights(1)
     ag_pass(0, 1, 2)
-    ag_pass(0, 0, 3)
-    ag_spread(5, 1)
-    ag_pass(0, 0, 1)
-    ag_spread(2, 0)
-    ag_pass(0, 1, 3)
-    ag_spread(2, 1)
+    ag_spread(5, 0)
+    ag_first_m(6)
+    ag_turn(0, 1, 1)
+    ag_turn(0, 1, 3)
+    ag_turn(0, 0, 1)
     ag_turn(0, 1, 2)
     ag_turn(0, 0, 3)
+    ag_cross(5, 1, 0, 1)
+    ag_turn(0, 0, 2)
+    ag_cross(5, 0, 0, 1)
+    own_weights(3)
+    ag_cross(2, 1, 0, 2)
+    ag_cross(2, 0, 0, 3)
+    ag_first(1)
+    ag_first_m(3)
+    ag_cross(2, 1, 1, 3)
+    ag_cross(6, 0, 0, 2)
+    ag_last(0)
+    do_pj0(2)
+    ag_spread(5, 1)
+    ag_cross(2, 0, 1, 1)
+    ag_cross(2, 1, 1, 1)
+    do_pj0(1)
+    ag_cross(6, 1, 0, 1)
+    ag_cross(2, 1, 1, 2)
+    do_pj0(0)
+    own_weights(4)
+    ag_cross(2, 0, 1, 2)
+    ag_cross(5, 1, 0, 2)
+    ag_pass(1, 0, 1)
+    ag_cross(2, 1, 0, 1)
+    do_at0(0)
+    ag_turn(1, 1, 0)
+    ag_pass(1, 1, 1)
     ag_cross(2, 0, 0, 2)
-    ag_cross(2, 1, 0, 2)
-    ag_turn(0, 0, 2)
-    own_weights(4)
-    ag_turn(0, 1, 1)
+    ag_cross(5, 0, 1, 1)
     ag_cross(2, 0, 0, 1)
+    ag_cross(6, 1, 0, 3)
+    ag_spread(6, 1)
+    ag_cross(2, 0, 1, 3)
+    ag_cross(6, 0, 0, 3)
+    do_at0(1)
+    do_op0(1)
+    ag_cross(3, 1, 0, 1)
+    ag_cross(5, 1, 0, 3)
+    ag_spread(6, 0)
+    ag_first_m(4)
+    do_op0(0)
+    ag_cross(5, 0, 1, 2)
+    do_nf0(1)
+    ag_last(2)
+    ag_cross(6, 1, 0, 2)
+    ag_cross(5, 1, 1, 3)
+    do_pj1(1, 1)
+    ag_cross(6, 0, 0, 1)
+    ag_cross(3, 0, 0, 1)
+    ag_cross(5, 0, 1, 3)
+    ag_turn(1, 0, 0)
+    do_pj1(1, 0)
+    ag_cross(5, 1, 1, 2)
+    do_at1(1)
+    ag_cross(5, 0, 0, 2)
+    ag_cross(5, 1, 1, 1)
+    do_op1(1)
     ag_cross(5, 0, 0, 3)
-    ag_turn(0, 1, 3)
-    ag_turn(0, 0, 1)
-    ag_spread(5, 0)
-    ag_first_m(6)
-    ag_first(1)
-    ag_cross(2, 1, 1, 2)
-    own_weights(3)
-    ag_cross(2, 1, 0, 1)
-    ag_cross(2, 0, 1, 1)
-    ag_cross(5, 1, 0, 2)
-    ag_cross(2, 0, 0, 3)
-    ag_last(0)
-    ag_cross(5, 0, 1, 1)
-    do_pj0(1)
-    ag_cross(2, 0, 1, 2)
-    ag_cross(6, 0, 0, 1)
-    ag_cross(5, 1, 0, 1)
-    ag_cross(2, 1, 0, 3)
-    ag_cross(5, 0, 1, 2)
-    do_pj0(0)
-    ag_cross(5, 0, 0, 1)
-    ag_cross(2, 1, 1, 1)
-    ag_cross(2, 0, 1, 3)
-    ag_cross(5, 1, 1, 1)
-    ag_first_m(3)
-    do_pj0(2)
-    do_at0(0)
-    ag_cross(6, 1, 0, 1)
-    ag_cross(6, 1, 0, 3)
-    ag_pass(1, 1, 1)
-    ag_cross(2, 1, 1, 3)
-    ag_spread(6, 1)
-    do_at0(1)
-    ag_pass(1, 0, 1)
-    do_op0(1)
-    ag_spread(6, 0)
-    ag_cross(5, 1, 1, 3)
-    ag_cross(3, 0, 0, 1)
-    ag_cross(5, 1, 0, 3)
-    do_nf0(1)
+    ag_turn(1, 1, 1)
+    ag_cross(6, 1, 1, 2)
+    do_nf1(1)
+    ag_cross(6, 1, 1, 3)
+    do_nf0(0)
+    ag_cross(6, 1, 1, 1)
+    ag_cross(6, 0, 1, 1)
+    ag_cross(6, 0, 1, 2)
+    ag_pass(1, 1, 2)
+    ag_last(5)
+    ag_cross(6, 0, 1, 3)
+    do_fu(1, 0)
+    ag_pass(1, 0, 3)
+    ag_spread(3, 1)
+    do_fu(1, 1)
+    do_fu(1, 2)
     ag_pass(1, 1, 3)
-    ag_cross(5, 1, 1, 2)
-    ag_last(2)
-    ag_cross(5, 0, 0, 2)
-    do_pj1(1, 1)
+    do_fu(1, 3)
+    ag_cross(4, 1, 0, 1)
+    ag_pass(1, 0, 2)
+    ag_spread(4, 0)
+    ag_last(6)
+    do_fd(1)
+    ag_turn(1, 1, 2)
+    ag_spread(4, 1)
+    ag_turn(1, 0, 3)
+    ag_cross(3, 1, 0, 2)
     ag_spread(3, 0)
-    do_pj1(1, 0)
+    ag_turn(1, 1, 3)
     ag_turn(1, 0, 1)
-    ag_cross(5, 0, 1, 3)
-    ag_turn(1, 1, 1)
-    ag_turn(1, 1, 0)
-    ag_spread(3, 1)
-    do_at1(1)
-    ag_cross(6, 0, 1, 1)
-    ag_cross(6, 0, 1, 3)
-    ag_turn(1, 1, 3)
-    do_op1(1)
-    ag_cross(6, 0, 0, 3)
-    ag_cross(6, 0, 1, 2)
-    ag_cross(6, 1, 1, 1)
-    do_nf1(1)
-    ag_cross(6, 0, 0, 2)
-    ag_last(5)
-    ag_turn(1, 0, 0)
+    ag_cross(4, 0, 0, 1)
+    do_n3(1)
+    ag_cross(3, 1, 1, 2)
+    ag_turn(1, 0, 2)
+    ag_cross(3, 1, 1, 1)
+    ag_cross(4, 0, 1, 1)
+    ag_cross(3, 0, 0, 2)
+    ag_cross(3, 1, 0, 3)
+    do_fb(1, 0)
+    ag_cross(4, 0, 0, 3)
+    ag_cross(4, 1, 1, 1)
+    do_fb(1, 1)
+    ag_cross(4, 1, 1, 2)
+    do_fh(1)
+    ag_cross(4, 0, 0, 2)
+    ag_cross(3, 0, 1, 2)
+    ag_last(1)
+    ag_cross(3, 0, 1, 3)
+    do_pj1(0, 0)
+    do_pj1(0, 1)
+    do_sb(1)
+    ag_cross(3, 1, 1, 3)
+    do_at1(0)
+    ag_cross(4, 1, 0, 3)
+    do_op1(0)
+    do_gm(1, 0)
+    do_gm(1, 1)
+    ag_cross(3, 0, 0, 3)
     ag_cross(3, 0, 1, 1)
-    ag_cross(6, 1, 1, 3)
-    do_fu(1, 0)
-    ag_cross(6, 1, 0, 2)
-    ag_cross(6, 1, 1, 2)
-    ag_cross(3, 1, 1, 1)
-    do_fu(1, 1)
-    ag_first_m(4)
-    do_fu(1, 2)
-    do_fu(1, 3)
-    ag_pass(1, 1, 2)
-    ag_cross(3, 1, 0, 1)
-    ag_last(6)
-    ag_pass(1, 0, 3)
-    do_fd(1)
-    ag_cross(3, 0, 0, 2)
-    ag_pass(1, 0, 2)
-    ag_cross(4, 0, 0, 1)
-    ag_spread(4, 1)
-    ag_spread(4, 0)
-    do_n3(1)
-    ag_cross(4, 1, 0, 3)
-    ag_turn(1, 0, 3)
-    ag_cross(3, 0, 1, 3)
-    ag_turn(1, 1, 2)
-    ag_turn(1, 0, 2)
-    ag_cross(4, 1, 0, 1)
-    do_fb(1, 0)
-    ag_cross(4, 1, 1, 1)
-    ag_cross(3, 0, 1, 2)
-    do_fb(1, 1)
-    ag_cross(3, 1, 0, 3)
-    ag_cross(3, 1, 0, 2)
-    do_op0(0)
-    do_fh(1)
-    ag_cross(4, 0, 1, 1)
-    do_nf0(0)
-    ag_last(1)
-    ag_cross(4, 1, 1, 2)
-    ag_cross(3, 1, 1, 2)
-    do_sb(1)
-    do_pj1(0, 0)
     ag_cross(4, 1, 0, 2)
-    ag_cross(4, 0, 0, 2)
-    do_pj1(0, 1)
-    do_at1(0)
-    do_op1(0)
-    ag_cross(3, 0, 0, 3)
-    do_gm(1, 0)
+    do_ab(1, 0)
     ag_cross(4, 0, 1, 2)
-    do_gm(1, 1)
-    ag_cross(3, 1, 1, 3)
     do_nf1(0)
+    ag_cross(4, 0, 1, 3)
+    f2_m(6, 0)
     ag_cross(4, 1, 1, 3)
     do_fg(1)
-    f2_m(6, 0)
-    do_ab(1, 0)
     rs2_m(6, 0)
+    f2_m(6, 1)
     do_ab(1, 1)
-    ag_cross(4, 0, 0, 3)
-    f2_m(6, 1)
     ag_last(3)
     do_fu(0, 0)
+    rs2_m(6, 1)
+    do_fu(0, 1)
     do_be(1)
-    do_fu(0, 1)
-    ag_cross(4, 0, 1, 3)
-    rs2_m(6, 1)
+    do_fu(0, 2)
+    ag_last(4)
     do_ag(1)
-    do_fu(0, 2)
     do_fu(0, 3)
-    ag_last(4)
     do_fd(0)
-    f2_m(5, 0)
     f5(6, 0)
     f2_m(5, 1)
-    rs2_m(5, 0)
     do_n3(0)
+    f2_m(5, 0)
     rs5(6, 0)
-    f2(2, 1)
-    f2(2, 0)
     rs2_m(5, 1)
-    rs2(2, 1)
     do_fb(0, 0)
     do_fb(0, 1)
     do_fh(0)
-    do_cb(1)
+    f2(2, 1)
+    f5(6, 1)
+    do_fg(0)
     do_sb(0)
-    f5(5, 0)
-    do_fg(0)
+    rs2_m(5, 0)
+    f5(5, 1)
     do_gm(0, 1)
-    f3(2, 1)
     do_gm(0, 0)
-    rs5(5, 0)
-    rs3(2, 1)
     do_ab(0, 0)
     f2_m(4, 1)
+    f5(5, 0)
+    rs5(5, 1)
+    rs2(2, 1)
+    f3_m(6, 0)
     rs2_m(4, 1)
-    f5(2, 1)
+    rs5(5, 0)
     do_be(0)
-    do_ag(0)
+    do_cb(1)
     f2_m(4, 0)
     do_cb(0)
-    rs2(2, 0)
-    rs5(2, 1)
-    f5(5, 1)
-    f5(6, 1)
-    rs2_m(4, 0)
+    do_ag(0)
+    f2(2, 0)
+    do_gm0(1)
     do_gm0(2)
     do_gm0(0)
-    do_gm0(1)
+    rs2_m(4, 0)
+    f5(4, 1)
+    do_ab0(0)
+    f2_m(3, 1)
+    rs5(4, 1)
+    rs2(2, 0)
     rs5(6, 1)
-    do_ab0(0)
     f2_m(3, 0)
-    f2_m(3, 1)
-    rs5(5, 1)
-    f5(4, 1)
+    rs2_m(3, 1)
+    f2(1, 1)
+    do_ab0(1)
+    f2(1, 0)
     rs2_m(3, 0)
-    f2(1, 1)
-    rs5(4, 1)
     f5(4, 0)
-    do_ab0(1)
     rs2(1, 1)
-    f2(1, 0)
+    rs2(1, 0)
+    f5(3, 1)
+    rs5(4, 0)
+    rs3_m(6, 0)
+    f3(2, 0)
+    do_be0(1)
+    rs3(2, 0)
     do_be0(0)
-    rs5(4, 0)
-    rs2(1, 0)
-    rs2_m(3, 1)
-    do_be0(1)
+    f3(2, 1)
+    f3_m(5, 0)
     do_ag0(0)
-    f3(2, 0)
+    rs5(3, 1)
+    f3(1, 0)
+    do_ag0(1)
+    rs3(1, 0)
+    f3(1, 1)
+    f2(0, 0)
+    rs3(1, 1)
     f5(3, 0)
-    f3(1, 1)
+    vec1()
+    rs2(0, 0)
+    f2(0, 1)
     rs5(3, 0)
-    do_ag0(1)
-    rs3(1, 1)
-    f3(1, 0)
+    f5(2, 0)
+    f5(1, 0)
+    rs5(2, 0)
+    rs3_m(5, 0)
+    f3_m(6, 1)
+    do_fin(1)
+    rs5(1, 0)
+    f2(7, 1)
+    rs3(2, 1)
+    rs2(0, 1)
+    f5(1, 1)
+    f2(7, 0)
+    f3_m(3, 1)
+    vec2()
+    rs3_m(6, 1)
+    rs2(7, 0)
+    f3(0, 0)
+    rs5(1, 1)
+    rs3(0, 0)
+    vec3()
+    f3(0, 1)
+    rs3(0, 1)
+    f3_m(4, 1)
+    f4_m(6)
+    f5(2, 1)
     f3_m(4, 0)
-    f2(0, 0)
-    rs3(2, 0)
-    f5(3, 1)
-    rs5(3, 1)
-    rs3(1, 0)
-    f2(0, 1)
-    f5(1, 1)
-    do_fin(0)
-    rs2(0, 1)
-    rs2(0, 0)
-    f3_m(6, 0)
-    do_fin(1)
-    rs5(1, 1)
-    vec1()
-    f2(7, 1)
     rs2(7, 1)
-    rs3_m(6, 0)
-    f3_m(4, 1)
-    f5(2, 0)
-    f2(7, 0)
-    f3(0, 1)
-    rs5(2, 0)
-    rs3(0, 1)
-    f3(0, 0)
-    vec2()
-    f5(1, 0)
-    rs5(1, 0)
-    f3_m(6, 1)
-    rs2(7, 0)
-    rs3(0, 0)
-    f3_m(5, 0)
-    rs3_m(4, 1)
-    f4(2)
+    rs5(2, 1)
+    rs3_m(3, 1)
+    f5(0, 0)
+    rs3_m(4, 0)
+    rs5(0, 0)
     f3_m(5, 1)
-    vec3()
-    rs3_m(4, 0)
-    f3_m(3, 0)
-    f5(0, 1)
-    rs3_m(6, 1)
-    rs5(0, 1)
-    rs3_m(5, 0)
-    held["g", 2] = rs4(2)
-    f5(0, 0)
-    rs3_m(3, 0)
-    f3_m(3, 1)
-    rs3_m(5, 1)
-    f3(7, 1)
-    rs3_m(3, 1)
-    rs5(0, 0)
     f4(1)
     f3(7, 0)
-    f4_m(6)
+    rs3_m(4, 1)
+    rs3_m(5, 1)
+    held["g", 6] = rs4_m(6)
+    rs3(7, 0)
+    f3_m(3, 0)
+    f3(7, 1)
     rs3(7, 1)
-    rs3(7, 0)
-    f5(7, 1)
-    f4_m(4)
+    rs3_m(3, 0)
     f4_m(5)
     f4_m(3)
+    f5(0, 1)
     held["g", 5] = rs4_m(5)
+    f5(7, 0)
+    rs5(0, 1)
+    do_fin(0)
+    rs5(7, 0)
+    held["g", 3] = rs4_m(3)
+    f4(2)
+    f5(7, 1)
     rs5(7, 1)
-    f5(7, 0)
+    f4_m(4)
+    vec4()
+    held["g", 2] = rs4(2)
+    f4(0)
     held["g", 4] = rs4_m(4)
-    held["g", 1] = rs4(1)
-    rs5(7, 0)
-    f4(0)
-    vec4()
-    held["g", 3] = rs4_m(3)
-    held["g", 6] = rs4_m(6)
     f4(7)
     held["g", 0] = rs4(0)
+    held["g", 1] = rs4(1)
     held["g", 7] = rs4(7)
     squares()
     for cp, when in rs_sends:
@@ -1344,7 +1344,6 @@
         cp.start()
         return cp
 
-    streams = [go(out3, S0, ssem.at[0]), go(gx, S1, ssem.at[1])]
     grads = [go(g32.at[u], G.at[u], gs.at[u]) for u in range(NU)]
     loads = []
     for u in range(NU):
@@ -1355,6 +1354,7 @@
             refs = tuple((a.at[i[0], i[1]], b.at[i[0], i[1]]) for a, b in ((fw, FW), (fm, FM), (fv, FV)))
         loads.append([go(a, b, isem.at[u, k]) for k, (a, b) in enumerate(refs)])
 
+    streams = [go(out3, S0, ssem.at[0]), go(gx, S1, ssem.at[1])]
     lane = lax.broadcasted_iota(jnp.int32, (1, 384), 1)
     for b in range(3):
         for j in range(2):
@@ -1377,14 +1377,6 @@
     vec_o[...], vec_mo[...], vec_vo[...] = adam_update(vec[...], vec_m[...], vec_v[...], clipped, RATE_VECTOR)
 
     outs = []
-    for k, (src, L, V, lo, vo) in enumerate(((S0, L0, V0, lang_out, vis_out), (S1, L1, V1, lang_grad, vis_grad))):
-        streams[k].wait()
-        for M, base, count, pad in ((L, 0, 20, LP), (V, WO, 36, RP)):
-            for p in range(0, count, 4):
-                rows = jnp.stack([src[base + i * pad + p : base + i * pad + p + 4, :] for i in range(8)])
-                M[p : p + 4] = jnp.swapaxes(rows, 0, 1)
-        outs += [go(L, lo, ssem.at[2 + 2 * k]), go(V, vo, ssem.at[3 + 2 * k])]
-
     for u in range(NU):
         grads[u].wait()
         for cp in loads[u]:
@@ -1405,7 +1397,7 @@
             s, j = (u - 3) // 2, (u - 3) % 2
 
             def step(i, carry, s=s, j=j, u=u):
-                r = pl.ds(pl.multiple_of(i * 16, 16), 16)
+                r = pl.ds(pl.multiple_of(i * 48, 16), 48)
                 new, m, v = adam_update(FW[s, j, r, :], FM[s, j, r, :], FV[s, j, r, :], G[u, r, :] * clip, RATE_MATRIX)
                 FW[s, j, r, :] = new
                 FM[s, j, r, :] = m
@@ -1413,11 +1405,19 @@
                 FC[s, j, r, :] = new.astype(BF16)
                 return carry
 
-            lax.fori_loop(0, 6, step, 0)
+            lax.fori_loop(0, 2, step, 0)
             refs = tuple(
                 (a.at[s, j], b.at[s, j]) for a, b in ((FW, fw_o), (FM, fm_o), (FV, fv_o), (FC, fc_o))
             )
         outs += [go(a, b, osem.at[u, k]) for k, (a, b) in enumerate(refs)]
+    for k, (src, L, V, lo, vo) in enumerate(((S0, L0, V0, lang_out, vis_out), (S1, L1, V1, lang_grad, vis_grad))):
+        streams[k].wait()
+        for M, base, count, pad in ((L, 0, 20, LP), (V, WO, 36, RP)):
+            for p in range(0, count, 4):
+                rows = jnp.stack([src[base + i * pad + p : base + i * pad + p + 4, :] for i in range(8)])
+                M[p : p + 4] = jnp.swapaxes(rows, 0, 1)
+        outs += [go(L, lo, ssem.at[2 + 2 * k]), go(V, vo, ssem.at[3 + 2 * k])]
+
     for cp in outs:
         cp.wait()
 

time: 282 us -> 280 us (level)
  no operation moved by 1% of the time
where the time goes in v6:
time: 280 us; the launch traced here: 276 us
  Pallas kernels  275 us (98%)
    pallas_call x1, Pallas kernels, fused(): pl.pallas_call(kernel, out_shape=[o[0] for o in outs], in_specs=[vmem, vm...  265 us
    pallas_call x1, Pallas kernels, fast_body(): pl.pallas_call(update_kernel, out_shape=[like(a) for a in streams] + [lik...  10 us

profile of v6, /device:TPU:0, one launch (start us, length us, event | category | flops | bytes accessed | tf_op | source)
XLA Modules:
  0.0 275.6 jit_solution(16914705843879944996)
XLA Ops:
  0.7 264.7 %shard_map.269 = (f32[512,768]{1,0:T(8,128)}, f32[512,768]{1,0:T(8,128)}, f32[7,96,768]{2,1,0:T(8,128)}, f32[2,32,768]{2,1,0:T(8,128)}, f32[8,128]{1,0:T(8,128)}...) custom-call(bf16[20,8,768]{2,1,0:T(8,128)(2,1)} %bitcast.11, ...), custom_call_target="tpu_custom_call" | custom-call | tf_op jit(solution)/shard_map/pallas_call | solution.py:1315
  265.3 10.0 %shard_map.270 = (f32[20,8,768]{2,1,0:T(8,128)}, f32[36,8,768]{2,1,0:T(8,128)}, f32[20,8,768]{2,1,0:T(8,128)}, f32[36,8,768]{2,1,0:T(8,128)}, f32[3,4,96,192]{3,...) custom-call(f32[2,32,768]{2,1,0:T(8,128)} %get-tuple-element.39.vg, ...), custom_call_target="tpu_custom_call" | custom-call | tf_op jit(solution)/shard_map/pallas_call | solution.py:1446
